TPU v7x, 32 devices: a whole 2x2x4 slice. The times are simulated.
32 devices in a mesh: rows: 8 (over z, y), seq: 4 (over x, core).
Axes of the slice: x: 2, y: 2, z: 4, core: 2. Of those that a mesh axis runs over, the one named last changes fastest.
Arguments:
- tokens: bfloat16 [2, 8, 1024, 1152], P(None, 'rows', 'seq'), may hold values from -6 to 6
- lengths: int32 [2, 8, 4], P(None, 'rows'), may hold values from 1 to 1024, as said below
- norm1_gain: bfloat16 [1152], P(('rows', 'seq')), may hold values from 0.25 to 1.75
- norm1_bias: bfloat16 [1152], P(('rows', 'seq')), may hold values from -3 to 3
- w_query: bfloat16 [1152, 1152], P(('rows', 'seq')), may hold values from -0.1875 to 0.1875
- query_bias: bfloat16 [1152], P(('rows', 'seq')), may hold values from -3 to 3
- w_key: bfloat16 [1152, 1152], P(('rows', 'seq')), may hold values from -0.1875 to 0.1875
- w_value: bfloat16 [1152, 1152], P(('rows', 'seq')), may hold values from -0.1875 to 0.1875
- value_bias: bfloat16 [1152], P(('rows', 'seq')), may hold values from -3 to 3
- w_out: bfloat16 [1152, 1152], P(('rows', 'seq')), may hold values from -3 to 3
- out_bias: bfloat16 [1152], P(('rows', 'seq')), may hold values from -3 to 3
- norm2_gain: bfloat16 [1152], P(('rows', 'seq')), may hold values from 0.25 to 1.75
- norm2_bias: bfloat16 [1152], P(('rows', 'seq')), may hold values from -3 to 3
- w_up: bfloat16 [1152, 4304], P(('rows', 'seq')), may hold values from -0.1875 to 0.1875
- up_bias: bfloat16 [4304], replicated, may hold values from -3 to 3
- w_down: bfloat16 [4304, 1152], P(None, ('rows', 'seq')), may hold values from -0.09375 to 0.09375
- down_bias: bfloat16 [1152], P(('rows', 'seq')), may hold values from -3 to 3
- cotangent: bfloat16 [2, 8, 1024, 1152], P(None, 'rows', 'seq'), may hold values from -6 to 6
Outputs:
- block_output: bfloat16 [2, 8, 1024, 1152], P(None, 'rows', 'seq')
- grad_tokens: float32 [2, 8, 1024, 1152], P(None, 'rows', 'seq')
- grad_norm1_gain: float32 [1152], P(('rows', 'seq'))
- grad_norm1_bias: float32 [1152], P(('rows', 'seq'))
- grad_w_query: float32 [1152, 1152], P(('rows', 'seq'))
- grad_query_bias: float32 [1152], P(('rows', 'seq'))
- grad_w_key: float32 [1152, 1152], P(('rows', 'seq'))
- grad_w_value: float32 [1152, 1152], P(('rows', 'seq'))
- grad_value_bias: float32 [1152], P(('rows', 'seq'))
- grad_w_out: float32 [1152, 1152], P(('rows', 'seq'))
- grad_out_bias: float32 [1152], P(('rows', 'seq'))
- grad_norm2_gain: float32 [1152], P(('rows', 'seq'))
- grad_norm2_bias: float32 [1152], P(('rows', 'seq'))
- grad_w_up: float32 [1152, 4304], P(('rows', 'seq'))
- grad_up_bias: float32 [4304], replicated
- grad_w_down: float32 [4304, 1152], P(None, ('rows', 'seq'))
- grad_down_bias: float32 [1152], P(('rows', 'seq'))
Inputs may be any that keep to these rules, and one draw needn't show every extreme that they name: In each row the first three entries are picture lengths and the last is the padding run; they sum to 1024; one picture holds the rest of the row, and the two other pictures and the padding run hold at most 64 tokens each.
All inputs are finite; a program needn't handle non-finite values.
Results may differ from a plain program's by a relative error of at most 0.012.
Values may be sent and summed in bfloat16 or wider, within the bound.
No kernel may reach another device: no remote copies, remote signals or barrier semaphores. Data moves between devices by JAX's collectives and lax.ppermute only.
A program may use at most 320 MiB of HBM per device.

v0:
```python
import jax
import jax.numpy as jnp
from jax import lax
from jax.sharding import PartitionSpec as P

H = 16
HD = 72


norm_epsilon = 1e-06
masked_score = -1e30


def layer_norm(values, gain, shift):
    center = jnp.mean(values, axis=-1, keepdims=True)
    centered = values - center
    spread = jnp.mean(centered * centered, axis=-1, keepdims=True)
    return centered * lax.rsqrt(spread + norm_epsilon) * gain + shift


def outer_sum(left, right):
    return lax.dot_general(
        left.reshape(-1, left.shape[-1]),
        right.reshape(-1, right.shape[-1]),
        (((0,), (0,)), ((), ())),
        preferred_element_type=jnp.float32,
    )


def back_dot(grad_rows, weight):
    return lax.dot_general(
        grad_rows,
        weight,
        (((grad_rows.ndim - 1,), (1,)), ((), ())),
        preferred_element_type=jnp.float32,
    )


def column_sum(grad_rows):
    return jnp.sum(grad_rows.astype(jnp.float32).reshape(-1, grad_rows.shape[-1]), axis=0)


def segment_ids(lengths, row_length):
    ends = jnp.cumsum(lengths, axis=-1)
    places = jnp.arange(row_length, dtype=jnp.int32)
    return jnp.sum((places[:, None] >= ends[..., None, :]).astype(jnp.int32), axis=-1)


def attention_scores(queries, full_keys, same_picture):
    rows_here, local_len, model_width = queries.shape
    query_heads = queries.reshape(rows_here, local_len, H, HD)
    key_heads = full_keys.reshape(rows_here, full_keys.shape[1], H, HD)
    scores = jnp.einsum(
        "rqhd,rkhd->rhqk", query_heads, key_heads, preferred_element_type=jnp.float32
    ) * HD ** (-0.5)
    return jnp.where(same_picture, scores, masked_score)


def forward_pass(row_tokens, same_picture, gathered, full_down, up_bias):
    (
        w_query,
        w_key,
        w_value,
        w_out,
        w_up,
        gain_one,
        shift_one,
        query_bias,
        value_bias,
        out_bias,
        gain_two,
        shift_two,
        down_bias,
    ) = gathered
    rows_here, local_len, model_width = row_tokens.shape
    inputs = row_tokens.astype(jnp.float32)
    normed = layer_norm(inputs, gain_one.astype(jnp.float32), shift_one.astype(jnp.float32)).astype(
        jnp.bfloat16
    )
    queries = (
        jnp.dot(normed, w_query, preferred_element_type=jnp.float32)
        + query_bias.astype(jnp.float32)
    ).astype(jnp.bfloat16)
    key_rows = jnp.dot(normed, w_key, preferred_element_type=jnp.float32).astype(jnp.bfloat16)
    values = (
        jnp.dot(normed, w_value, preferred_element_type=jnp.float32)
        + value_bias.astype(jnp.float32)
    ).astype(jnp.bfloat16)
    full_keys, full_values = (
        lax.all_gather(key_rows, "seq", axis=1, tiled=True),
        lax.all_gather(values, "seq", axis=1, tiled=True),
    )
    full_len = full_keys.shape[1]
    scores = attention_scores(queries, full_keys, same_picture)
    row_top = jnp.max(scores, axis=-1, keepdims=True)
    shifted = jnp.exp(scores - row_top)
    row_total = jnp.sum(shifted, axis=-1, keepdims=True)
    log_total = row_top + jnp.log(row_total)
    attend_weights = (shifted / row_total).astype(jnp.bfloat16)
    value_heads = full_values.reshape(rows_here, full_len, H, HD)
    attended = (
        jnp.einsum(
            "rhqk,rkhd->rqhd", attend_weights, value_heads, preferred_element_type=jnp.float32
        )
        .reshape(rows_here, local_len, model_width)
        .astype(jnp.bfloat16)
    )
    residual_one = (
        inputs
        + jnp.dot(attended, w_out, preferred_element_type=jnp.float32)
        + out_bias.astype(jnp.float32)
    )
    normed_two = layer_norm(
        residual_one, gain_two.astype(jnp.float32), shift_two.astype(jnp.float32)
    ).astype(jnp.bfloat16)
    hidden = jnp.dot(normed_two, w_up, preferred_element_type=jnp.float32) + up_bias.astype(
        jnp.float32
    )
    active = jax.nn.gelu(hidden, approximate=True).astype(jnp.bfloat16)
    output = (
        residual_one
        + jnp.dot(active, full_down, preferred_element_type=jnp.float32)
        + down_bias.astype(jnp.float32)
    )
    saved = (
        inputs,
        normed,
        queries,
        full_keys,
        full_values,
        log_total,
        attended,
        residual_one,
        normed_two,
        hidden,
        active,
    )
    return (output, saved)


def backward_pass(saved, grad_out, same_picture, gathered, full_down):
    (
        w_query,
        w_key,
        w_value,
        w_out,
        w_up,
        gain_one,
        shift_one,
        query_bias,
        value_bias,
        out_bias,
        gain_two,
        shift_two,
        down_bias,
    ) = gathered
    (
        inputs,
        normed,
        queries,
        full_keys,
        full_values,
        log_total,
        attended,
        residual_one,
        normed_two,
        hidden,
        active,
    ) = saved
    rows_here, local_len, model_width = inputs.shape
    full_len = full_keys.shape[1]
    grad_mlp = grad_out.astype(jnp.bfloat16)
    d_w_down = outer_sum(active, grad_mlp)
    d_down_bias = column_sum(grad_mlp)
    grad_active = back_dot(grad_mlp, full_down)
    unused_gelu, gelu_pull = jax.vjp(lambda pre_act: jax.nn.gelu(pre_act, approximate=True), hidden)
    grad_hidden = gelu_pull(grad_active)[0].astype(jnp.bfloat16)
    d_up_bias = column_sum(grad_hidden)
    d_w_up = outer_sum(normed_two, grad_hidden)
    grad_normed_two = back_dot(grad_hidden, w_up)
    unused_two, norm_pull_two = jax.vjp(
        layer_norm, residual_one, gain_two.astype(jnp.float32), shift_two.astype(jnp.float32)
    )
    grad_through, d_gain_two, d_shift_two = norm_pull_two(grad_normed_two)
    grad_residual = grad_out + grad_through
    grad_branch = grad_residual.astype(jnp.bfloat16)
    d_out_bias = column_sum(grad_branch)
    d_w_out = outer_sum(attended, grad_branch)
    grad_attended = back_dot(grad_branch, w_out).astype(jnp.bfloat16)
    scores = attention_scores(queries, full_keys, same_picture)
    attend_probs = jnp.exp(scores - log_total)
    value_heads = full_values.reshape(rows_here, full_len, H, HD)
    key_heads = full_keys.reshape(rows_here, full_len, H, HD)
    query_heads = queries.reshape(rows_here, local_len, H, HD)
    grad_heads = grad_attended.reshape(rows_here, local_len, H, HD)
    grad_value_part = jnp.einsum(
        "rhqk,rqhd->rkhd",
        attend_probs.astype(jnp.bfloat16),
        grad_heads,
        preferred_element_type=jnp.float32,
    )
    grad_probs = jnp.einsum(
        "rqhd,rkhd->rhqk", grad_heads, value_heads, preferred_element_type=jnp.float32
    )
    inner = jnp.sum(attend_probs * grad_probs, axis=-1, keepdims=True)
    grad_scores = (attend_probs * (grad_probs - inner)).astype(jnp.bfloat16)
    grad_queries = (
        (
            jnp.einsum(
                "rhqk,rkhd->rqhd", grad_scores, key_heads, preferred_element_type=jnp.float32
            )
            * HD ** (-0.5)
        )
        .reshape(rows_here, local_len, model_width)
        .astype(jnp.bfloat16)
    )
    grad_key_part = jnp.einsum(
        "rhqk,rqhd->rkhd", grad_scores, query_heads, preferred_element_type=jnp.float32
    ) * HD ** (-0.5)
    grad_key_sum, grad_value_sum = (
        lax.psum_scatter(
            grad_key_part.reshape(rows_here, full_len, model_width).astype(jnp.bfloat16),
            "seq",
            scatter_dimension=1,
            tiled=True,
        ).astype(jnp.float32),
        lax.psum_scatter(
            grad_value_part.reshape(rows_here, full_len, model_width).astype(jnp.bfloat16),
            "seq",
            scatter_dimension=1,
            tiled=True,
        ).astype(jnp.float32),
    )
    grad_keys = grad_key_sum.astype(jnp.bfloat16)
    grad_values = grad_value_sum.astype(jnp.bfloat16)
    d_query_bias = column_sum(grad_queries)
    d_value_bias = column_sum(grad_values)
    d_w_query = outer_sum(normed, grad_queries)
    d_w_key = outer_sum(normed, grad_keys)
    d_w_value = outer_sum(normed, grad_values)
    grad_normed = (
        back_dot(grad_queries, w_query)
        + back_dot(grad_keys, w_key)
        + back_dot(grad_values, w_value)
    )
    unused_one, norm_pull_one = jax.vjp(
        layer_norm, inputs, gain_one.astype(jnp.float32), shift_one.astype(jnp.float32)
    )
    grad_input, d_gain_one, d_shift_one = norm_pull_one(grad_normed)
    grad_tokens = grad_residual + grad_input
    main_grads = (
        d_w_query,
        d_w_key,
        d_w_value,
        d_w_out,
        d_w_up,
        d_gain_one,
        d_shift_one,
        d_query_bias,
        d_value_bias,
        d_out_bias,
        d_gain_two,
        d_shift_two,
        d_down_bias,
    )
    return (grad_tokens, main_grads, d_w_down, d_up_bias)


def on_device(
    tokens,
    lengths,
    norm1_gain,
    norm1_bias,
    w_query,
    query_bias,
    w_key,
    w_value,
    value_bias,
    w_out,
    out_bias,
    norm2_gain,
    norm2_bias,
    w_up,
    up_bias,
    w_down,
    down_bias,
    cotangent,
):
    micro_count, rows_here, local_len, model_width = tokens.shape
    full_len = local_len * lax.axis_size("seq")
    offset = lax.axis_index("seq") * local_len
    segments = segment_ids(lengths, full_len)
    query_segments = lax.dynamic_slice_in_dim(segments, offset, local_len, axis=2)
    same_all = query_segments[:, :, None, :, None] == segments[:, :, None, None, :]
    outputs = []
    grad_list = []
    for step_index in range(micro_count):
        gathered = (
            lax.all_gather(w_query, ("rows", "seq"), axis=0, tiled=True),
            lax.all_gather(w_key, ("rows", "seq"), axis=0, tiled=True),
            lax.all_gather(w_value, ("rows", "seq"), axis=0, tiled=True),
            lax.all_gather(w_out, ("rows", "seq"), axis=0, tiled=True),
            lax.all_gather(w_up, ("rows", "seq"), axis=0, tiled=True),
            lax.all_gather(norm1_gain, ("rows", "seq"), axis=0, tiled=True),
            lax.all_gather(norm1_bias, ("rows", "seq"), axis=0, tiled=True),
            lax.all_gather(query_bias, ("rows", "seq"), axis=0, tiled=True),
            lax.all_gather(value_bias, ("rows", "seq"), axis=0, tiled=True),
            lax.all_gather(out_bias, ("rows", "seq"), axis=0, tiled=True),
            lax.all_gather(norm2_gain, ("rows", "seq"), axis=0, tiled=True),
            lax.all_gather(norm2_bias, ("rows", "seq"), axis=0, tiled=True),
            lax.all_gather(down_bias, ("rows", "seq"), axis=0, tiled=True),
        )
        full_down = lax.all_gather(w_down, ("rows", "seq"), axis=1, tiled=True)
        output, saved = forward_pass(
            tokens[step_index], same_all[step_index], gathered, full_down, up_bias
        )
        outputs.append(output.astype(jnp.bfloat16))
        gathered = (
            lax.all_gather(w_query, ("rows", "seq"), axis=0, tiled=True),
            lax.all_gather(w_key, ("rows", "seq"), axis=0, tiled=True),
            lax.all_gather(w_value, ("rows", "seq"), axis=0, tiled=True),
            lax.all_gather(w_out, ("rows", "seq"), axis=0, tiled=True),
            lax.all_gather(w_up, ("rows", "seq"), axis=0, tiled=True),
            lax.all_gather(norm1_gain, ("rows", "seq"), axis=0, tiled=True),
            lax.all_gather(norm1_bias, ("rows", "seq"), axis=0, tiled=True),
            lax.all_gather(query_bias, ("rows", "seq"), axis=0, tiled=True),
            lax.all_gather(value_bias, ("rows", "seq"), axis=0, tiled=True),
            lax.all_gather(out_bias, ("rows", "seq"), axis=0, tiled=True),
            lax.all_gather(norm2_gain, ("rows", "seq"), axis=0, tiled=True),
            lax.all_gather(norm2_bias, ("rows", "seq"), axis=0, tiled=True),
            lax.all_gather(down_bias, ("rows", "seq"), axis=0, tiled=True),
        )
        full_down = lax.all_gather(w_down, ("rows", "seq"), axis=1, tiled=True)
        grad_tokens, main_grads, d_w_down, d_up_bias = backward_pass(
            saved,
            cotangent[step_index].astype(jnp.float32),
            same_all[step_index],
            gathered,
            full_down,
        )
        grad_list.append(grad_tokens)
        if step_index == 0:
            totals = main_grads
            total_down = d_w_down
            total_up = d_up_bias
        else:
            totals = jax.tree.map(jnp.add, totals, main_grads)
            total_down = total_down + d_w_down
            total_up = total_up + d_up_bias
    owned = (
        lax.psum_scatter(totals[0], ("rows", "seq"), scatter_dimension=0, tiled=True),
        lax.psum_scatter(totals[1], ("rows", "seq"), scatter_dimension=0, tiled=True),
        lax.psum_scatter(totals[2], ("rows", "seq"), scatter_dimension=0, tiled=True),
        lax.psum_scatter(totals[3], ("rows", "seq"), scatter_dimension=0, tiled=True),
        lax.psum_scatter(totals[4], ("rows", "seq"), scatter_dimension=0, tiled=True),
        lax.psum_scatter(totals[5], ("rows", "seq"), scatter_dimension=0, tiled=True),
        lax.psum_scatter(totals[6], ("rows", "seq"), scatter_dimension=0, tiled=True),
        lax.psum_scatter(totals[7], ("rows", "seq"), scatter_dimension=0, tiled=True),
        lax.psum_scatter(totals[8], ("rows", "seq"), scatter_dimension=0, tiled=True),
        lax.psum_scatter(totals[9], ("rows", "seq"), scatter_dimension=0, tiled=True),
        lax.psum_scatter(totals[10], ("rows", "seq"), scatter_dimension=0, tiled=True),
        lax.psum_scatter(totals[11], ("rows", "seq"), scatter_dimension=0, tiled=True),
        lax.psum_scatter(totals[12], ("rows", "seq"), scatter_dimension=0, tiled=True),
    )
    down_part = lax.psum_scatter(total_down, ("rows", "seq"), scatter_dimension=1, tiled=True)
    up_part = lax.psum(total_up, ("rows", "seq"))
    block_output = jnp.stack(outputs)
    grad_all = jnp.stack(grad_list)
    return (
        block_output,
        grad_all,
        owned[5],
        owned[6],
        owned[0],
        owned[7],
        owned[1],
        owned[2],
        owned[8],
        owned[3],
        owned[9],
        owned[10],
        owned[11],
        owned[4],
        up_part,
        down_part,
        owned[12],
    )


def solution(mesh):
    return jax.shard_map(
        on_device,
        mesh=mesh,
        in_specs=(
            P(None, "rows", "seq", None),
            P(None, "rows", None),
            P(("rows", "seq")),
            P(("rows", "seq")),
            P(("rows", "seq"), None),
            P(("rows", "seq")),
            P(("rows", "seq"), None),
            P(("rows", "seq"), None),
            P(("rows", "seq")),
            P(("rows", "seq"), None),
            P(("rows", "seq")),
            P(("rows", "seq")),
            P(("rows", "seq")),
            P(("rows", "seq"), None),
            P(),
            P(None, ("rows", "seq")),
            P(("rows", "seq")),
            P(None, "rows", "seq", None),
        ),
        out_specs=(
            P(None, "rows", "seq", None),
            P(None, "rows", "seq", None),
            P(("rows", "seq")),
            P(("rows", "seq")),
            P(("rows", "seq"), None),
            P(("rows", "seq")),
            P(("rows", "seq"), None),
            P(("rows", "seq"), None),
            P(("rows", "seq")),
            P(("rows", "seq"), None),
            P(("rows", "seq")),
            P(("rows", "seq")),
            P(("rows", "seq")),
            P(("rows", "seq"), None),
            P(),
            P(None, ("rows", "seq")),
            P(("rows", "seq")),
        ),
        check_vma=False,
    )
```

profile of v0, /device:TPU:0, one launch (start us, length us, event | category | flops | bytes accessed | tf_op | source)
XLA Modules:
  0.0 1929.3 jit_solution(9243860199371607097)
XLA Ops:
  16.8 42.6 %all-reduce.29 = (bf16[1152]{0:T(1024)(128)(2,1)S(1)}, bf16[1152]{0:T(1024)(128)(2,1)S(1)}, bf16[1152]{0:T(1024)(128)(2,1)S(1)}, bf16[1152]{0:T(1024)(128)(2,1)S...) all-reduce(bf16[1152]{0:T(1024)(128)(2,1)S(1)} %dynamic-update-slic, ...), channel_id=1, replica_groups=mesh['rows'=8,'seq'=4] {'rows','seq'}, use_global_device_ids=true, to_apply=%add.2 | all-reduce | flops 9216 | bytes 36864
  61.5 11.0 all-gather.29.cloned.1.call-done
  72.5 5.2 reshape.1314
  81.3 51.7 %all-gather.33.cloned.1.call-done = bf16[32,36,1152]{2,1,0:T(8,128)(2,1)} async-done(((bf16[1,36,1152]{2,1,0:T(8,128)(2,1)}), bf16[32,36,1152]{2,1,0:T(8,128)(2,1)}) %all-gather.33.cloned.1.call-update) | async-done | bytes 2654224 | tf_op jit(solution)/shard_map/all_gather | solution.py:300
  133.1 5.2 reshape.1318
  154.4 39.1 %all-gather.31.cloned.1.call-done = bf16[32,36,1152]{2,1,0:T(8,128)(2,1)} async-done(((bf16[1,36,1152]{2,1,0:T(8,128)(2,1)}), bf16[32,36,1152]{2,1,0:T(8,128)(2,1)}) %all-gather.31.cloned.1.call-update) | async-done | bytes 2654224 | tf_op jit(solution)/shard_map/all_gather | solution.py:299
  193.5 5.2 reshape.1316
  206.5 47.3 %all-gather.35.cloned.1.call-done = bf16[32,36,1152]{2,1,0:T(8,128)(2,1)} async-done(((bf16[1,36,1152]{2,1,0:T(8,128)(2,1)}), bf16[32,36,1152]{2,1,0:T(8,128)(2,1)}) %all-gather.35.cloned.1.call-update) | async-done | bytes 2654224 | tf_op jit(solution)/shard_map/all_gather | solution.py:302
  253.8 5.2 reshape.1320
  259.0 19.7 %all-gather.25.cloned.1.call-done = bf16[1024,1152]{1,0:T(8,128)(2,1)} async-done(((bf16[256,1152]{1,0:T(8,128)(2,1)}), bf16[1024,1152]{1,0:T(8,128)(2,1)}) %all-gather.25.cloned.1.call-update) | async-done | bytes 2359312 | tf_op jit(solution)/shard_map/all_gather | solution.py:91
  282.9 21.8 %all-gather.27.cloned.1.call-done = bf16[1024,1152]{1,0:T(8,128)(2,1)} async-done(((bf16[256,1152]{1,0:T(8,128)(2,1)}), bf16[1024,1152]{1,0:T(8,128)(2,1)}) %all-gather.27.cloned.1.call-update) | async-done | bytes 2359312 | tf_op jit(solution)/shard_map/all_gather | solution.py:90
  307.6 22.8 %all-gather.21.cloned.1.call-done = bf16[1024,1152]{1,0:T(8,128)(2,1)} async-done(((bf16[256,1152]{1,0:T(8,128)(2,1)}), bf16[1024,1152]{1,0:T(8,128)(2,1)}) %all-gather.21.cloned.1.call-update) | async-done | bytes 2359312 | tf_op jit(solution)/shard_map/all_gather | solution.py:91
  334.7 21.4 %all-gather.23.cloned.1.call-done = bf16[1024,1152]{1,0:T(8,128)(2,1)} async-done(((bf16[256,1152]{1,0:T(8,128)(2,1)}), bf16[1024,1152]{1,0:T(8,128)(2,1)}) %all-gather.23.cloned.1.call-update) | async-done | bytes 2359312 | tf_op jit(solution)/shard_map/all_gather | solution.py:90
  360.3 4.5 fusion.142
  371.4 4.9 fusion.62
  389.5 5.1 fusion.63
  399.4 49.3 %all-gather.37.cloned.1.call-done = bf16[32,36,4304]{2,1,0:T(8,128)(2,1)} async-done(((bf16[1,36,4304]{2,1,0:T(8,128)(2,1)}), bf16[32,36,4304]{2,1,0:T(8,128)(2,1)}) %all-gather.37.cloned.1.call-update) | async-done | bytes 9916432 | tf_op jit(solution)/shard_map/all_gather | solution.py:303
  448.7 14.7 reshape.1322
  463.4 10.6 convolution_add_fusion.6
  474.0 6.8 convolution_add_fusion.7
  480.8 12.0 fusion.107
  492.8 46.5 %all-gather.39.cloned.1.call-done = bf16[32,36,4304]{2,1,0:T(8,128)(2,1)} async-done(((bf16[1,36,4304]{2,1,0:T(8,128)(2,1)}), bf16[32,36,4304]{2,1,0:T(8,128)(2,1)}) %all-gather.39.cloned.1.call-update) | async-done | bytes 9916432 | tf_op jit(solution)/shard_map/all_gather | solution.py:313
  539.3 14.5 reshape.1324
  553.7 11.0 convert_reduce_fusion.1
  564.7 11.0 convert_reduce_fusion
  575.8 7.8 fusion.147
  583.6 8.2 multiply_reduce_fusion.3
  596.9 12.2 multiply_reduce_fusion.1
  609.1 12.0 multiply_convert_fusion.1
  626.4 19.2 convolution_add_fusion.1
  645.6 242.6 %fusion.5 = f32[4304,40]{0,1:T(8,128)} fusion(f32[4304,1152]{0,1:T(8,128)} %convolution_add_fusion.1), kind=kCustom, calls=%all-reduce-scatter.5 | all-reduce-scatter fusion | flops 5509121 | bytes 20521472
  890.4 7.4 collective-permute-start.37
  905.7 9.5 fusion.44
  915.2 11.8 multiply_reduce_fusion
  933.6 13.0 multiply_convert_fusion
  959.1 4.7 fusion.126
  963.8 10.5 fusion.47
  974.3 8.1 fusion.43
  982.5 8.2 fusion.42
  990.7 8.8 fusion.123
  1000.7 6.0 convolution_add_fusion.5
  1006.7 17.7 convolution_add_fusion
  1036.6 18.0 concatenate.5
  1056.6 4.6 fusion.104
  1061.2 4.5 fusion.101
  1065.7 6.2 convolution_add_fusion.4
  1071.9 6.2 convolution_add_fusion.3
  1078.1 500.0 %fusion.137 = (f32[48,1152]{1,0:T(8,128)S(1)}, f32[48,1152]{1,0:T(8,128)}, f32[48,1152]{1,0:T(8,128)}, f32[48,1152]{1,0:T(8,128)}, f32[40,4304]{1,0:T(8,128)}) fusion(f32[1152,1152]{1,0:T(8,128)} %convolution_add_fusion.5, f32[1152,1152]{1,0:T(8,128)} %convolution_add_fusion.4, f32[1152,1152]{1,0:T(8,128)} %convolution_add_fusion.3, ...), kind=kCustom, calls=%all-reduce-scatter.6 | all-reduce-scatter fusion | flops 12587010 | bytes 42639872
  1578.1 38.0 %collective-permute-start.6 = (f32[48,1152]{1,0:T(8,128)S(1)}, f32[48,1152]{1,0:T(8,128)S(1)}, u32[]{:S(2)}, u32[]{:S(2)}) collective-permute-start(f32[48,1152]{1,0:T(8,128)S(1)} %get-tuple-element.61), channel_id=1, source_target_pairs={{0,7},{1,8},{2,9},{3,10},{4,11},{5,12},{6,13},{7,14},{8,15},{9,16}... | collective-permute-start | bytes 663560
  1616.2 15.8 collective-permute-start.5
  1641.2 14.5 collective-permute-start.7
  1663.9 5.1 collective-permute-start.23
  1682.3 5.1 collective-permute-start.14
  1719.9 5.4 collective-permute-start.18
  1725.8 48.3 %all-reduce.28 = (f32[1152]{0:T(1024)}, f32[1152]{0:T(1024)S(1)}, f32[1152]{0:T(1024)S(1)}, f32[1152]{0:T(1024)S(1)}, f32[1152]{0:T(1024)S(1)}, /*index=5*/f32[1...) all-reduce(f32[1152]{0:T(1024)S(1)} %add.407, ...), channel_id=10, replica_groups=mesh['rows'=8,'seq'=4] {'rows','seq'}, use_global_device_ids=true, to_apply=%region_30.31.clone | all-reduce | flops 13520 | bytes 108160
  1782.7 4.9 collective-permute-start.17
  1789.6 4.6 collective-permute-start.30
  1801.4 14.6 concatenate
  1816.0 6.8 concatenate.1
  1828.4 15.1 concatenate.2
  1852.9 4.3 collective-permute-start.34
  1860.6 22.4 %collective-permute-start.32 = (f32[40,4304]{1,0:T(8,128)S(1)}, f32[40,4304]{1,0:T(8,128)}, u32[]{:S(2)}, u32[]{:S(2)}) collective-permute-start(f32[40,4304]{1,0:T(8,128)S(1)} %copy-done.30), channel_id=1, source_target_pairs={{0,1},{1,2},{2,3},{3,4},{4,5},{5,6},{6,7},{7,8},{8,9},{9,10},{10,1... | collective-permute-start | bytes 2065928
  1887.8 14.5 concatenate.3
  1906.2 15.4 concatenate.4
  (537 shorter events, 242.0 us)
Async XLA Ops:
  7.2 65.3 %all-gather.29.cloned.1.call-start = ((), (), s32[]{:S(2)}) async-start(), calls=%async_computation.12 | async-start | bytes 3041280 | tf_op jit(solution)/shard_map/all_gather | solution.py:301
  7.9 125.1 %all-gather.33.cloned.1.call-start = ((), (), s32[]{:S(2)}) async-start(), calls=%async_computation.14 | async-start | bytes 3041280 | tf_op jit(solution)/shard_map/all_gather | solution.py:300
  8.7 184.8 %all-gather.31.cloned.1.call-start = ((), (), s32[]{:S(2)}) async-start(), calls=%async_computation.13 | async-start | bytes 3041280 | tf_op jit(solution)/shard_map/all_gather | solution.py:299
  9.4 244.4 %all-gather.35.cloned.1.call-start = ((), (), s32[]{:S(2)}) async-start(), calls=%async_computation.15 | async-start | bytes 3041280 | tf_op jit(solution)/shard_map/all_gather | solution.py:302
  10.0 268.7 %all-gather.25.cloned.1.call-start = ((), (), s32[]{:S(2)}) async-start(), calls=%async_computation.10 | async-start | bytes 2949120 | tf_op jit(solution)/shard_map/all_gather | solution.py:91
  59.5 143.1 %copy-start.58 = (f32[1152]{0:T(1024)}, f32[1152]{0:T(1024)S(1)}, u32[]{:S(2)}) copy-start(f32[1152]{0:T(1024)S(1)} %convert_element_type.490) | copy-start | bytes 13828
  59.5 143.1 %copy-start.52 = (f32[1152]{0:T(1024)}, f32[1152]{0:T(1024)S(1)}, u32[]{:S(2)}) copy-start(f32[1152]{0:T(1024)S(1)} %convert_element_type.489) | copy-start | bytes 13828
  81.3 223.4 %all-gather.27.cloned.1.call-start = ((), (), s32[]{:S(2)}) async-start(), calls=%async_computation.11 | async-start | bytes 2949120 | tf_op jit(solution)/shard_map/all_gather | solution.py:90
  141.9 188.5 %all-gather.21.cloned.1.call-start = ((), (), s32[]{:S(2)}) async-start(), calls=%async_computation.8 | async-start | bytes 2949120 | tf_op jit(solution)/shard_map/all_gather | solution.py:91
  145.7 210.4 %all-gather.23.cloned.1.call-start = ((), (), s32[]{:S(2)}) async-start(), calls=%async_computation.9 | async-start | bytes 2949120 | tf_op jit(solution)/shard_map/all_gather | solution.py:90
  149.4 299.3 %all-gather.37.cloned.1.call-start = ((), (), s32[]{:S(2)}) async-start(), calls=%async_computation.16 | async-start | bytes 11489280 | tf_op jit(solution)/shard_map/all_gather | solution.py:303
  150.1 389.1 %all-gather.39.cloned.1.call-start = ((), (), s32[]{:S(2)}) async-start(), calls=%async_computation.17 | async-start | bytes 11489280 | tf_op jit(solution)/shard_map/all_gather | solution.py:313
  150.7 905.9 %reduce-scatter.17.cloned.1.call-start = ((), (), s32[]{:S(2)}) async-start(), calls=%async_computation.4 | async-start | bytes 2949120 | tf_op jit(solution)/shard_map/reduce_scatter | solution.py:221
  153.0 321.0 %copy-start.63 = (f32[1152]{0:T(1024)}, f32[1152]{0:T(1024)S(1)}, u32[]{:S(2)}) copy-start(f32[1152]{0:T(1024)S(1)} %convert_element_type.507) | copy-start | bytes 13828
  153.0 438.9 %copy-start.60 = (f32[1152]{0:T(1024)}, f32[1152]{0:T(1024)S(1)}, u32[]{:S(2)}) copy-start(f32[1152]{0:T(1024)S(1)} %convert_element_type.506) | copy-start | bytes 13828
  397.8 194.1 %copy-start.107 = (f32[256]{0:T(256)}, f32[256]{0:T(256)S(1)}, u32[]{:S(2)}) copy-start(f32[256]{0:T(256)S(1)} %broadcast_multiply_fusion.2) | copy-start | bytes 3076
  398.1 193.8 %copy-start.127 = (f32[256]{0:T(256)}, f32[256]{0:T(256)S(1)}, u32[]{:S(2)}) copy-start(f32[256]{0:T(256)S(1)} %fusion.120) | copy-start | bytes 3076
  398.1 193.8 %copy-start.122 = (f32[256]{0:T(256)}, f32[256]{0:T(256)S(1)}, u32[]{:S(2)}) copy-start(f32[256]{0:T(256)S(1)} %fusion.118) | copy-start | bytes 3076
  625.1 436.1 %reduce-scatter.19.cloned.1.call-start = ((), (), s32[]{:S(2)}) async-start(), calls=%async_computation.5 | async-start | bytes 2949120 | tf_op jit(solution)/shard_map/reduce_scatter | solution.py:227
  645.6 255.1 %copy-start.33 = (bf16[256,1152]{1,0:T(8,128)(2,1)S(1)}, bf16[256,1152]{1,0:T(8,128)(2,1)}, u32[]{:S(2)}) copy-start(bf16[256,1152]{1,0:T(8,128)(2,1)} %get-tuple-element.77) | copy-start | bytes 1769476
  888.2 148.3 %collective-permute-start.38 = (f32[4304,40]{0,1:T(8,128)}, f32[4304,40]{0,1:T(8,128)}, u32[]{:S(2)}, u32[]{:S(2)}) collective-permute-start(f32[4304,40]{0,1:T(8,128)} %fusion.5), channel_id=1, source_target_pairs={{0,3},{1,4},{2,5},{3,6},{4,7},{5,8},{6,9},{7,10},{8,11},{9,12},{10... | collective-permute-start | bytes 2065928
  890.4 146.2 %collective-permute-start.37 = (f32[4304,40]{0,1:T(8,128)}, f32[4304,40]{0,1:T(8,128)}, u32[]{:S(2)}, u32[]{:S(2)}) collective-permute-start(f32[4304,40]{0,1:T(8,128)} %fusion.5), channel_id=1, source_target_pairs={{0,2},{1,3},{2,4},{3,5},{4,6},{5,7},{6,8},{7,9},{8,10},{9,11},{10,... | collective-permute-start | bytes 2065928
  897.7 138.9 %collective-permute-start.36 = (f32[4304,40]{0,1:T(8,128)}, f32[4304,40]{0,1:T(8,128)}, u32[]{:S(2)}, u32[]{:S(2)}) collective-permute-start(f32[4304,40]{0,1:T(8,128)} %fusion.5), channel_id=1, source_target_pairs={{0,1},{1,2},{2,3},{3,4},{4,5},{5,6},{6,7},{7,8},{8,9},{9,10},{10,1... | collective-permute-start | bytes 2065928
  927.0 138.7 %reduce-scatter.21.cloned.1.call-start = ((), (), s32[]{:S(2)}) async-start(), calls=%async_computation.6 | async-start | bytes 2949120 | tf_op jit(solution)/shard_map/reduce_scatter | solution.py:221
  957.9 114.1 %reduce-scatter.23.cloned.1.call-start = ((), (), s32[]{:S(2)}) async-start(), calls=%async_computation.7 | async-start | bytes 2949120 | tf_op jit(solution)/shard_map/reduce_scatter | solution.py:227
  1027.4 9.1 collective-permute-start.39
  1078.1 555.2 %copy-start.41 = (bf16[1,256,1152]{1,2,0:T(8,128)(2,1)S(1)}, bf16[1,256,1152]{1,2,0:T(8,128)(2,1)}, u32[]{:S(2)}) copy-start(bf16[1,256,1152]{1,2,0:T(8,128)(2,1)} %reduce-scatter.21.cloned.1.call-done) | copy-start | bytes 1769476
  1078.1 555.2 %copy-start.49 = (f32[256,1152]{1,0:T(8,128)S(1)}, f32[256,1152]{1,0:T(8,128)}, u32[]{:S(2)}) copy-start(f32[256,1152]{1,0:T(8,128)} %fusion.148) | copy-start | bytes 3538948
  1578.1 96.5 %collective-permute-start.6 = (f32[48,1152]{1,0:T(8,128)S(1)}, f32[48,1152]{1,0:T(8,128)S(1)}, u32[]{:S(2)}, u32[]{:S(2)}) collective-permute-start(f32[48,1152]{1,0:T(8,128)S(1)} %get-tuple-element.61), channel_id=1, source_target_pairs={{0,7},{1,8},{2,9},{3,10},{4,11},{5,12},{6,13},{7,14},{8,15},{9,16}... | collective-permute-start | bytes 663560
  1616.2 62.7 %collective-permute-start.5 = (f32[48,1152]{1,0:T(8,128)S(1)}, f32[48,1152]{1,0:T(8,128)S(1)}, u32[]{:S(2)}, u32[]{:S(2)}) collective-permute-start(f32[48,1152]{1,0:T(8,128)S(1)} %get-tuple-element.61), channel_id=1, source_target_pairs={{0,6},{1,7},{2,8},{3,9},{4,10},{5,11},{6,12},{7,13},{8,14},{9,15},... | collective-permute-start | bytes 663560
  1632.0 50.3 %collective-permute-start.4 = (f32[48,1152]{1,0:T(8,128)S(1)}, f32[48,1152]{1,0:T(8,128)S(1)}, u32[]{:S(2)}, u32[]{:S(2)}) collective-permute-start(f32[48,1152]{1,0:T(8,128)S(1)} %get-tuple-element.61), channel_id=1, source_target_pairs={{0,5},{1,6},{2,7},{3,8},{4,9},{5,10},{6,11},{7,12},{8,13},{9,14},{... | collective-permute-start | bytes 663560
  1641.2 20.0 %collective-permute-start.7 = (f32[36,1152]{1,0:T(8,128)S(1)}, f32[36,1152]{1,0:T(8,128)}, u32[]{:S(2)}, u32[]{:S(2)}) collective-permute-start(f32[36,1152]{1,0:T(8,128)S(1)} %slice.28), channel_id=1, source_target_pairs={{0,8},{1,9},{2,10},{3,11},{4,12},{5,13},{6,14},{7,15},{8,16},{9,17... | collective-permute-start | bytes 497672
  1656.6 7.4 collective-permute-start.15
  1661.2 26.3 %collective-permute-start.3 = (f32[48,1152]{1,0:T(8,128)S(1)}, f32[48,1152]{1,0:T(8,128)S(1)}, u32[]{:S(2)}, u32[]{:S(2)}) collective-permute-start(f32[48,1152]{1,0:T(8,128)S(1)} %get-tuple-element.61), channel_id=1, source_target_pairs={{0,4},{1,5},{2,6},{3,7},{4,8},{5,9},{6,10},{7,11},{8,12},{9,13},{1... | collective-permute-start | bytes 663560
  1663.9 8.3 collective-permute-start.23
  1672.2 17.4 collective-permute-start.2
  1674.6 18.1 collective-permute-start.1
  1678.9 17.6 collective-permute-start
  1682.3 18.4 collective-permute-start.14
  1687.4 14.6 collective-permute-start.13
  1689.6 17.2 collective-permute-start.12
  1692.7 17.4 collective-permute-start.11
  1696.6 17.5 collective-permute-start.10
  1700.7 17.5 collective-permute-start.9
  1702.8 17.1 collective-permute-start.8
  1706.8 75.9 %collective-permute-start.22 = (f32[48,1152]{1,0:T(8,128)}, f32[48,1152]{1,0:T(8,128)S(1)}, u32[]{:S(2)}, u32[]{:S(2)}) collective-permute-start(f32[48,1152]{1,0:T(8,128)} %get-tuple-element.63), channel_id=1, source_target_pairs={{0,7},{1,8},{2,9},{3,10},{4,11},{5,12},{6,13},{7,14},{8,15},{9,16}... | collective-permute-start | bytes 663560
  1710.1 77.5 %collective-permute-start.21 = (f32[48,1152]{1,0:T(8,128)}, f32[48,1152]{1,0:T(8,128)S(1)}, u32[]{:S(2)}, u32[]{:S(2)}) collective-permute-start(f32[48,1152]{1,0:T(8,128)} %get-tuple-element.63), channel_id=1, source_target_pairs={{0,6},{1,7},{2,8},{3,9},{4,10},{5,11},{6,12},{7,13},{8,14},{9,15},... | collective-permute-start | bytes 663560
  1714.1 75.5 %collective-permute-start.20 = (f32[48,1152]{1,0:T(8,128)}, f32[48,1152]{1,0:T(8,128)S(1)}, u32[]{:S(2)}, u32[]{:S(2)}) collective-permute-start(f32[48,1152]{1,0:T(8,128)} %get-tuple-element.63), channel_id=1, source_target_pairs={{0,5},{1,6},{2,7},{3,8},{4,9},{5,10},{6,11},{7,12},{8,13},{9,14},{... | collective-permute-start | bytes 663560
  1718.2 76.0 %collective-permute-start.19 = (f32[48,1152]{1,0:T(8,128)}, f32[48,1152]{1,0:T(8,128)S(1)}, u32[]{:S(2)}, u32[]{:S(2)}) collective-permute-start(f32[48,1152]{1,0:T(8,128)} %get-tuple-element.63), channel_id=1, source_target_pairs={{0,4},{1,5},{2,6},{3,7},{4,8},{5,9},{6,10},{7,11},{8,12},{9,13},{1... | collective-permute-start | bytes 663560
  1719.9 77.5 %collective-permute-start.18 = (f32[48,1152]{1,0:T(8,128)}, f32[48,1152]{1,0:T(8,128)S(1)}, u32[]{:S(2)}, u32[]{:S(2)}) collective-permute-start(f32[48,1152]{1,0:T(8,128)} %get-tuple-element.63), channel_id=1, source_target_pairs={{0,3},{1,4},{2,5},{3,6},{4,7},{5,8},{6,9},{7,10},{8,11},{9,12},{10... | collective-permute-start | bytes 663560
  1782.7 40.1 %collective-permute-start.17 = (f32[48,1152]{1,0:T(8,128)}, f32[48,1152]{1,0:T(8,128)}, u32[]{:S(2)}, u32[]{:S(2)}) collective-permute-start(f32[48,1152]{1,0:T(8,128)} %get-tuple-element.63), channel_id=1, source_target_pairs={{0,2},{1,3},{2,4},{3,5},{4,6},{5,7},{6,8},{7,9},{8,10},{9,11},{10,... | collective-permute-start | bytes 663560
  1787.6 37.5 %collective-permute-start.16 = (f32[48,1152]{1,0:T(8,128)}, f32[48,1152]{1,0:T(8,128)}, u32[]{:S(2)}, u32[]{:S(2)}) collective-permute-start(f32[48,1152]{1,0:T(8,128)} %get-tuple-element.63), channel_id=1, source_target_pairs={{0,1},{1,2},{2,3},{3,4},{4,5},{5,6},{6,7},{7,8},{8,9},{9,10},{10,1... | collective-permute-start | bytes 663560
  1789.6 56.7 %collective-permute-start.30 = (f32[48,1152]{1,0:T(8,128)}, f32[48,1152]{1,0:T(8,128)}, u32[]{:S(2)}, u32[]{:S(2)}) collective-permute-start(f32[48,1152]{1,0:T(8,128)} %get-tuple-element.64), channel_id=1, source_target_pairs={{0,7},{1,8},{2,9},{3,10},{4,11},{5,12},{6,13},{7,14},{8,15},{9,16}... | collective-permute-start | bytes 663560
  1794.2 55.1 %collective-permute-start.29 = (f32[48,1152]{1,0:T(8,128)}, f32[48,1152]{1,0:T(8,128)}, u32[]{:S(2)}, u32[]{:S(2)}) collective-permute-start(f32[48,1152]{1,0:T(8,128)} %get-tuple-element.64), channel_id=1, source_target_pairs={{0,6},{1,7},{2,8},{3,9},{4,10},{5,11},{6,12},{7,13},{8,14},{9,15},... | collective-permute-start | bytes 663560
  1797.4 46.1 %collective-permute-start.31 = (f32[36,1152]{1,0:T(8,128)}, f32[36,1152]{1,0:T(8,128)}, u32[]{:S(2)}, u32[]{:S(2)}) collective-permute-start(f32[36,1152]{1,0:T(8,128)} %slice.31), channel_id=1, source_target_pairs={{0,8},{1,9},{2,10},{3,11},{4,12},{5,13},{6,14},{7,15},{8,16},{9,17... | collective-permute-start | bytes 497672
  1822.8 30.1 %collective-permute-start.28 = (f32[48,1152]{1,0:T(8,128)S(1)}, f32[48,1152]{1,0:T(8,128)S(1)}, u32[]{:S(2)}, u32[]{:S(2)}) collective-permute-start(f32[48,1152]{1,0:T(8,128)S(1)} %copy-done.45), channel_id=1, source_target_pairs={{0,5},{1,6},{2,7},{3,8},{4,9},{5,10},{6,11},{7,12},{8,13},{9,14},{... | collective-permute-start | bytes 663560
  1825.1 32.2 %collective-permute-start.27 = (f32[48,1152]{1,0:T(8,128)S(1)}, f32[48,1152]{1,0:T(8,128)S(1)}, u32[]{:S(2)}, u32[]{:S(2)}) collective-permute-start(f32[48,1152]{1,0:T(8,128)S(1)} %copy-done.45), channel_id=1, source_target_pairs={{0,4},{1,5},{2,6},{3,7},{4,8},{5,9},{6,10},{7,11},{8,12},{9,13},{1... | collective-permute-start | bytes 663560
  1843.6 17.1 collective-permute-start.26
  1846.4 36.7 %collective-permute-start.25 = (f32[48,1152]{1,0:T(8,128)S(1)}, f32[48,1152]{1,0:T(8,128)S(1)}, u32[]{:S(2)}, u32[]{:S(2)}) collective-permute-start(f32[48,1152]{1,0:T(8,128)S(1)} %copy-done.45), channel_id=1, source_target_pairs={{0,2},{1,3},{2,4},{3,5},{4,6},{5,7},{6,8},{7,9},{8,10},{9,11},{10,... | collective-permute-start | bytes 663560
  1849.3 38.5 %collective-permute-start.24 = (f32[48,1152]{1,0:T(8,128)S(1)}, f32[48,1152]{1,0:T(8,128)}, u32[]{:S(2)}, u32[]{:S(2)}) collective-permute-start(f32[48,1152]{1,0:T(8,128)S(1)} %copy-done.45), channel_id=1, source_target_pairs={{0,1},{1,2},{2,3},{3,4},{4,5},{5,6},{6,7},{7,8},{8,9},{9,10},{10,1... | collective-permute-start | bytes 663560
  1852.9 53.3 %collective-permute-start.34 = (f32[40,4304]{1,0:T(8,128)S(1)}, f32[40,4304]{1,0:T(8,128)}, u32[]{:S(2)}, u32[]{:S(2)}) collective-permute-start(f32[40,4304]{1,0:T(8,128)S(1)} %copy-done.30), channel_id=1, source_target_pairs={{0,3},{1,4},{2,5},{3,6},{4,7},{5,8},{6,9},{7,10},{8,11},{9,12},{10... | collective-permute-start | bytes 2065928
  1857.3 49.0 %collective-permute-start.33 = (f32[40,4304]{1,0:T(8,128)S(1)}, f32[40,4304]{1,0:T(8,128)}, u32[]{:S(2)}, u32[]{:S(2)}) collective-permute-start(f32[40,4304]{1,0:T(8,128)S(1)} %copy-done.30), channel_id=1, source_target_pairs={{0,2},{1,3},{2,4},{3,5},{4,6},{5,7},{6,8},{7,9},{8,10},{9,11},{10,... | collective-permute-start | bytes 2065928
  1860.6 45.6 %collective-permute-start.32 = (f32[40,4304]{1,0:T(8,128)S(1)}, f32[40,4304]{1,0:T(8,128)}, u32[]{:S(2)}, u32[]{:S(2)}) collective-permute-start(f32[40,4304]{1,0:T(8,128)S(1)} %copy-done.30), channel_id=1, source_target_pairs={{0,1},{1,2},{2,3},{3,4},{4,5},{5,6},{6,7},{7,8},{8,9},{9,10},{10,1... | collective-permute-start | bytes 2065928
  1883.7 22.5 %collective-permute-start.35 = (f32[4,4304]{1,0:T(4,128)}, f32[4,4304]{1,0:T(4,128)}, u32[]{:S(2)}, u32[]{:S(2)}) collective-permute-start(f32[4,4304]{1,0:T(4,128)} %slice.32), channel_id=1, source_target_pairs={{0,4},{1,5},{2,6},{3,7},{4,8},{5,9},{6,10},{7,11},{8,12},{9,13},{1... | collective-permute-start | bytes 206600
  (145 other events, 2458.3 us)
Sparse Core Ops, SparseCore 0:
  11.0 61.4 all-gather.28
  75.4 57.6 all-gather.32
  136.0 57.4 all-gather.30
  196.3 57.4 all-gather.34
  255.8 22.8 all-gather.24
  280.6 24.0 all-gather.26
  306.3 24.0 all-gather.20
  332.0 24.0 all-gather.22
  358.9 89.6 all-gather.36
  451.4 87.8 all-gather.38
  625.2 44.6 reduce-scatter.16
  927.1 32.4 reduce-scatter.18
  962.8 33.0 reduce-scatter.20
  999.8 32.5 reduce-scatter.22
where the time goes:
time: 1940 us; the launch traced here: 1930 us
  blocking collectives  834 us (43%)
  waiting for transfers between devices  338 us (17%)
  matrix products  286 us (15%)
  starting transfers between devices  210 us (11%)
  local copies, waits for them, and re-layouts  196 us (10%)
  other arithmetic  50.2 us (3%)
    unnamed x4, blocking collectives  834 us
    unnamed x40, starting transfers between devices  209 us
    unnamed x358, local copies, waits for them, and re-layouts  175 us
    dot_general x12, matrix products, outer_sum(): lax.dot_general(left.reshape(-1, left.shape[-1]), right.reshape(-1, right...  95.3 us
    dot_general x12, matrix products, back_dot(): lax.dot_general(grad_rows, weight, (((grad_rows.ndim - 1,), (1,)), ((), (...  53.4 us
    all_gather x1, waiting for transfers between devices, on_device(): lax.all_gather(w_key, ('rows', 'seq'), axis=0, tiled=True)  51.7 us
    all_gather x1, waiting for transfers between devices, on_device(): lax.all_gather(w_up, ('rows', 'seq'), axis=0, tiled=True)  49.3 us
    all_gather x1, waiting for transfers between devices, on_device(): lax.all_gather(w_out, ('rows', 'seq'), axis=0, tiled=True)  47.3 us
  transfers between devices with their start and end apart: 54, of which 12 were waited for; matrix products, arithmetic and copies ran while one was open for 34% of the time, Pallas kernels for 0%

commit v1 on v0

v1 whole, which is shorter than its diff:
```python
import functools

import jax
import jax.numpy as jnp
from jax import lax
from jax.experimental import pallas as pl
from jax.experimental.pallas import tpu as pltpu
from jax.sharding import PartitionSpec as P

H = 16
HD = 72
AXES = ("rows", "seq")
norm_epsilon = 1e-06
BIG = 1e30
LANE = 128
WIN = 256
bf16 = jnp.bfloat16
f32 = jnp.float32
NT = (((1,), (1,)), ((), ()))
TN = (((0,), (0,)), ((), ()))
NN = (((1,), (0,)), ((), ()))


def dot(a, b, dims=NN, out=f32):
    return lax.dot_general(a, b, dims, preferred_element_type=f32).astype(out)


class Places:
    def __init__(self, n_rows, n_seq):
        self.nz, self.ny, self.nx, self.nc = n_rows // 2, 2, n_seq // 2, 2
        every = [
            (z, y, x, c)
            for z in range(self.nz)
            for y in range(2)
            for x in range(2)
            for c in range(2)
        ]
        nz = self.nz

        def flat(z, y, x, c):
            return ((z * 2 + y) * 2 + x) * 2 + c

        def pairs(f):
            return [(flat(*t), flat(*f(*t))) for t in every]

        self.to_core = pairs(lambda z, y, x, c: (z, y, x, 1 - c))
        self.to_x = pairs(lambda z, y, x, c: (z, y, 1 - x, c))
        self.to_y = pairs(lambda z, y, x, c: (z, 1 - y, x, c))
        self.to_z = pairs(lambda z, y, x, c: ((z + 1) % nz, y, x, c))
        r, s = lax.axis_index("rows"), lax.axis_index("seq")
        self.z, self.y, self.x, self.c = r // 2, r % 2, s // 2, s % 2


def send(value, pairs):
    return lax.ppermute(value, AXES, pairs)


def place_kernel(n_in, n_dyn, plan, *refs):
    dyn = refs[0]
    ins, out, sem = refs[1 : 1 + n_in], refs[1 + n_in], refs[2 + n_in]
    d = [dyn[i] for i in range(n_dyn)]
    copies = []
    for j, (i, src, dst) in enumerate(plan):
        copies.append(pltpu.make_async_copy(ins[i].at[src], out.at[dst(*d)], sem.at[j]))
    for copy in copies:
        copy.start()
    for copy in copies:
        copy.wait()


def place(at, ins, plan, block):
    rows, cols = block
    dyn = jnp.stack([at.z, at.y, at.x]).astype(jnp.int32)
    shape = (at.nz, 2, 2, rows, cols)
    if rows % 8 == 0:
        out = pl.pallas_call(
            functools.partial(place_kernel, len(ins), 3, plan),
            out_shape=jax.ShapeDtypeStruct(shape, ins[0].dtype),
            in_specs=[pl.BlockSpec(memory_space=pltpu.SMEM)]
            + [pl.BlockSpec(memory_space=pl.ANY)] * len(ins),
            out_specs=pl.BlockSpec(memory_space=pltpu.VMEM),
            scratch_shapes=[pltpu.SemaphoreType.DMA((len(plan),))],
            compiler_params=pltpu.CompilerParams(vmem_limit_bytes=16 * 1024 * 1024),
            cost_estimate=pl.CostEstimate(
                flops=0,
                bytes_accessed=4 * at.nz * 4 * rows * cols,
                transcendentals=0,
            ),
        )(dyn, *ins)
    else:
        out = jnp.zeros(shape, ins[0].dtype)
        for i, src, dst in plan:
            piece = ins[i][src]
            out = lax.dynamic_update_slice(
                out, piece[None, None, None], (*dst(at.z, at.y, at.x), 0, 0)
            )
    return out.reshape(at.nz * 4 * rows, cols)


def ring(at, value):
    held = [value]
    for _ in range(at.nz - 1):
        value = send(value, at.to_z)
        held.append(value)
    return held


def flip(here, by):
    return here + by - 2 * by * here


def gather(at, mine, order):
    rows, cols = mine.shape
    nz = at.nz
    plan = []
    first, second = (at.to_x, at.to_y) if order in ("zxy", "xzy") else (at.to_y, at.to_x)
    x_first = order in ("zxy", "xzy")

    def slot(k, a, b):
        dx, dy = (a, b) if x_first else (b, a)
        return lambda z, y, x: (lax.rem(z - k + nz, nz), flip(y, dy), flip(x, dx))

    if order[0] == "z":
        line = jnp.stack(ring(at, mine))
        one = send(line, first)
        two = send(line, second)
        both = send(one, second)
        ins = [line, one, two, both]
        for i, (a, b) in enumerate(((0, 0), (1, 0), (0, 1), (1, 1))):
            for k in range(nz):
                plan.append((i, (k,), slot(k, a, b)))
    else:
        pair = jnp.stack([mine, send(mine, first)])
        line = ring(at, pair)
        ins = line + [send(v, second) for v in line]
        for b in range(2):
            for k in range(nz):
                for a in range(2):
                    plan.append((b * nz + k, (a,), slot(k, a, b)))
    return place(at, ins, plan, (rows, cols))


def relative_order(at, order, chip_rows, width):
    nz = at.nz
    place_of = jnp.arange(width, dtype=jnp.int32)
    block, row = place_of // chip_rows, place_of % chip_rows
    if order == "yzx":
        b, k, a = block // (2 * nz), (block // 2) % nz, block % 2
    elif order == "xzy":
        a, k, b = block // (2 * nz), (block // 2) % nz, block % 2
    elif order == "yxz":
        b, a, k = block // (2 * nz), (block // nz) % 2, block % nz
    else:
        a, b, k = block // (2 * nz), (block // nz) % 2, block % nz
    z = (at.z - 1 - k + 2 * nz) % nz
    natural = ((z * 2 + flip(at.y, b)) * 2 + flip(at.x, a)) * chip_rows + row
    return (jnp.arange(width, dtype=jnp.int32)[:, None] == natural[None, :]).astype(bf16)


def scatter(at, left_own, right_own, left_peer, right_peer, order):
    width = left_own.shape[1]
    n = right_own.shape[1]
    half = width // 2
    first = at.to_y if order[0] == "y" else at.to_x
    from_core = send(dot(left_peer, right_peer, TN, bf16), at.to_core)
    going = (dot(left_own[:, half:], right_own, TN) + from_core[half:].astype(f32)).astype(bf16)
    came = send(going, first)
    kept = (
        dot(left_own[:, :half], right_own, TN)
        + from_core[:half].astype(f32)
        + came.astype(f32)
    ).astype(bf16)
    if order[2] == "z":
        second = at.to_x if order[1] == "x" else at.to_y
        quarter = half // 2
        kept = (
            kept[:quarter].astype(f32) + send(kept[quarter:], second).astype(f32)
        ).astype(bf16)
        kept = kept.reshape(at.nz, quarter // at.nz, n)
        total = kept[0]
        for k in range(1, at.nz):
            total = send(total.astype(bf16), at.to_z).astype(f32) + kept[k].astype(f32)
    else:
        second = at.to_x if order[2] == "x" else at.to_y
        kept = kept.reshape(at.nz, 2, half // at.nz // 2, n)
        total = kept[0]
        for k in range(1, at.nz):
            total = send(total.astype(bf16), at.to_z).astype(f32) + kept[k].astype(f32)
        total = total[0] + send(total[1].astype(bf16), second).astype(f32)
    rows = total.shape[0] // 2
    mine = jnp.where(at.c == 0, total[:rows], total[rows:])
    theirs = jnp.where(at.c == 0, total[rows:], total[:rows])
    return mine, send(theirs, at.to_core)


def window(h):
    tile = jnp.minimum((h * HD) // LANE, (H * HD - WIN) // LANE)
    start = pl.multiple_of(tile * LANE, LANE)
    return start, h * HD - start


def head_masks(h, rows):
    start, off = window(h)
    lane = lax.broadcasted_iota(jnp.int32, (rows, WIN), 1)
    inside = (lane >= off) & (lane < off + HD)
    at = jnp.where(off > WIN - HD - 4, 0, WIN - 4)
    feature = (lane >= at) & (lane < at + 4)
    return start, inside, feature


def attend_kernel(q_ref, ko_ref, kr_ref, vo_ref, vr_ref, qf_ref, kf_ref, out_ref, lse_ref, acc):
    t, n = q_ref.shape[0], ko_ref.shape[0]
    acc[...] = jnp.zeros_like(acc)
    scale = (HD ** -0.5) * 1.4426950408889634
    zero = jnp.zeros((), bf16)

    def head(h, carry):
        start, in_k, feat_k = head_masks(h, n)
        _, _, feat_q = head_masks(h, t)
        at = pl.ds(start, WIN)
        q = jnp.where(feat_q, qf_ref[...], q_ref[:, at])
        keys, vals = [], []
        for i, (kref, vref) in enumerate(((ko_ref, vo_ref), (kr_ref, vr_ref))):
            feats = jnp.where(feat_k, kf_ref[i * n : (i + 1) * n, :], zero)
            keys.append(jnp.where(in_k, kref[:, at], feats))
            vals.append(jnp.where(in_k, vref[:, at], zero))
        k = jnp.concatenate(keys, axis=0)
        v_t = jnp.concatenate(vals, axis=0).T
        s = lax.dot_general(k, q, NT, preferred_element_type=f32)
        top = jnp.max(s, axis=0, keepdims=True) * scale
        p = jnp.exp2(s * scale - top)
        total = jnp.sum(p, axis=0, keepdims=True)
        o_t = lax.dot_general(v_t, p.astype(bf16), NN, preferred_element_type=f32)
        acc[:, at] += (o_t / total).T
        lse_ref[pl.ds(h, 1), :] = top + jnp.log2(total)
        return carry

    lax.fori_loop(0, H, head, 0)
    out_ref[...] = acc[...].astype(bf16)


def attend(q, ko, kr, vo, vr, qf, kf):
    t, d = q.shape
    return pl.pallas_call(
        attend_kernel,
        out_shape=(
            jax.ShapeDtypeStruct((t, d), bf16),
            jax.ShapeDtypeStruct((H, t), f32),
        ),
        scratch_shapes=[pltpu.VMEM((t, d), f32)],
        compiler_params=pltpu.CompilerParams(vmem_limit_bytes=48 * 1024 * 1024),
        cost_estimate=pl.CostEstimate(
            flops=4 * H * t * 2 * t * WIN, bytes_accessed=12 * t * d, transcendentals=H * t * 2 * t
        ),
    )(q, ko, kr, vo, vr, qf, kf)


def back_kernel(
    q_ref, ko_ref, kr_ref, vo_ref, vr_ref, do_ref, qf_ref, kf_ref, lse_ref,
    dq_ref, dko_ref, dvo_ref, dkr_ref, dvr_ref, dq, dk, dv,
):
    t, n = q_ref.shape[0], ko_ref.shape[0]
    scale = HD ** -0.5
    scale_two = scale * 1.4426950408889634
    zero = jnp.zeros((), bf16)
    dq[...] = jnp.zeros_like(dq)
    dk[...] = jnp.zeros_like(dk)
    dv[...] = jnp.zeros_like(dv)

    def head(h, carry):
        start, in_k, feat_k = head_masks(h, n)
        _, in_q, feat_q = head_masks(h, t)
        at = pl.ds(start, WIN)
        q_win = q_ref[:, at]
        q = jnp.where(feat_q, qf_ref[...], q_win)
        q_only = jnp.where(in_q, q_win, zero)
        do = jnp.where(in_q, do_ref[:, at], zero)
        keys, vals, only = [], [], []
        for i, (kref, vref) in enumerate(((ko_ref, vo_ref), (kr_ref, vr_ref))):
            feats = jnp.where(feat_k, kf_ref[i * n : (i + 1) * n, :], zero)
            k_win = kref[:, at]
            keys.append(jnp.where(in_k, k_win, feats))
            only.append(jnp.where(in_k, k_win, zero))
            vals.append(vref[:, at])
        k = jnp.concatenate(keys, axis=0)
        k_t = jnp.concatenate(only, axis=0).T
        v = jnp.concatenate(vals, axis=0)
        s = lax.dot_general(k, q, NT, preferred_element_type=f32)
        p = jnp.exp2(s * scale_two - lse_ref[pl.ds(h, 1), :])
        dp = lax.dot_general(v, do, NT, preferred_element_type=f32)
        dv[:, at] += lax.dot_general(p.astype(bf16), do, NN, preferred_element_type=f32)
        inner = jnp.sum(p * dp, axis=0, keepdims=True)
        ds = (p * (dp - inner)).astype(bf16)
        dk[:, at] += lax.dot_general(ds, q_only, NN, preferred_element_type=f32)
        dq[:, at] += lax.dot_general(k_t, ds, NN, preferred_element_type=f32).T
        return carry

    lax.fori_loop(0, H, head, 0)
    dq_ref[...] = (dq[...] * scale).astype(bf16)
    dko_ref[...] = (dk[:n, :] * scale).astype(bf16)
    dkr_ref[...] = (dk[n:, :] * scale).astype(bf16)
    dvo_ref[...] = dv[:n, :].astype(bf16)
    dvr_ref[...] = dv[n:, :].astype(bf16)


def attend_back(q, ko, kr, vo, vr, do, qf, kf, lse):
    t, d = q.shape
    n = ko.shape[0]
    return pl.pallas_call(
        back_kernel,
        out_shape=(jax.ShapeDtypeStruct((t, d), bf16),)
        + (jax.ShapeDtypeStruct((n, d), bf16),) * 4,
        scratch_shapes=[
            pltpu.VMEM((t, d), f32),
            pltpu.VMEM((2 * n, d), f32),
            pltpu.VMEM((2 * n, d), f32),
        ],
        compiler_params=pltpu.CompilerParams(vmem_limit_bytes=60 * 1024 * 1024),
        cost_estimate=pl.CostEstimate(
            flops=10 * H * t * 2 * n * WIN,
            bytes_accessed=24 * t * d,
            transcendentals=H * t * 2 * n,
        ),
    )(q, ko, kr, vo, vr, do, qf, kf, lse)


def norm_parts(values):
    center = jnp.mean(values, axis=-1, keepdims=True)
    centered = values - center
    spread = jnp.mean(centered * centered, axis=-1, keepdims=True)
    inverse = lax.rsqrt(spread + norm_epsilon)
    return centered * inverse, inverse


def norm_back(incoming, gain, unit, inverse):
    scaled = incoming * gain
    return (
        scaled
        - jnp.mean(scaled, axis=-1, keepdims=True)
        - unit * jnp.mean(scaled * unit, axis=-1, keepdims=True)
    ) * inverse


def column_sum(rows):
    return jnp.sum(rows.astype(f32), axis=0)


def gelu_and_slope(z):
    root = 0.7978845608028654
    cube = 0.044715
    t = jnp.tanh(root * (z + cube * z * z * z))
    value = 0.5 * z * (1.0 + t)
    slope = 0.5 * (1.0 + t) + 0.5 * z * (1.0 - t * t) * root * (1.0 + 3.0 * cube * z * z)
    return value, slope


def lane_cut(width):
    tiles = width // LANE
    one = (tiles * 65) // 100
    return one * LANE


def on_device(
    tokens,
    lengths,
    norm1_gain,
    norm1_bias,
    w_query,
    query_bias,
    w_key,
    w_value,
    value_bias,
    w_out,
    out_bias,
    norm2_gain,
    norm2_bias,
    w_up,
    up_bias,
    w_down,
    down_bias,
    cotangent,
):
    at = Places(lax.axis_size("rows"), lax.axis_size("seq"))
    micro, rows_here, local_len, width = tokens.shape
    full_len = local_len * lax.axis_size("seq")
    own_rows, hidden_width = w_up.shape
    chip_rows = 2 * own_rows
    zero_core = at.c == 0

    def by_core(a, b):
        return jnp.where(zero_core, a, b)

    vectors = jnp.stack(
        [norm1_gain, norm1_bias, query_bias, value_bias, out_bias, norm2_gain, norm2_bias, down_bias]
    )
    vectors = lax.all_gather(vectors, AXES, axis=0)
    vectors = jnp.swapaxes(vectors, 0, 1).reshape(8, width).astype(f32)
    gain_one, shift_one, bias_q, bias_v, bias_o, gain_two, shift_two, bias_d = [
        vectors[i][None] for i in range(8)
    ]

    def swap_in(values):
        mine = lax.dynamic_index_in_dim(values, at.x, 0, keepdims=False)
        theirs = lax.dynamic_index_in_dim(values, 1 - at.x, 0, keepdims=False)
        came = send(theirs, at.to_x)
        low = jnp.where(at.x == 0, mine, came)
        high = jnp.where(at.x == 0, came, mine)
        return jnp.stack([low, high]).reshape(2 * rows_here * local_len, width)

    def swap_out(values):
        values = values.reshape(2, rows_here, local_len, width)
        mine = lax.dynamic_index_in_dim(values, at.x, 0, keepdims=False)
        theirs = lax.dynamic_index_in_dim(values, 1 - at.x, 0, keepdims=False)
        came = send(theirs.astype(bf16), at.to_x).astype(mine.dtype)
        return jnp.stack([jnp.where(at.x == 0, mine, came), jnp.where(at.x == 0, came, mine)])

    half_width = -(-hidden_width // (2 * LANE)) * LANE
    cut = lane_cut(half_width)
    up_full = jnp.pad(w_up, ((0, 0), (0, 2 * half_width - hidden_width)))
    eye = jnp.eye(own_rows, dtype=bf16)
    down_t = dot(eye, w_down, NT, bf16)
    down_full = jnp.pad(down_t, ((0, 0), (0, 2 * half_width - hidden_width)))
    low = [w_query, w_key, up_full[:, :half_width], down_full[:, :half_width]]
    high = [w_value, w_out, up_full[:, half_width:], down_full[:, half_width:]]
    low, high = jnp.concatenate(low, axis=1), jnp.concatenate(high, axis=1)
    keep, give = by_core(low, high), by_core(high, low)
    both = jnp.concatenate([keep, send(give, at.to_core)], axis=0)
    spot = jnp.arange(chip_rows, dtype=jnp.int32)
    spot = flip(at.c, spot // own_rows) * own_rows + spot % own_rows
    turn = (jnp.arange(chip_rows, dtype=jnp.int32)[:, None] == spot[None, :]).astype(bf16)
    ends = [0, width, 2 * width]
    ends += [ends[-1] + cut, ends[-1] + half_width]
    ends += [ends[-1] + cut, ends[-1] + half_width]
    shards = [dot(turn, both[:, a:b], NN, bf16) for a, b in zip(ends[:-1], ends[1:])]
    x_in = swap_in(tokens)
    grad_out = swap_in(cotangent)

    orders = ["zxy", "zyx", "xzy", "yzx", "xzy", "yzx"]
    own = [gather(at, s, o) for s, o in zip(shards, orders)]
    other = [send(w, at.to_core) for w in own]
    weight_q, weight_v = by_core(own[0], other[0]), by_core(other[0], own[0])
    weight_k, weight_o = by_core(own[1], other[1]), by_core(other[1], own[1])
    up_parts = [own[2], own[3], other[2], other[3]]
    down_parts = [own[4], own[5], other[4], other[5]]
    bias_up = jnp.pad(up_bias.astype(f32), (0, 2 * half_width - hidden_width))
    bias_own = by_core(bias_up[:half_width], bias_up[half_width:])
    bias_other = by_core(bias_up[half_width:], bias_up[:half_width])
    bias_parts = [bias_own[:cut], bias_own[cut:], bias_other[:cut], bias_other[cut:]]

    row_lengths = lax.dynamic_index_in_dim(lengths, at.x, 0, keepdims=False)[0]
    ends_at = jnp.cumsum(row_lengths)
    inside = jnp.arange(2 * local_len, dtype=jnp.int32)
    def segment_of(core):
        spots = (inside // local_len) * (full_len // 2) + core * local_len + inside % local_len
        return jnp.sum((spots[:, None] >= ends_at[None, :]).astype(jnp.int32), axis=-1)
    seg_own, seg_other = segment_of(at.c), segment_of(1 - at.c)
    lane = (jnp.arange(WIN, dtype=jnp.int32) % 4)[None, :]
    feat_q = (seg_own[:, None] == lane).astype(bf16)
    seg_keys = jnp.concatenate([seg_own, seg_other])
    feat_k = jnp.where(seg_keys[:, None] == lane, 0.0, -BIG).astype(bf16)

    inputs = x_in.astype(f32)
    unit_one, inverse_one = norm_parts(inputs)
    normed = (unit_one * gain_one + shift_one).astype(bf16)
    queries = (dot(normed, weight_q) + bias_q).astype(bf16)
    keys = dot(normed, weight_k, NN, bf16)
    values = (dot(normed, weight_v) + bias_v).astype(bf16)
    keys_other, values_other = send(keys, at.to_core), send(values, at.to_core)
    attended, lse = attend(queries, keys, keys_other, values, values_other, feat_q, feat_k)
    residual_one = inputs + dot(attended, weight_o) + bias_o
    unit_two, inverse_two = norm_parts(residual_one)
    normed_two = (unit_two * gain_two + shift_two).astype(bf16)
    active, slopes = [], []
    for w, b in zip(up_parts, bias_parts):
        value, slope = gelu_and_slope(dot(normed_two, w) + b[None])
        active.append(value.astype(bf16))
        slopes.append(slope.astype(bf16))
    result = residual_one + bias_d
    for a, w in zip(active, down_parts):
        result = result + dot(a, w, NT)
    block_output = swap_out(result.astype(bf16))

    order_y = relative_order(at, "yzx", chip_rows, width)
    order_x = relative_order(at, "xzy", chip_rows, width)
    order_one = relative_order(at, "yxz", chip_rows, width)
    order_two = relative_order(at, "xyz", chip_rows, width)
    out_y, out_x = dot(grad_out, order_y, NN, bf16), dot(grad_out, order_x, NN, bf16)
    d_down = [
        scatter(at, out_y, active[0], out_y, active[2], "yzx"),
        scatter(at, out_x, active[1], out_x, active[3], "xzy"),
    ]
    grad_hidden = [
        (dot(grad_out, w) * s.astype(f32)).astype(bf16) for w, s in zip(down_parts, slopes)
    ]
    two_y, two_x = dot(normed_two, order_y, NN, bf16), dot(normed_two, order_x, NN, bf16)
    d_up = [
        scatter(at, two_y, grad_hidden[0], two_y, grad_hidden[2], "yzx"),
        scatter(at, two_x, grad_hidden[1], two_x, grad_hidden[3], "xzy"),
    ]
    grad_normed_two = dot(grad_hidden[0], up_parts[0], NT)
    for g, w in zip(grad_hidden[1:], up_parts[1:]):
        grad_normed_two = grad_normed_two + dot(g, w, NT)
    grad_residual = grad_out.astype(f32) + norm_back(
        grad_normed_two, gain_two, unit_two, inverse_two
    )
    grad_branch = grad_residual.astype(bf16)
    grad_attended = dot(grad_branch, weight_o, NT, bf16)
    grad_q, gko, gvo, gkr, gvr = attend_back(
        queries, keys, keys_other, values, values_other, grad_attended, feat_q, feat_k, lse
    )
    grad_k = (gko.astype(f32) + send(gkr, at.to_core).astype(f32)).astype(bf16)
    grad_v = (gvo.astype(f32) + send(gvr, at.to_core).astype(f32)).astype(bf16)
    one = dot(normed, order_one, NN, bf16)
    two = dot(normed, order_two, NN, bf16)
    attended_two = dot(attended, order_two, NN, bf16)
    d_qv = scatter(at, one, by_core(grad_q, grad_v), one, by_core(grad_v, grad_q), "yxz")
    d_ko = scatter(
        at,
        by_core(two, attended_two),
        by_core(grad_k, grad_branch),
        by_core(attended_two, two),
        by_core(grad_branch, grad_k),
        "xyz",
    )
    grad_normed = (
        dot(grad_q, weight_q, NT) + dot(grad_k, weight_k, NT) + dot(grad_v, weight_v, NT)
    )
    grad_tokens = grad_residual + norm_back(grad_normed, gain_one, unit_one, inverse_one)
    grad_tokens = swap_out(grad_tokens)

    hidden_sums = [column_sum(g) for g in grad_hidden]
    own_sums = jnp.concatenate(hidden_sums[:2])
    other_sums = jnp.concatenate(hidden_sums[2:])
    up_sums = jnp.concatenate([by_core(own_sums, other_sums), by_core(other_sums, own_sums)])
    early = jnp.concatenate(
        [
            column_sum(grad_out),
            column_sum(grad_branch),
            column_sum(grad_normed_two * unit_two),
            column_sum(grad_normed_two),
            up_sums,
        ]
    )
    late = jnp.concatenate(
        [
            column_sum(grad_q),
            column_sum(grad_v),
            column_sum(grad_normed * unit_one),
            column_sum(grad_normed),
        ]
    )
    early = lax.psum(early, AXES)
    late = lax.psum(late, AXES)
    my_start = (lax.axis_index("rows") * lax.axis_size("seq") + lax.axis_index("seq")) * own_rows

    def my_part(vector, i):
        return lax.dynamic_slice_in_dim(vector, i * width + my_start, own_rows)

    d_up_bias = early[4 * width : 4 * width + hidden_width]

    def halves(parts):
        mine = jnp.concatenate([p[0] for p in parts], axis=1)
        theirs = jnp.concatenate([p[1] for p in parts], axis=1)
        both = jnp.concatenate([by_core(mine, theirs), by_core(theirs, mine)], axis=1)
        return both[:, :hidden_width]

    d_w_up = halves(d_up)
    d_w_down = halves(d_down).T
    return (
        block_output,
        grad_tokens,
        my_part(late, 2),
        my_part(late, 3),
        by_core(d_qv[0], d_qv[1]),
        my_part(late, 0),
        by_core(d_ko[0], d_ko[1]),
        by_core(d_qv[1], d_qv[0]),
        my_part(late, 1),
        by_core(d_ko[1], d_ko[0]),
        my_part(early, 1),
        my_part(early, 2),
        my_part(early, 3),
        d_w_up,
        d_up_bias,
        d_w_down,
        my_part(early, 0),
    )


def solution(mesh):
    feature = P(AXES)
    matrix = P(AXES, None)
    row = P(None, "rows", "seq", None)
    return jax.shard_map(
        on_device,
        mesh=mesh,
        in_specs=(
            row,
            P(None, "rows", None),
            feature,
            feature,
            matrix,
            feature,
            matrix,
            matrix,
            feature,
            matrix,
            feature,
            feature,
            feature,
            matrix,
            P(),
            P(None, AXES),
            feature,
            row,
        ),
        out_specs=(
            row,
            row,
            feature,
            feature,
            matrix,
            feature,
            matrix,
            matrix,
            feature,
            matrix,
            feature,
            feature,
            feature,
            matrix,
            P(),
            P(None, AXES),
            feature,
        ),
        check_vma=False,
    )
```

time: 1940 us -> 812 us (0.42)
  blocking collectives: 834 us -> 107 us
  local copies, waits for them, and re-layouts: 196 us -> 19.5 us
  starting transfers between devices: 210 us -> 55.2 us
  matrix products: 286 us -> 143 us
  Pallas kernels: 0 us -> 92.5 us
  other arithmetic: 50.2 us -> 30.7 us
    unnamed x4 -> x0, blocking collectives: 834 us -> none
    ppermute x0 -> x101, waiting for transfers between devices: none -> 352 us  [send(): return lax.ppermute(value, AXES, pairs)]
    all_gather x10 -> x0, waiting for transfers between devices: 331 us -> none  [the longest x1 51.7 us: on_device(): lax.all_gather(w_key, ('rows', 'seq'), axis=0, tiled=True)]
    unnamed x40 -> x0, starting transfers between devices: 209 us -> none
    unnamed x358 -> x194, local copies, waits for them, and re-layouts: 175 us -> 11 us
    dot_general x48 -> x56, matrix products: 286 us -> 143 us  [dot(): return lax.dot_general(a, b, dims, preferred_element_type=f32).astype(out)]
    pallas_call x0 -> x8, Pallas kernels: none -> 92.5 us  [the longest x1 40.6 us: attend_back(): pl.pallas_call(back_kernel, out_shape=(jax.ShapeDtypeStruct((t, d), bf16)...]
    all_gather x0 -> x1, blocking collectives: none -> 59.2 us  [on_device(): vectors = lax.all_gather(vectors, AXES, axis=0)]
  transfers between devices with their start and end apart: 54 -> 101, of which waited for: 12 -> 50; matrix products, arithmetic and copies ran while one was open for 34% -> 21% of each run, Pallas kernels for 0% -> 12%
where the time goes in v1:
time: 812 us; the launch traced here: 803 us
  waiting for transfers between devices  352 us (43%)
  matrix products  143 us (18%)
  blocking collectives  107 us (13%)
  Pallas kernels  92.5 us (11%)
  starting transfers between devices  55.2 us (7%)
  other arithmetic  30.7 us (4%)
  local copies, waits for them, and re-layouts  19.5 us (2%)
    ppermute x101, waiting for transfers between devices, send(): return lax.ppermute(value, AXES, pairs)  352 us
    dot_general x56, matrix products, dot(): return lax.dot_general(a, b, dims, preferred_element_type=f32).astype(out)  143 us
    all_gather x1, blocking collectives, on_device(): vectors = lax.all_gather(vectors, AXES, axis=0)  59.2 us
    ppermute x101, starting transfers between devices, send(): return lax.ppermute(value, AXES, pairs)  55.2 us
    psum x1, blocking collectives, on_device(): late = lax.psum(late, AXES)  47.8 us
    pallas_call x1, Pallas kernels, attend_back(): pl.pallas_call(back_kernel, out_shape=(jax.ShapeDtypeStruct((t, d), bf16)...  40.6 us
    pallas_call x6, Pallas kernels, place(): pl.pallas_call(functools.partial(place_kernel, len(ins), 3, plan), out_sh...  27.1 us
    pallas_call x1, Pallas kernels, attend(): pl.pallas_call(attend_kernel, out_shape=(jax.ShapeDtypeStruct((t, d), bf1...  24.8 us
  transfers between devices with their start and end apart: 101, of which 50 were waited for; matrix products, arithmetic and copies ran while one was open for 21% of the time, Pallas kernels for 12%

profile of v1, /device:TPU:0, one launch (start us, length us, event | category | flops | bytes accessed | tf_op | source)
XLA Modules:
  0.0 803.1 jit_solution(16142455568787103339)
XLA Ops:
  10.2 59.2 %all-gather = bf16[256,36]{1,0:T(8,128)(2,1)S(1)} all-gather(bf16[8,36]{1,0:T(8,128)(2,1)S(1)} %stack.172), channel_id=2, replica_groups=mesh['rows'=8,'seq'=4] {'rows','seq'}, dimensions={0}, use_global_device_ids=true | all-gather | bytes 19008 | tf_op jit(solution)/shard_map/all_gather | solution.py:396
  72.3 8.6 %collective-permute-done.2 = bf16[72,1152]{1,0:T(8,128)(2,1)S(1)} collective-permute-done((bf16[72,1152]{1,0:T(8,128)(2,1)S(1)}, bf16[72,1152]{1,0:T(8,128)(2,1)S(1)}, u32[]{:S(2)}, u32[]{:S(2)}) %collective-permute-start.2) | collective-permute-done | bytes 165920 | tf_op jit(solution)/shard_map/ppermute | solution.py:55
  83.9 4.3 collective-permute-done.3
  88.4 4.4 collective-permute-done.10
  96.2 3.8 collective-permute-done.11
  102.2 3.7 collective-permute-done.34
  107.7 5.7 collective-permute-done.5.refs_2_
  121.4 13.0 %collective-permute-done.6.refs_3_ = bf16[4,72,1152]{2,1,0:T(8,128)(2,1)S(1)} collective-permute-done((bf16[4,72,1152]{2,1,0:T(8,128)(2,1)S(1)}, bf16[4,72,1152]{2,1,0:T(8,128)(2,1)S(1)}, u32[]{:S(2)}, u32[]{:S(2)}) %collective-permute-start.6) | collective-permute-done | bytes 663584 | tf_op jit(solution)/shard_map/ppermute | solution.py:55
  134.4 11.6 %collective-permute-done.7.refs_4_ = bf16[4,72,1152]{2,1,0:T(8,128)(2,1)S(1)} collective-permute-done((bf16[4,72,1152]{2,1,0:T(8,128)(2,1)S(1)}, bf16[4,72,1152]{2,1,0:T(8,128)(2,1)S(1)}, u32[]{:S(2)}, u32[]{:S(2)}) %collective-permute-start.7) | collective-permute-done | bytes 663584 | tf_op jit(solution)/shard_map/ppermute | solution.py:55
  146.0 4.1 shard_map.305
  151.1 4.1 shard_map.306
  155.9 4.8 collective-permute-done.43.refs_2_
  160.7 5.2 collective-permute-done.35.refs_2_
  173.0 3.2 collective-permute-done.36.refs_3_
  177.9 9.1 %collective-permute-done.27.refs_2_ = bf16[2,72,1408]{2,1,0:T(8,128)(2,1)S(1)} collective-permute-done((bf16[2,72,1408]{2,1,0:T(8,128)(2,1)S(1)}, bf16[2,72,1408]{2,1,0:T(8,128)(2,1)S(1)}, u32[]{:S(2)}, u32[]{:S(2)}) %collective-permute-start.27) | collective-permute-done | bytes 405536 | tf_op jit(solution)/shard_map/ppermute | solution.py:55
  191.3 4.5 collective-permute-done.19.refs_2_
  197.7 3.7 collective-permute-done.45.refs_4_
  206.3 5.1 collective-permute-done.37.refs_4_
  220.2 5.2 collective-permute-done.20.refs_3_
  241.0 3.5 collective-permute-done.33.refs_8_
  249.9 4.2 shard_map.311
  254.1 4.3 shard_map.310
  258.4 5.2 shard_map.309
  264.1 3.4 collective-permute-done.25.refs_8_
  267.5 5.2 shard_map.308
  277.5 24.8 %shard_map.307 = (bf16[512,1152]{1,0:T(8,128)(2,1)S(1)}, f32[16,512]{1,0:T(8,128)S(1)}) custom-call(bf16[512,1152]{1,0:T(8,128)(2,1)S(1)} %fusion.21.q_ref, bf16[512,1152]{1,0:T(8,128)(2,1)S(1)} %copy-done.8, bf16[512,1152]{1,0:T(8,128)(2,1)S(1)} %copy-done.10, bf16[512,1152]{1,0:T(8,128)(2,1)} %copy-done.72, ...), custom_call_target="tpu_custom_call" | custom-call | flops 8589934592 | bytes 7077888 | tf_op jit(solution)/shard_map/pallas_call | solution.py:244
  303.3 4.9 fusion.200
  313.7 3.4 fusion.191
  324.2 4.7 convolution_add_fusion.10
  329.0 4.3 convert_reduce_fusion.8
  333.3 3.9 convolution_convert_fusion
  339.9 6.5 fusion.189
  346.3 3.3 convert_reduce_fusion.1
  349.7 3.5 fusion.188
  353.2 4.8 fusion.20
  363.1 5.6 convert_reduce_fusion
  368.7 3.7 convolution_convert_fusion.1
  377.1 3.3 convert_reduce_fusion.7
  385.5 4.1 fusion.202
  389.6 3.0 multiply_reduce_fusion
  396.1 3.1 convolution_convert_fusion.7.do_ref
  399.2 40.6 %shard_map.312 = (bf16[512,1152]{1,0:T(8,128)(2,1)}, bf16[512,1152]{1,0:T(8,128)(2,1)}, bf16[512,1152]{1,0:T(8,128)(2,1)}, bf16[512,1152]{1,0:T(8,128)(2,1)}, bf16[512,1152]{1,0:T(8,128)(2,1)}) custom-call(bf16[512,1152]{1,0:T(8,128)(2,1)} %copy-done.12, bf16[512,1152]{1,0:T(8,128)(2,1)} %copy-done.7, bf16[512,1152]{1,0:T(8,128)(2,1)} %copy-done.9, ...), custom_call_target="tpu_custom_call" | custom-call | flops 21474836480 | bytes 14155776 | tf_op jit(solution)/shard_map/pallas_call | solution.py:309
  440.3 3.2 fusion.27
  443.5 3.4 broadcast_select_fusion.5
  469.0 47.8 %all-reduce.3 = (f32[4608]{0:T(1024)S(1)}, f32[8960]{0:T(1024)S(1)}) all-reduce(f32[4608]{0:T(1024)S(1)} %pad_maximum_fusion.18, f32[8960]{0:T(1024)S(1)} %select_dynamic-update-slice_fusion), channel_id=1, replica_groups=mesh['rows'=8,'seq'=4] {'rows','seq'}, use_global_device_ids=true, to_apply=%region_15.16 | all-reduce | flops 13568 | bytes 108544 | tf_op jit(solution)/shard_map/psum | solution.py:553
  518.6 3.5 convolution_convert_fusion.3
  534.0 15.2 %collective-permute-done.80 = bf16[576,768]{1,0:T(8,128)(2,1)S(1)} collective-permute-done((bf16[576,768]{1,0:T(8,128)(2,1)S(1)}, bf16[576,768]{1,0:T(8,128)(2,1)S(1)}, u32[]{:S(2)}, u32[]{:S(2)}) %collective-permute-start.80) | collective-permute-done | bytes 884768 | tf_op jit(solution)/shard_map/ppermute | solution.py:55
  550.7 17.1 %collective-permute-done.94 = bf16[576,768]{1,0:T(8,128)(2,1)S(1)} collective-permute-done((bf16[576,768]{1,0:T(8,128)(2,1)S(1)}, bf16[576,768]{1,0:T(8,128)(2,1)S(1)}, u32[]{:S(2)}, u32[]{:S(2)}) %collective-permute-start.94) | collective-permute-done | bytes 884768 | tf_op jit(solution)/shard_map/ppermute | solution.py:55
  571.1 5.7 collective-permute-done.81
  576.9 8.1 %collective-permute-done.95 = bf16[2,72,768]{2,1,0:T(8,128)(2,1)S(1)} collective-permute-done((bf16[2,72,768]{2,1,0:T(8,128)(2,1)S(1)}, bf16[2,72,768]{2,1,0:T(8,128)(2,1)S(1)}, u32[]{:S(2)}, u32[]{:S(2)}) %collective-permute-start.95) | collective-permute-done | bytes 221216 | tf_op jit(solution)/shard_map/ppermute | solution.py:55
  585.0 7.7 collective-permute-done.82
  592.7 7.7 collective-permute-done.96
  605.1 3.1 add_convert_fusion.1
  612.0 63.1 %collective-permute-done.84 = bf16[72,768]{1,0:T(8,128)(2,1)S(1)} collective-permute-done((bf16[72,768]{1,0:T(8,128)(2,1)S(1)}, bf16[72,768]{1,0:T(8,128)(2,1)S(1)}, u32[]{:S(2)}, u32[]{:S(2)}) %collective-permute-start.84) | collective-permute-done | bytes 110624 | tf_op jit(solution)/shard_map/ppermute | solution.py:55
  675.6 4.2 collective-permute-done.98
  690.2 22.6 %collective-permute-done.60 = bf16[576,1152]{1,0:T(8,128)(2,1)S(1)} collective-permute-done((bf16[576,1152]{1,0:T(8,128)(2,1)S(1)}, bf16[576,1152]{1,0:T(8,128)(2,1)S(1)}, u32[]{:S(2)}, u32[]{:S(2)}) %collective-permute-start.60) | collective-permute-done | bytes 1327136 | tf_op jit(solution)/shard_map/ppermute | solution.py:55
  717.6 7.4 collective-permute-done.89
  725.2 11.2 %collective-permute-done.76 = bf16[2,72,1408]{2,1,0:T(8,128)(2,1)S(1)} collective-permute-done((bf16[2,72,1408]{2,1,0:T(8,128)(2,1)S(1)}, bf16[2,72,1408]{2,1,0:T(8,128)(2,1)S(1)}, u32[]{:S(2)}, u32[]{:S(2)}) %collective-permute-start.76) | collective-permute-done | bytes 405536 | tf_op jit(solution)/shard_map/ppermute | solution.py:55
  736.5 10.3 %collective-permute-done.90 = bf16[2,72,1408]{2,1,0:T(8,128)(2,1)S(1)} collective-permute-done((bf16[2,72,1408]{2,1,0:T(8,128)(2,1)S(1)}, bf16[2,72,1408]{2,1,0:T(8,128)(2,1)S(1)}, u32[]{:S(2)}, u32[]{:S(2)}) %collective-permute-start.90) | collective-permute-done | bytes 405536 | tf_op jit(solution)/shard_map/ppermute | solution.py:55
  748.1 20.5 %collective-permute-done.62 = bf16[72,1152]{1,0:T(8,128)(2,1)S(1)} collective-permute-done((bf16[72,1152]{1,0:T(8,128)(2,1)S(1)}, bf16[72,1152]{1,0:T(8,128)(2,1)S(1)}, u32[]{:S(2)}, u32[]{:S(2)}) %collective-permute-start.62) | collective-permute-done | bytes 165920 | tf_op jit(solution)/shard_map/ppermute | solution.py:55
  768.7 8.3 %collective-permute-done.69 = bf16[72,1152]{1,0:T(8,128)(2,1)S(1)} collective-permute-done((bf16[72,1152]{1,0:T(8,128)(2,1)S(1)}, bf16[72,1152]{1,0:T(8,128)(2,1)S(1)}, u32[]{:S(2)}, u32[]{:S(2)}) %collective-permute-start.69) | collective-permute-done | bytes 165920 | tf_op jit(solution)/shard_map/ppermute | solution.py:55
  777.9 6.8 collective-permute-done.63
  785.3 3.1 collective-permute-done.70
  790.6 4.9 collective-permute-done.64
  (530 shorter events, 198.5 us)
Async XLA Ops:
  4.2 67.3 %collective-permute-start.1 = (bf16[36,6656]{1,0:T(8,128)(2,1)}, bf16[36,6656]{1,0:T(8,128)(2,1)S(1)}, u32[]{:S(2)}, u32[]{:S(2)}) collective-permute-start(bf16[36,6656]{1,0:T(8,128)(2,1)} %get-tuple-element.73), channel_id=1, source_target_pairs={{0,1},{1,0},{2,3},{3,2},{4,5},{5,4},{6,7},{7,6},{8,9},{9,8},{10,11... | collective-permute-start | bytes 1437704 | tf_op jit(solution)/shard_map/ppermute | solution.py:55
  5.6 100.4 %collective-permute-start = (bf16[1,256,1152]{2,1,0:T(8,128)(2,1)}, bf16[1,256,1152]{2,1,0:T(8,128)(2,1)}, u32[]{:S(2)}, u32[]{:S(2)}) collective-permute-start(bf16[1,256,1152]{2,1,0:T(8,128)(2,1)} %dynamic-slice_bitcast_fusion.2), channel_id=1, source_target_pairs={{0,2},{1,3},{2,0},{3,1},{4,6},{5,7},{6,4},{7,5},{8,10},{9,11},{10,... | collective-permute-start | bytes 1769480 | tf_op jit(solution)/shard_map/ppermute | solution.py:55
  9.2 108.5 %collective-permute-start.55 = (bf16[1,256,1152]{2,1,0:T(8,128)(2,1)S(1)}, bf16[1,256,1152]{2,1,0:T(8,128)(2,1)}, u32[]{:S(2)}, u32[]{:S(2)}) collective-permute-start(bf16[1,256,1152]{2,1,0:T(8,128)(2,1)S(1)} %dynamic-slice_bitcast_fusion), channel_id=1, source_target_pairs={{0,2},{1,3},{2,0},{3,1},{4,6},{5,7},{6,4},{7,5},{8,10},{9,11},{10,... | collective-permute-start | bytes 1769480 | tf_op jit(solution)/shard_map/ppermute | solution.py:55
  71.7 30.1 %collective-permute-start.42 = (bf16[72,768]{1,0:T(8,128)(2,1)S(1)}, bf16[72,768]{1,0:T(8,128)(2,1)S(1)}, u32[]{:S(2)}, u32[]{:S(2)}) collective-permute-start(bf16[72,768]{1,0:T(8,128)(2,1)S(1)} %convolution_convert_fusion.13), channel_id=1, source_target_pairs={{0,4},{1,5},{2,6},{3,7},{4,0},{5,1},{6,2},{7,3},{8,12},{9,13},{10,... | collective-permute-start | bytes 331784 | tf_op jit(solution)/shard_map/ppermute | solution.py:55
  72.2 11.6 %collective-permute-start.9 = (bf16[72,1152]{1,0:T(8,128)(2,1)S(1)}, bf16[72,1152]{1,0:T(8,128)(2,1)S(1)}, u32[]{:S(2)}, u32[]{:S(2)}) collective-permute-start(bf16[72,1152]{1,0:T(8,128)(2,1)S(1)} %convolution_convert_fusion.11), channel_id=1, source_target_pairs={{0,8},{1,9},{2,10},{3,11},{4,12},{5,13},{6,14},{7,15},{8,16},{9,17... | collective-permute-start | bytes 497672 | tf_op jit(solution)/shard_map/ppermute | solution.py:55
  95.9 17.5 %collective-permute-start.5 = (bf16[4,72,1152]{2,1,0:T(8,128)(2,1)S(1)}, bf16[4,72,1152]{2,1,0:T(8,128)(2,1)S(1)}, u32[]{:S(2)}, u32[]{:S(2)}) collective-permute-start(bf16[4,72,1152]{2,1,0:T(8,128)(2,1)S(1)} %pad_maximum_fusion.6.refs_1_), channel_id=1, source_target_pairs={{0,2},{1,3},{2,0},{3,1},{4,6},{5,7},{6,4},{7,5},{8,10},{9,11},{10,... | collective-permute-start | bytes 1990664 | tf_op jit(solution)/shard_map/ppermute | solution.py:55
  101.8 18.4 %collective-permute-start.12 = (bf16[4,72,1152]{2,1,0:T(8,128)(2,1)S(1)}, bf16[4,72,1152]{2,1,0:T(8,128)(2,1)S(1)}, u32[]{:S(2)}, u32[]{:S(2)}) collective-permute-start(bf16[4,72,1152]{2,1,0:T(8,128)(2,1)S(1)} %pad_maximum_fusion.7.refs_1_), channel_id=1, source_target_pairs={{0,4},{1,5},{2,6},{3,7},{4,0},{5,1},{6,2},{7,3},{8,12},{9,13},{10,... | collective-permute-start | bytes 1990664 | tf_op jit(solution)/shard_map/ppermute | solution.py:55
  105.9 49.3 %collective-permute-start.26 = (bf16[72,1408]{1,0:T(8,128)(2,1)S(1)}, bf16[72,1408]{1,0:T(8,128)(2,1)S(1)}, u32[]{:S(2)}, u32[]{:S(2)}) collective-permute-start(bf16[72,1408]{1,0:T(8,128)(2,1)S(1)} %convolution_convert_fusion.9), channel_id=1, source_target_pairs={{0,2},{1,3},{2,0},{3,1},{4,6},{5,7},{6,4},{7,5},{8,10},{9,11},{10,... | collective-permute-start | bytes 608264 | tf_op jit(solution)/shard_map/ppermute | solution.py:55
  106.0 28.4 %collective-permute-start.6 = (bf16[4,72,1152]{2,1,0:T(8,128)(2,1)S(1)}, bf16[4,72,1152]{2,1,0:T(8,128)(2,1)S(1)}, u32[]{:S(2)}, u32[]{:S(2)}) collective-permute-start(bf16[4,72,1152]{2,1,0:T(8,128)(2,1)S(1)} %pad_maximum_fusion.6.refs_1_), channel_id=1, source_target_pairs={{0,4},{1,5},{2,6},{3,7},{4,0},{5,1},{6,2},{7,3},{8,12},{9,13},{10,... | collective-permute-start | bytes 1990664 | tf_op jit(solution)/shard_map/ppermute | solution.py:55
  113.4 32.6 %collective-permute-start.7 = (bf16[4,72,1152]{2,1,0:T(8,128)(2,1)S(1)}, bf16[4,72,1152]{2,1,0:T(8,128)(2,1)S(1)}, u32[]{:S(2)}, u32[]{:S(2)}) collective-permute-start(bf16[4,72,1152]{2,1,0:T(8,128)(2,1)S(1)} %collective-permute-done.5.refs_2_), channel_id=1, source_target_pairs={{0,4},{1,5},{2,6},{3,7},{4,0},{5,1},{6,2},{7,3},{8,12},{9,13},{10,... | collective-permute-start | bytes 1990664 | tf_op jit(solution)/shard_map/ppermute | solution.py:55
  117.7 33.3 %collective-permute-start.13 = (bf16[4,72,1152]{2,1,0:T(8,128)(2,1)S(1)}, bf16[4,72,1152]{2,1,0:T(8,128)(2,1)S(1)}, u32[]{:S(2)}, u32[]{:S(2)}) collective-permute-start(bf16[4,72,1152]{2,1,0:T(8,128)(2,1)S(1)} %pad_maximum_fusion.7.refs_1_), channel_id=1, source_target_pairs={{0,2},{1,3},{2,0},{3,1},{4,6},{5,7},{6,4},{7,5},{8,10},{9,11},{10,... | collective-permute-start | bytes 1990664 | tf_op jit(solution)/shard_map/ppermute | solution.py:55
  120.2 30.8 %collective-permute-start.14 = (bf16[4,72,1152]{2,1,0:T(8,128)(2,1)S(1)}, bf16[4,72,1152]{2,1,0:T(8,128)(2,1)S(1)}, u32[]{:S(2)}, u32[]{:S(2)}) collective-permute-start(bf16[4,72,1152]{2,1,0:T(8,128)(2,1)S(1)} %collective-permute-done.12.refs_2_), channel_id=1, source_target_pairs={{0,2},{1,3},{2,0},{3,1},{4,6},{5,7},{6,4},{7,5},{8,10},{9,11},{10,... | collective-permute-start | bytes 1990664 | tf_op jit(solution)/shard_map/ppermute | solution.py:55
  134.4 21.4 %collective-permute-start.18 = (bf16[72,1408]{1,0:T(8,128)(2,1)S(1)}, bf16[72,1408]{1,0:T(8,128)(2,1)S(1)}, u32[]{:S(2)}, u32[]{:S(2)}) collective-permute-start(bf16[72,1408]{1,0:T(8,128)(2,1)S(1)} %convolution_convert_fusion.10), channel_id=1, source_target_pairs={{0,2},{1,3},{2,0},{3,1},{4,6},{5,7},{6,4},{7,5},{8,10},{9,11},{10,... | collective-permute-start | bytes 608264 | tf_op jit(solution)/shard_map/ppermute | solution.py:55
  150.2 62.5 %collective-permute-start.8 = (bf16[1152,1152]{1,0:T(8,128)(2,1)S(1)}, bf16[1152,1152]{1,0:T(8,128)(2,1)S(1)}, u32[]{:S(2)}, u32[]{:S(2)}) collective-permute-start(bf16[1152,1152]{1,0:T(8,128)(2,1)S(1)} %bitcast.229), channel_id=1, source_target_pairs={{0,1},{1,0},{2,3},{3,2},{4,5},{5,4},{6,7},{7,6},{8,9},{9,8},{10,11... | collective-permute-start | bytes 7962632 | tf_op jit(solution)/shard_map/ppermute | solution.py:55
  155.2 74.5 %collective-permute-start.15 = (bf16[1152,1152]{1,0:T(8,128)(2,1)S(1)}, bf16[1152,1152]{1,0:T(8,128)(2,1)S(1)}, u32[]{:S(2)}, u32[]{:S(2)}) collective-permute-start(bf16[1152,1152]{1,0:T(8,128)(2,1)S(1)} %bitcast.234), channel_id=1, source_target_pairs={{0,1},{1,0},{2,3},{3,2},{4,5},{5,4},{6,7},{7,6},{8,9},{9,8},{10,11... | collective-permute-start | bytes 7962632 | tf_op jit(solution)/shard_map/ppermute | solution.py:55
  173.0 14.1 %collective-permute-start.27 = (bf16[2,72,1408]{2,1,0:T(8,128)(2,1)S(1)}, bf16[2,72,1408]{2,1,0:T(8,128)(2,1)S(1)}, u32[]{:S(2)}, u32[]{:S(2)}) collective-permute-start(bf16[2,72,1408]{2,1,0:T(8,128)(2,1)S(1)} %pad_maximum_fusion.11.refs_1_), channel_id=1, source_target_pairs={{0,8},{1,9},{2,10},{3,11},{4,12},{5,13},{6,14},{7,15},{8,16},{9,17... | collective-permute-start | bytes 1216520 | tf_op jit(solution)/shard_map/ppermute | solution.py:55
  176.1 15.2 %collective-permute-start.30 = (bf16[2,72,1408]{2,1,0:T(8,128)(2,1)S(1)}, bf16[2,72,1408]{2,1,0:T(8,128)(2,1)S(1)}, u32[]{:S(2)}, u32[]{:S(2)}) collective-permute-start(bf16[2,72,1408]{2,1,0:T(8,128)(2,1)S(1)} %pad_maximum_fusion.11.refs_1_), channel_id=1, source_target_pairs={{0,4},{1,5},{2,6},{3,7},{4,0},{5,1},{6,2},{7,3},{8,12},{9,13},{10,... | collective-permute-start | bytes 1216520 | tf_op jit(solution)/shard_map/ppermute | solution.py:55
  177.4 18.4 %collective-permute-start.19 = (bf16[2,72,1408]{2,1,0:T(8,128)(2,1)S(1)}, bf16[2,72,1408]{2,1,0:T(8,128)(2,1)S(1)}, u32[]{:S(2)}, u32[]{:S(2)}) collective-permute-start(bf16[2,72,1408]{2,1,0:T(8,128)(2,1)S(1)} %pad_maximum_fusion.10.refs_1_), channel_id=1, source_target_pairs={{0,8},{1,9},{2,10},{3,11},{4,12},{5,13},{6,14},{7,15},{8,16},{9,17... | collective-permute-start | bytes 1216520 | tf_op jit(solution)/shard_map/ppermute | solution.py:55
  195.8 15.6 %collective-permute-start.28 = (bf16[2,72,1408]{2,1,0:T(8,128)(2,1)S(1)}, bf16[2,72,1408]{2,1,0:T(8,128)(2,1)S(1)}, u32[]{:S(2)}, u32[]{:S(2)}) collective-permute-start(bf16[2,72,1408]{2,1,0:T(8,128)(2,1)S(1)} %collective-permute-done.27.refs_2_), channel_id=1, source_target_pairs={{0,8},{1,9},{2,10},{3,11},{4,12},{5,13},{6,14},{7,15},{8,16},{9,17... | collective-permute-start | bytes 1216520 | tf_op jit(solution)/shard_map/ppermute | solution.py:55
  211.4 14.0 %collective-permute-start.20 = (bf16[2,72,1408]{2,1,0:T(8,128)(2,1)S(1)}, bf16[2,72,1408]{2,1,0:T(8,128)(2,1)S(1)}, u32[]{:S(2)}, u32[]{:S(2)}) collective-permute-start(bf16[2,72,1408]{2,1,0:T(8,128)(2,1)S(1)} %collective-permute-done.19.refs_2_), channel_id=1, source_target_pairs={{0,8},{1,9},{2,10},{3,11},{4,12},{5,13},{6,14},{7,15},{8,16},{9,17... | collective-permute-start | bytes 1216520 | tf_op jit(solution)/shard_map/ppermute | solution.py:55
  212.7 17.1 %collective-permute-start.29 = (bf16[2,72,1408]{2,1,0:T(8,128)(2,1)S(1)}, bf16[2,72,1408]{2,1,0:T(8,128)(2,1)S(1)}, u32[]{:S(2)}, u32[]{:S(2)}) collective-permute-start(bf16[2,72,1408]{2,1,0:T(8,128)(2,1)S(1)} %collective-permute-done.28.refs_3_), channel_id=1, source_target_pairs={{0,8},{1,9},{2,10},{3,11},{4,12},{5,13},{6,14},{7,15},{8,16},{9,17... | collective-permute-start | bytes 1216520 | tf_op jit(solution)/shard_map/ppermute | solution.py:55
  214.6 18.8 %collective-permute-start.31 = (bf16[2,72,1408]{2,1,0:T(8,128)(2,1)S(1)}, bf16[2,72,1408]{2,1,0:T(8,128)(2,1)S(1)}, u32[]{:S(2)}, u32[]{:S(2)}) collective-permute-start(bf16[2,72,1408]{2,1,0:T(8,128)(2,1)S(1)} %collective-permute-done.27.refs_2_), channel_id=1, source_target_pairs={{0,4},{1,5},{2,6},{3,7},{4,0},{5,1},{6,2},{7,3},{8,12},{9,13},{10,... | collective-permute-start | bytes 1216520 | tf_op jit(solution)/shard_map/ppermute | solution.py:55
  218.2 15.1 %collective-permute-start.41 = (bf16[2,72,768]{2,1,0:T(8,128)(2,1)S(1)}, bf16[2,72,768]{2,1,0:T(8,128)(2,1)S(1)}, u32[]{:S(2)}, u32[]{:S(2)}) collective-permute-start(bf16[2,72,768]{2,1,0:T(8,128)(2,1)S(1)} %collective-permute-done.37.refs_4_), channel_id=1, source_target_pairs={{0,2},{1,3},{2,0},{3,1},{4,6},{5,7},{6,4},{7,5},{8,10},{9,11},{10,... | collective-permute-start | bytes 663560 | tf_op jit(solution)/shard_map/ppermute | solution.py:55
  225.4 11.7 %collective-permute-start.32 = (bf16[2,72,1408]{2,1,0:T(8,128)(2,1)S(1)}, bf16[2,72,1408]{2,1,0:T(8,128)(2,1)S(1)}, u32[]{:S(2)}, u32[]{:S(2)}) collective-permute-start(bf16[2,72,1408]{2,1,0:T(8,128)(2,1)S(1)} %collective-permute-done.28.refs_3_), channel_id=1, source_target_pairs={{0,4},{1,5},{2,6},{3,7},{4,0},{5,1},{6,2},{7,3},{8,12},{9,13},{10,... | collective-permute-start | bytes 1216520 | tf_op jit(solution)/shard_map/ppermute | solution.py:55
  229.8 14.7 %collective-permute-start.33 = (bf16[2,72,1408]{2,1,0:T(8,128)(2,1)S(1)}, bf16[2,72,1408]{2,1,0:T(8,128)(2,1)S(1)}, u32[]{:S(2)}, u32[]{:S(2)}) collective-permute-start(bf16[2,72,1408]{2,1,0:T(8,128)(2,1)S(1)} %collective-permute-done.29.refs_4_), channel_id=1, source_target_pairs={{0,4},{1,5},{2,6},{3,7},{4,0},{5,1},{6,2},{7,3},{8,12},{9,13},{10,... | collective-permute-start | bytes 1216520 | tf_op jit(solution)/shard_map/ppermute | solution.py:55
  233.3 41.4 %collective-permute-start.16 = (bf16[512,1152]{1,0:T(8,128)(2,1)S(1)}, bf16[512,1152]{1,0:T(8,128)(2,1)S(1)}, u32[]{:S(2)}, u32[]{:S(2)}) collective-permute-start(bf16[512,1152]{1,0:T(8,128)(2,1)S(1)} %convolution_convert_fusion.8.ko_ref), channel_id=1, source_target_pairs={{0,1},{1,0},{2,3},{3,2},{4,5},{5,4},{6,7},{7,6},{8,9},{9,8},{10,11... | collective-permute-start | bytes 3538952 | tf_op jit(solution)/shard_map/ppermute | solution.py:55
  233.4 42.8 %collective-permute-start.17 = (bf16[512,1152]{1,0:T(8,128)(2,1)S(1)}, bf16[512,1152]{1,0:T(8,128)(2,1)}, u32[]{:S(2)}, u32[]{:S(2)}) collective-permute-start(bf16[512,1152]{1,0:T(8,128)(2,1)S(1)} %fusion.22.vo_ref), channel_id=1, source_target_pairs={{0,1},{1,0},{2,3},{3,2},{4,5},{5,4},{6,7},{7,6},{8,9},{9,8},{10,11... | collective-permute-start | bytes 3538952 | tf_op jit(solution)/shard_map/ppermute | solution.py:55
  237.1 26.4 %collective-permute-start.23 = (bf16[2,72,1408]{2,1,0:T(8,128)(2,1)S(1)}, bf16[2,72,1408]{2,1,0:T(8,128)(2,1)S(1)}, u32[]{:S(2)}, u32[]{:S(2)}) collective-permute-start(bf16[2,72,1408]{2,1,0:T(8,128)(2,1)S(1)} %collective-permute-done.19.refs_2_), channel_id=1, source_target_pairs={{0,4},{1,5},{2,6},{3,7},{4,0},{5,1},{6,2},{7,3},{8,12},{9,13},{10,... | collective-permute-start | bytes 1216520 | tf_op jit(solution)/shard_map/ppermute | solution.py:55
  239.4 24.2 %collective-permute-start.24 = (bf16[2,72,1408]{2,1,0:T(8,128)(2,1)S(1)}, bf16[2,72,1408]{2,1,0:T(8,128)(2,1)S(1)}, u32[]{:S(2)}, u32[]{:S(2)}) collective-permute-start(bf16[2,72,1408]{2,1,0:T(8,128)(2,1)S(1)} %collective-permute-done.20.refs_3_), channel_id=1, source_target_pairs={{0,4},{1,5},{2,6},{3,7},{4,0},{5,1},{6,2},{7,3},{8,12},{9,13},{10,... | collective-permute-start | bytes 1216520 | tf_op jit(solution)/shard_map/ppermute | solution.py:55
  244.4 23.1 %collective-permute-start.25 = (bf16[2,72,1408]{2,1,0:T(8,128)(2,1)S(1)}, bf16[2,72,1408]{2,1,0:T(8,128)(2,1)S(1)}, u32[]{:S(2)}, u32[]{:S(2)}) collective-permute-start(bf16[2,72,1408]{2,1,0:T(8,128)(2,1)S(1)} %collective-permute-done.21.refs_4_), channel_id=1, source_target_pairs={{0,4},{1,5},{2,6},{3,7},{4,0},{5,1},{6,2},{7,3},{8,12},{9,13},{10,... | collective-permute-start | bytes 1216520 | tf_op jit(solution)/shard_map/ppermute | solution.py:55
  263.6 86.1 %collective-permute-start.53 = (bf16[1152,768]{1,0:T(8,128)(2,1)}, bf16[1152,768]{1,0:T(8,128)(2,1)}, u32[]{:S(2)}, u32[]{:S(2)}) collective-permute-start(bf16[1152,768]{1,0:T(8,128)(2,1)} %bitcast.42), channel_id=1, source_target_pairs={{0,1},{1,0},{2,3},{3,2},{4,5},{5,4},{6,7},{7,6},{8,9},{9,8},{10,11... | collective-permute-start | bytes 5308424 | tf_op jit(solution)/shard_map/ppermute | solution.py:55
  263.7 73.5 %collective-permute-start.52 = (bf16[1152,768]{1,0:T(8,128)(2,1)}, bf16[1152,768]{1,0:T(8,128)(2,1)}, u32[]{:S(2)}, u32[]{:S(2)}) collective-permute-start(bf16[1152,768]{1,0:T(8,128)(2,1)} %bitcast.39), channel_id=1, source_target_pairs={{0,1},{1,0},{2,3},{3,2},{4,5},{5,4},{6,7},{7,6},{8,9},{9,8},{10,11... | collective-permute-start | bytes 5308424 | tf_op jit(solution)/shard_map/ppermute | solution.py:55
  267.5 72.3 %collective-permute-start.51 = (bf16[1152,1408]{1,0:T(8,128)(2,1)S(1)}, bf16[1152,1408]{1,0:T(8,128)(2,1)}, u32[]{:S(2)}, u32[]{:S(2)}) collective-permute-start(bf16[1152,1408]{1,0:T(8,128)(2,1)S(1)} %bitcast.226), channel_id=1, source_target_pairs={{0,1},{1,0},{2,3},{3,2},{4,5},{5,4},{6,7},{7,6},{8,9},{9,8},{10,11... | collective-permute-start | bytes 9732104 | tf_op jit(solution)/shard_map/ppermute | solution.py:55
  275.7 48.5 %collective-permute-start.50 = (bf16[1152,1408]{1,0:T(8,128)(2,1)S(1)}, bf16[1152,1408]{1,0:T(8,128)(2,1)}, u32[]{:S(2)}, u32[]{:S(2)}) collective-permute-start(bf16[1152,1408]{1,0:T(8,128)(2,1)S(1)} %bitcast.223), channel_id=1, source_target_pairs={{0,1},{1,0},{2,3},{3,2},{4,5},{5,4},{6,7},{7,6},{8,9},{9,8},{10,11... | collective-permute-start | bytes 9732104 | tf_op jit(solution)/shard_map/ppermute | solution.py:55
  358.9 93.3 %collective-permute-start.54 = (bf16[1,256,1152]{2,1,0:T(8,128)(2,1)}, bf16[1,256,1152]{2,1,0:T(8,128)(2,1)}, u32[]{:S(2)}, u32[]{:S(2)}) collective-permute-start(bf16[1,256,1152]{2,1,0:T(8,128)(2,1)} %dynamic-slice_bitcast_fusion.1), channel_id=1, source_target_pairs={{0,2},{1,3},{2,0},{3,1},{4,6},{5,7},{6,4},{7,5},{8,10},{9,11},{10,... | collective-permute-start | bytes 1769480 | tf_op jit(solution)/shard_map/ppermute | solution.py:55
  439.8 14.9 %collective-permute-start.57 = (bf16[512,1152]{1,0:T(8,128)(2,1)}, bf16[512,1152]{1,0:T(8,128)(2,1)S(1)}, u32[]{:S(2)}, u32[]{:S(2)}) collective-permute-start(bf16[512,1152]{1,0:T(8,128)(2,1)} %get-tuple-element.30), channel_id=1, source_target_pairs={{0,1},{1,0},{2,3},{3,2},{4,5},{5,4},{6,7},{7,6},{8,9},{9,8},{10,11... | collective-permute-start | bytes 3538952 | tf_op jit(solution)/shard_map/ppermute | solution.py:55
  439.8 19.6 %collective-permute-start.56 = (bf16[512,1152]{1,0:T(8,128)(2,1)}, bf16[512,1152]{1,0:T(8,128)(2,1)S(1)}, u32[]{:S(2)}, u32[]{:S(2)}) collective-permute-start(bf16[512,1152]{1,0:T(8,128)(2,1)} %get-tuple-element.28), channel_id=1, source_target_pairs={{0,1},{1,0},{2,3},{3,2},{4,5},{5,4},{6,7},{7,6},{8,9},{9,8},{10,11... | collective-permute-start | bytes 3538952 | tf_op jit(solution)/shard_map/ppermute | solution.py:55
  446.9 153.6 %collective-permute-start.73 = (bf16[1152,1408]{1,0:T(8,128)(2,1)}, bf16[1152,1408]{1,0:T(8,128)(2,1)}, u32[]{:S(2)}, u32[]{:S(2)}) collective-permute-start(bf16[1152,1408]{1,0:T(8,128)(2,1)} %convolution_convert_fusion.1), channel_id=1, source_target_pairs={{0,1},{1,0},{2,3},{3,2},{4,5},{5,4},{6,7},{7,6},{8,9},{9,8},{10,11... | collective-permute-start | bytes 9732104 | tf_op jit(solution)/shard_map/ppermute | solution.py:55
  447.0 77.0 %collective-permute-start.79 = (bf16[1152,768]{1,0:T(8,128)(2,1)}, bf16[1152,768]{1,0:T(8,128)(2,1)}, u32[]{:S(2)}, u32[]{:S(2)}) collective-permute-start(bf16[1152,768]{1,0:T(8,128)(2,1)} %convolution_convert_fusion.6), channel_id=1, source_target_pairs={{0,1},{1,0},{2,3},{3,2},{4,5},{5,4},{6,7},{7,6},{8,9},{9,8},{10,11... | collective-permute-start | bytes 5308424 | tf_op jit(solution)/shard_map/ppermute | solution.py:55
  452.2 151.4 %collective-permute-start.87 = (bf16[1152,1408]{1,0:T(8,128)(2,1)}, bf16[1152,1408]{1,0:T(8,128)(2,1)}, u32[]{:S(2)}, u32[]{:S(2)}) collective-permute-start(bf16[1152,1408]{1,0:T(8,128)(2,1)} %convolution_convert_fusion), channel_id=1, source_target_pairs={{0,1},{1,0},{2,3},{3,2},{4,5},{5,4},{6,7},{7,6},{8,9},{9,8},{10,11... | collective-permute-start | bytes 9732104 | tf_op jit(solution)/shard_map/ppermute | solution.py:55
  454.7 71.7 %collective-permute-start.93 = (bf16[1152,768]{1,0:T(8,128)(2,1)}, bf16[1152,768]{1,0:T(8,128)(2,1)}, u32[]{:S(2)}, u32[]{:S(2)}) collective-permute-start(bf16[1152,768]{1,0:T(8,128)(2,1)} %convolution_convert_fusion.5), channel_id=1, source_target_pairs={{0,1},{1,0},{2,3},{3,2},{4,5},{5,4},{6,7},{7,6},{8,9},{9,8},{10,11... | collective-permute-start | bytes 5308424 | tf_op jit(solution)/shard_map/ppermute | solution.py:55
  468.2 62.8 %collective-permute-start.58 = (bf16[1,256,1152]{2,1,0:T(8,128)(2,1)}, bf16[1,256,1152]{2,1,0:T(8,128)(2,1)}, u32[]{:S(2)}, u32[]{:S(2)}) collective-permute-start(bf16[1,256,1152]{2,1,0:T(8,128)(2,1)} %fusion.106), channel_id=1, source_target_pairs={{0,2},{1,3},{2,0},{3,1},{4,6},{5,7},{6,4},{7,5},{8,10},{9,11},{10,... | collective-permute-start | bytes 1769480 | tf_op jit(solution)/shard_map/ppermute | solution.py:55
  524.0 155.9 %collective-permute-start.59 = (bf16[1152,1152]{1,0:T(8,128)(2,1)S(1)}, bf16[1152,1152]{1,0:T(8,128)(2,1)S(1)}, u32[]{:S(2)}, u32[]{:S(2)}) collective-permute-start(bf16[1152,1152]{1,0:T(8,128)(2,1)S(1)} %convolution_convert_fusion.3), channel_id=1, source_target_pairs={{0,1},{1,0},{2,3},{3,2},{4,5},{5,4},{6,7},{7,6},{8,9},{9,8},{10,11... | collective-permute-start | bytes 7962632 | tf_op jit(solution)/shard_map/ppermute | solution.py:55
  526.4 22.7 %collective-permute-start.80 = (bf16[576,768]{1,0:T(8,128)(2,1)S(1)}, bf16[576,768]{1,0:T(8,128)(2,1)S(1)}, u32[]{:S(2)}, u32[]{:S(2)}) collective-permute-start(bf16[576,768]{1,0:T(8,128)(2,1)S(1)} %add_convert_fusion.11), channel_id=1, source_target_pairs={{0,2},{1,3},{2,0},{3,1},{4,6},{5,7},{6,4},{7,5},{8,10},{9,11},{10,... | collective-permute-start | bytes 2654216 | tf_op jit(solution)/shard_map/ppermute | solution.py:55
  531.1 36.8 %collective-permute-start.94 = (bf16[576,768]{1,0:T(8,128)(2,1)S(1)}, bf16[576,768]{1,0:T(8,128)(2,1)S(1)}, u32[]{:S(2)}, u32[]{:S(2)}) collective-permute-start(bf16[576,768]{1,0:T(8,128)(2,1)S(1)} %add_convert_fusion.9), channel_id=1, source_target_pairs={{0,2},{1,3},{2,0},{3,1},{4,6},{5,7},{6,4},{7,5},{8,10},{9,11},{10,... | collective-permute-start | bytes 2654216 | tf_op jit(solution)/shard_map/ppermute | solution.py:55
  549.1 132.5 %collective-permute-start.66 = (bf16[1152,1152]{1,0:T(8,128)(2,1)S(1)}, bf16[1152,1152]{1,0:T(8,128)(2,1)S(1)}, u32[]{:S(2)}, u32[]{:S(2)}) collective-permute-start(bf16[1152,1152]{1,0:T(8,128)(2,1)S(1)} %convolution_convert_fusion.2), channel_id=1, source_target_pairs={{0,1},{1,0},{2,3},{3,2},{4,5},{5,4},{6,7},{7,6},{8,9},{9,8},{10,11... | collective-permute-start | bytes 7962632 | tf_op jit(solution)/shard_map/ppermute | solution.py:55
  603.6 79.8 %collective-permute-start.74 = (bf16[576,1408]{1,0:T(8,128)(2,1)S(1)}, bf16[576,1408]{1,0:T(8,128)(2,1)S(1)}, u32[]{:S(2)}, u32[]{:S(2)}) collective-permute-start(bf16[576,1408]{1,0:T(8,128)(2,1)S(1)} %add_convert_fusion.3), channel_id=1, source_target_pairs={{0,4},{1,5},{2,6},{3,7},{4,0},{5,1},{6,2},{7,3},{8,12},{9,13},{10,... | collective-permute-start | bytes 4866056 | tf_op jit(solution)/shard_map/ppermute | solution.py:55
  608.3 78.0 %collective-permute-start.88 = (bf16[576,1408]{1,0:T(8,128)(2,1)S(1)}, bf16[576,1408]{1,0:T(8,128)(2,1)S(1)}, u32[]{:S(2)}, u32[]{:S(2)}) collective-permute-start(bf16[576,1408]{1,0:T(8,128)(2,1)S(1)} %add_convert_fusion.1), channel_id=1, source_target_pairs={{0,4},{1,5},{2,6},{3,7},{4,0},{5,1},{6,2},{7,3},{8,12},{9,13},{10,... | collective-permute-start | bytes 4866056 | tf_op jit(solution)/shard_map/ppermute | solution.py:55
  610.5 64.6 %collective-permute-start.84 = (bf16[72,768]{1,0:T(8,128)(2,1)S(1)}, bf16[72,768]{1,0:T(8,128)(2,1)S(1)}, u32[]{:S(2)}, u32[]{:S(2)}) collective-permute-start(bf16[72,768]{1,0:T(8,128)(2,1)S(1)} %fusion.136), channel_id=1, source_target_pairs={{0,4},{1,5},{2,6},{3,7},{4,0},{5,1},{6,2},{7,3},{8,12},{9,13},{10,... | collective-permute-start | bytes 331784 | tf_op jit(solution)/shard_map/ppermute | solution.py:55
  679.8 121.0 %collective-permute-start.86 = (f32[36,768]{1,0:T(8,128)S(1)}, f32[36,768]{1,0:T(8,128)S(1)}, u32[]{:S(2)}, u32[]{:S(2)}) collective-permute-start(f32[36,768]{1,0:T(8,128)S(1)} %get-tuple-element.101), channel_id=1, source_target_pairs={{0,1},{1,0},{2,3},{3,2},{4,5},{5,4},{6,7},{7,6},{8,9},{9,8},{10,11... | collective-permute-start | bytes 331784 | tf_op jit(solution)/shard_map/ppermute | solution.py:55
  679.9 122.0 %collective-permute-start.100 = (f32[36,768]{1,0:T(8,128)S(1)}, f32[36,768]{1,0:T(8,128)S(1)}, u32[]{:S(2)}, u32[]{:S(2)}) collective-permute-start(f32[36,768]{1,0:T(8,128)S(1)} %get-tuple-element.99), channel_id=1, source_target_pairs={{0,1},{1,0},{2,3},{3,2},{4,5},{5,4},{6,7},{7,6},{8,9},{9,8},{10,11... | collective-permute-start | bytes 331784 | tf_op jit(solution)/shard_map/ppermute | solution.py:55
  681.7 31.1 %collective-permute-start.60 = (bf16[576,1152]{1,0:T(8,128)(2,1)S(1)}, bf16[576,1152]{1,0:T(8,128)(2,1)S(1)}, u32[]{:S(2)}, u32[]{:S(2)}) collective-permute-start(bf16[576,1152]{1,0:T(8,128)(2,1)S(1)} %fusion.16), channel_id=1, source_target_pairs={{0,4},{1,5},{2,6},{3,7},{4,0},{5,1},{6,2},{7,3},{8,12},{9,13},{10,... | collective-permute-start | bytes 3981320 | tf_op jit(solution)/shard_map/ppermute | solution.py:55
  683.4 30.9 %collective-permute-start.67 = (bf16[576,1152]{1,0:T(8,128)(2,1)S(1)}, bf16[576,1152]{1,0:T(8,128)(2,1)S(1)}, u32[]{:S(2)}, u32[]{:S(2)}) collective-permute-start(bf16[576,1152]{1,0:T(8,128)(2,1)S(1)} %fusion.17), channel_id=1, source_target_pairs={{0,2},{1,3},{2,0},{3,1},{4,6},{5,7},{6,4},{7,5},{8,10},{9,11},{10,... | collective-permute-start | bytes 3981320 | tf_op jit(solution)/shard_map/ppermute | solution.py:55
  686.3 29.8 %collective-permute-start.75 = (bf16[2,72,1408]{2,1,0:T(8,128)(2,1)S(1)}, bf16[2,72,1408]{2,1,0:T(8,128)(2,1)S(1)}, u32[]{:S(2)}, u32[]{:S(2)}) collective-permute-start(bf16[2,72,1408]{2,1,0:T(8,128)(2,1)S(1)} %bitcast.268), channel_id=1, source_target_pairs={{0,8},{1,9},{2,10},{3,11},{4,12},{5,13},{6,14},{7,15},{8,16},{9,17... | collective-permute-start | bytes 1216520 | tf_op jit(solution)/shard_map/ppermute | solution.py:55
  712.8 12.3 %collective-permute-start.89 = (bf16[2,72,1408]{2,1,0:T(8,128)(2,1)S(1)}, bf16[2,72,1408]{2,1,0:T(8,128)(2,1)S(1)}, u32[]{:S(2)}, u32[]{:S(2)}) collective-permute-start(bf16[2,72,1408]{2,1,0:T(8,128)(2,1)S(1)} %bitcast.269), channel_id=1, source_target_pairs={{0,8},{1,9},{2,10},{3,11},{4,12},{5,13},{6,14},{7,15},{8,16},{9,17... | collective-permute-start | bytes 1216520 | tf_op jit(solution)/shard_map/ppermute | solution.py:55
  714.3 32.7 %collective-permute-start.61 = (bf16[288,1152]{1,0:T(8,128)(2,1)S(1)}, bf16[288,1152]{1,0:T(8,128)(2,1)S(1)}, u32[]{:S(2)}, u32[]{:S(2)}) collective-permute-start(bf16[288,1152]{1,0:T(8,128)(2,1)S(1)} %slice.478), channel_id=1, source_target_pairs={{0,2},{1,3},{2,0},{3,1},{4,6},{5,7},{6,4},{7,5},{8,10},{9,11},{10,... | collective-permute-start | bytes 1990664 | tf_op jit(solution)/shard_map/ppermute | solution.py:55
  716.1 31.1 %collective-permute-start.68 = (bf16[288,1152]{1,0:T(8,128)(2,1)S(1)}, bf16[288,1152]{1,0:T(8,128)(2,1)S(1)}, u32[]{:S(2)}, u32[]{:S(2)}) collective-permute-start(bf16[288,1152]{1,0:T(8,128)(2,1)S(1)} %slice.490), channel_id=1, source_target_pairs={{0,4},{1,5},{2,6},{3,7},{4,0},{5,1},{6,2},{7,3},{8,12},{9,13},{10,... | collective-permute-start | bytes 1990664 | tf_op jit(solution)/shard_map/ppermute | solution.py:55
  725.1 11.3 %collective-permute-start.76 = (bf16[2,72,1408]{2,1,0:T(8,128)(2,1)S(1)}, bf16[2,72,1408]{2,1,0:T(8,128)(2,1)S(1)}, u32[]{:S(2)}, u32[]{:S(2)}) collective-permute-start(bf16[2,72,1408]{2,1,0:T(8,128)(2,1)S(1)} %fusion.76), channel_id=1, source_target_pairs={{0,8},{1,9},{2,10},{3,11},{4,12},{5,13},{6,14},{7,15},{8,16},{9,17... | collective-permute-start | bytes 1216520 | tf_op jit(solution)/shard_map/ppermute | solution.py:55
  736.4 10.4 %collective-permute-start.90 = (bf16[2,72,1408]{2,1,0:T(8,128)(2,1)S(1)}, bf16[2,72,1408]{2,1,0:T(8,128)(2,1)S(1)}, u32[]{:S(2)}, u32[]{:S(2)}) collective-permute-start(bf16[2,72,1408]{2,1,0:T(8,128)(2,1)S(1)} %fusion.74), channel_id=1, source_target_pairs={{0,8},{1,9},{2,10},{3,11},{4,12},{5,13},{6,14},{7,15},{8,16},{9,17... | collective-permute-start | bytes 1216520 | tf_op jit(solution)/shard_map/ppermute | solution.py:55
  746.9 30.2 %collective-permute-start.77 = (bf16[2,72,1408]{2,1,0:T(8,128)(2,1)S(1)}, bf16[2,72,1408]{2,1,0:T(8,128)(2,1)S(1)}, u32[]{:S(2)}, u32[]{:S(2)}) collective-permute-start(bf16[2,72,1408]{2,1,0:T(8,128)(2,1)S(1)} %fusion.75), channel_id=1, source_target_pairs={{0,8},{1,9},{2,10},{3,11},{4,12},{5,13},{6,14},{7,15},{8,16},{9,17... | collective-permute-start | bytes 1216520 | tf_op jit(solution)/shard_map/ppermute | solution.py:55
  747.0 30.3 %collective-permute-start.91 = (bf16[2,72,1408]{2,1,0:T(8,128)(2,1)S(1)}, bf16[2,72,1408]{2,1,0:T(8,128)(2,1)S(1)}, u32[]{:S(2)}, u32[]{:S(2)}) collective-permute-start(bf16[2,72,1408]{2,1,0:T(8,128)(2,1)S(1)} %fusion.73), channel_id=1, source_target_pairs={{0,8},{1,9},{2,10},{3,11},{4,12},{5,13},{6,14},{7,15},{8,16},{9,17... | collective-permute-start | bytes 1216520 | tf_op jit(solution)/shard_map/ppermute | solution.py:55
  747.2 21.4 %collective-permute-start.62 = (bf16[72,1152]{1,0:T(8,128)(2,1)S(1)}, bf16[72,1152]{1,0:T(8,128)(2,1)S(1)}, u32[]{:S(2)}, u32[]{:S(2)}) collective-permute-start(bf16[72,1152]{1,0:T(8,128)(2,1)S(1)} %slice.479), channel_id=1, source_target_pairs={{0,8},{1,9},{2,10},{3,11},{4,12},{5,13},{6,14},{7,15},{8,16},{9,17... | collective-permute-start | bytes 497672 | tf_op jit(solution)/shard_map/ppermute | solution.py:55
  777.1 11.2 %collective-permute-start.70 = (bf16[72,1152]{1,0:T(8,128)(2,1)S(1)}, bf16[72,1152]{1,0:T(8,128)(2,1)S(1)}, u32[]{:S(2)}, u32[]{:S(2)}) collective-permute-start(bf16[72,1152]{1,0:T(8,128)(2,1)S(1)} %add_convert_fusion.15), channel_id=1, source_target_pairs={{0,8},{1,9},{2,10},{3,11},{4,12},{5,13},{6,14},{7,15},{8,16},{9,17... | collective-permute-start | bytes 497672 | tf_op jit(solution)/shard_map/ppermute | solution.py:55
  777.3 11.1 %collective-permute-start.78 = (bf16[72,1408]{1,0:T(8,128)(2,1)S(1)}, bf16[72,1408]{1,0:T(8,128)(2,1)S(1)}, u32[]{:S(2)}, u32[]{:S(2)}) collective-permute-start(bf16[72,1408]{1,0:T(8,128)(2,1)S(1)} %fusion.125), channel_id=1, source_target_pairs={{0,2},{1,3},{2,0},{3,1},{4,6},{5,7},{6,4},{7,5},{8,10},{9,11},{10,... | collective-permute-start | bytes 608264 | tf_op jit(solution)/shard_map/ppermute | solution.py:55
  (130 other events, 2338.7 us)

commit v2 on v1

v2 whole, which is shorter than its diff:
```python
import functools

import jax
import jax.numpy as jnp
from jax import lax
from jax.experimental import pallas as pl
from jax.experimental.pallas import tpu as pltpu
from jax.sharding import PartitionSpec as P

H = 16
HD = 72
AXES = ("rows", "seq")
norm_epsilon = 1e-06
BIG = 1e30
LANE = 128
WIN = 256
bf16 = jnp.bfloat16
f32 = jnp.float32
COST = pl.CostEstimate(flops=5 * 10**9, bytes_accessed=10**7, transcendentals=10**6)
NT = (((1,), (1,)), ((), ()))
TN = (((0,), (0,)), ((), ()))
NN = (((1,), (0,)), ((), ()))


def dot(a, b, dims=NN, out=f32):
    return lax.dot_general(a, b, dims, preferred_element_type=f32).astype(out)


class Places:
    def __init__(self, n_rows, n_seq):
        self.nz, self.ny, self.nx, self.nc = n_rows // 2, 2, n_seq // 2, 2
        every = [
            (z, y, x, c)
            for z in range(self.nz)
            for y in range(2)
            for x in range(2)
            for c in range(2)
        ]
        nz = self.nz

        def flat(z, y, x, c):
            return ((z * 2 + y) * 2 + x) * 2 + c

        def pairs(f):
            return [(flat(*t), flat(*f(*t))) for t in every]

        self.to_core = pairs(lambda z, y, x, c: (z, y, x, 1 - c))
        self.to_x = pairs(lambda z, y, x, c: (z, y, 1 - x, c))
        self.to_y = pairs(lambda z, y, x, c: (z, 1 - y, x, c))
        self.to_z = pairs(lambda z, y, x, c: ((z + 1) % nz, y, x, c))
        assert nz & (nz - 1) == 0
        self.z_swaps = [
            pairs(lambda z, y, x, c, bit=1 << i: (z ^ bit, y, x, c))
            for i in range(nz.bit_length() - 1)
        ]
        r, s = lax.axis_index("rows"), lax.axis_index("seq")
        self.z, self.y, self.x, self.c = r // 2, r % 2, s // 2, s % 2


def send(value, pairs):
    return lax.ppermute(value, AXES, pairs)


class Going:
    def __init__(self, value):
        self.value, self.here = value, False


class Line:
    def __init__(self):
        self.token = jnp.zeros((8, LANE), f32)
        self.queue = []

    def pin(self, *values):
        return lax.optimization_barrier((values, self.token))[0]

    def close(self, *values):
        values, self.token = lax.optimization_barrier((values, self.token))
        return values if len(values) > 1 else values[0]

    def done(self, *going):
        while not all(g.here for g in going):
            first = self.queue.pop(0)
            first.value, first.here = self.close(first.value), True
        return [g.value for g in going] if len(going) > 1 else going[0].value

    def run(self, step, *values):
        out = step(*self.pin(*values))
        return self.close(*out) if isinstance(out, tuple) else self.close(out)

    def start(self, value, pairs):
        self.queue.append(Going(send(self.pin(value)[0], pairs)))
        return self.queue[-1]


def flip(here, by):
    return here + by - 2 * by * here


def place_kernel(n_in, n_out, plan, *refs):
    dyn = refs[0]
    ins, outs, sem = refs[1 : 1 + n_in], refs[1 + n_in : 1 + n_in + n_out], refs[1 + n_in + n_out]
    nz = outs[0].shape[0]
    copies = []
    for j, (i, src, src_col, out, dst, dst_col, wide) in enumerate(plan):
        zi, yi, xi = dst(dyn[0], dyn[1], dyn[2])
        zi = lax.rem(zi + dyn[3 + out], nz)
        source = ins[i].at[(*src, slice(None), pl.ds(src_col, wide))]
        target = outs[out].at[zi, yi, xi, :, pl.ds(dst_col, wide)]
        copies.append(pltpu.make_async_copy(source, target, sem.at[j]))
    for copy in copies:
        copy.start()
    for copy in copies:
        copy.wait()


def place(at, ins, plan, rows, widths, turned):
    turns = [jnp.where(at.c == 1, at.nz // 2 if t else 0, 0) for t in turned]
    cut_plan = []
    for i, src, src_col, dst, col, wide in plan:
        left = 0
        for out, out_wide in enumerate(widths):
            low, high = max(col, left), min(col + wide, left + out_wide)
            if low < high:
                cut_plan.append((i, src, src_col + low - col, out, dst, low - left, high - low))
            left += out_wide
    shapes = [(at.nz, 2, 2, rows, w) for w in widths]
    if rows % 8 == 0:
        dyn = jnp.stack([at.z, at.y, at.x, *turns]).astype(jnp.int32)
        outs = pl.pallas_call(
            functools.partial(place_kernel, len(ins), len(widths), cut_plan),
            out_shape=[jax.ShapeDtypeStruct(shape, ins[0].dtype) for shape in shapes],
            in_specs=[pl.BlockSpec(memory_space=pltpu.SMEM)]
            + [pl.BlockSpec(memory_space=pl.ANY)] * len(ins),
            out_specs=[pl.BlockSpec(memory_space=pltpu.VMEM)] * len(widths),
            scratch_shapes=[pltpu.SemaphoreType.DMA((len(cut_plan),))],
            compiler_params=pltpu.CompilerParams(vmem_limit_bytes=16 * 1024 * 1024),
            cost_estimate=COST,
        )(dyn, *ins)
    else:
        outs = [jnp.zeros(shape, ins[0].dtype) for shape in shapes]
        for i, src, src_col, out, dst, dst_col, wide in cut_plan:
            piece = ins[i][src][:, src_col : src_col + wide]
            zi, yi, xi = dst(at.z, at.y, at.x)
            zi = (zi + turns[out]) % at.nz
            outs[out] = lax.dynamic_update_slice(
                outs[out], piece[None, None, None], (zi, yi, xi, 0, dst_col)
            )
    return tuple(o.reshape(at.nz * 4 * rows, w) for o, w in zip(outs, widths))


class Pieces:
    def __init__(self, at, rows, cols):
        self.at, self.rows, self.cols = at, rows, cols
        self.arrays, self.plan = [], []

    def add(self, array, places):
        i, nz = len(self.arrays), self.at.nz
        self.arrays.append(array)
        for index, src_col, (k, dx, dy), col, wide in places:

            def slot(z, y, x, k=k, dx=dx, dy=dy):
                return lax.rem(z - k + nz, nz), flip(y, dy), flip(x, dx)

            self.plan.append((i, index, src_col, slot, col, wide))

    def place(self, line, widths, turned=(False, False)):
        return line.run(
            lambda *v: place(self.at, v, self.plan, self.rows, widths, turned[: len(widths)]),
            *self.arrays,
        )


def pick(values, i, axis=0):
    return lax.dynamic_index_in_dim(values, i, axis, keepdims=False)


class Scatter:
    def __init__(self, line, at, cut, pairs, ends=()):
        self.line, self.at, self.cut, self.pairs = line, at, cut, pairs
        self.ends = ends
        self.ring_at = 0
        self.total = self.low = self.high = self.extra = self.extra_came = None

    def blocks(self, total):
        at = self.at
        return total.reshape(at.nz, 2, 2, 2 * at.own_rows, total.shape[1])

    def cut_out(self, total):
        at, cut = self.at, self.cut
        self.whole = total
        self.low, self.high = [], []

        def step(total):
            v = self.blocks(total)
            low, high = pick(v[..., :cut], 1 - at.y, 1), pick(v[..., cut:], 1 - at.x, 2)
            ends = [0, *self.ends, at.nz]
            return tuple(v[i:j] for v in (low, high) for i, j in zip(ends[:-1], ends[1:]))

        self.parts = list(self.line.run(step, total))

    def begin(self):
        n = len(self.ends) + 1
        i = len(self.low)
        self.low.append(self.line.start(self.parts[i], self.at.to_y))
        self.high.append(self.line.start(self.parts[n + i], self.at.to_x))

    def more(self, total):
        self.extra = total
        part = self.line.run(lambda v: pick(self.blocks(v), 1 - self.at.x, 2), total)
        self.extra_came = self.line.start(part, self.at.to_x)

    def first_of(self, kept):
        return kept, pick(kept, (self.at.z - 1 + self.at.nz) % self.at.nz)

    def arrive(self):
        for going in (self.total, self.low, self.high, self.extra_came):
            if isinstance(going, Going):
                self.line.done(going)
            elif isinstance(going, list):
                self.line.done(*going)

    def keep_run(self):
        at, cut = self.at, self.cut
        came = self.line.done(*self.low, *self.high)
        n = len(self.low)
        extra = () if self.extra is None else (self.extra, self.line.done(self.extra_came))

        def step(total, *came):
            low, high = jnp.concatenate(came[:n]), jnp.concatenate(came[n : 2 * n])
            v = self.blocks(total)
            low = pick(v[..., :cut], at.y, 1).astype(f32) + low.astype(f32)
            high = pick(v[..., cut:], at.x, 2).astype(f32) + high.astype(f32)
            parts = [low, high]
            if extra:
                mine, other = came[2 * n :]
                parts.append(pick(self.blocks(mine), at.x, 2).astype(f32) + other.astype(f32))
            parts = [p.astype(bf16) for p in parts]
            if self.pairs:
                return self.first_of(jnp.concatenate(parts, axis=-1))
            low, high = parts
            return (
                pick(low, at.x, 1), pick(high, at.y, 1),
                pick(low, 1 - at.x, 1), pick(high, 1 - at.y, 1),
            )

        self.kept = self.line.run(step, self.whole, *came, *extra)
        self.whole = self.extra = self.extra_came = self.low = self.high = None

    def keep_start(self):
        kept = self.kept
        if self.pairs:
            self.kept = kept[0]
            self.total = self.line.start(kept[1], self.at.to_z)
        else:
            self.kept = kept[:2]
            self.low = self.line.start(kept[2], self.at.to_x)
            self.high = self.line.start(kept[3], self.at.to_y)

    def keep(self):
        self.keep_run()
        self.keep_start()

    def second(self):
        low, high = self.line.done(self.low, self.high)

        def step(kept_low, kept_high, low, high):
            low = (kept_low.astype(f32) + low.astype(f32)).astype(bf16)
            high = (kept_high.astype(f32) + high.astype(f32)).astype(bf16)
            return self.first_of(jnp.concatenate([low, high], axis=-1))

        self.kept, first = self.line.run(step, *self.kept, low, high)
        self.total = self.line.start(first, self.at.to_z)

    def ring(self):
        at, cut, k = self.at, self.cut, self.ring_at
        if k == at.nz - 1:
            return
        self.ring_at += 1
        last = self.ring_at == at.nz - 1

        def step(total, kept):
            total = total.astype(f32) + pick(kept, (at.z - 2 - k + at.nz) % at.nz).astype(f32)
            if not last:
                return total.astype(bf16)
            if self.pairs:
                low, high = total[..., :cut], total[..., cut:]
                return (
                    jnp.concatenate([pick(low, at.x), pick(high, at.y)], axis=-1),
                    pick(low, 1 - at.x).astype(bf16),
                    pick(high, 1 - at.y).astype(bf16),
                )
            return total

        came = self.line.done(self.total)
        total = self.line.run(step, came, self.kept)
        if not last:
            self.total = self.line.start(total, at.to_z)
        elif self.pairs:
            self.total, self.low, self.high = total
        else:
            self.total = total

    def last_step(self):
        for _ in range(self.at.nz):
            self.ring()

    def last_start(self):
        self.last_step()
        self.low = self.line.start(self.low, self.at.to_x)
        self.high = self.line.start(self.high, self.at.to_y)

    def last(self):
        rows = self.at.own_rows
        self.last_step()

        def step(total, *came):
            if came:
                total = total + jnp.concatenate(came, axis=-1).astype(f32)
            low, high = total[:rows], total[rows:]
            return jnp.where(self.at.c == 0, low, high), jnp.where(self.at.c == 0, high, low)

        came = self.line.done(self.low, self.high) if self.pairs else ()
        self.mine, theirs = self.line.run(step, self.total, *came)
        self.theirs = self.line.start(theirs, self.at.to_core)

    def result(self):
        theirs = self.line.done(self.theirs)
        return (
            jnp.where(self.at.c == 0, self.mine, theirs),
            jnp.where(self.at.c == 0, theirs, self.mine),
        )


class Sums:
    def __init__(self, line, at, value):
        self.line, self.value = line, value
        self.steps = [at.to_core, at.to_x, at.to_y] + at.z_swaps
        self.going = None

    def step(self):
        if self.going is not None:
            came = self.line.done(self.going)
            self.value = self.line.run(lambda v, c: v + c, self.value, came)
        self.going = self.line.start(self.value, self.steps.pop(0)) if self.steps else None

    def result(self):
        while self.going is not None:
            self.step()
        return self.value


CHUNK = 512


def window(h, wide):
    start = pl.multiple_of(jnp.minimum((h * HD) // LANE, (wide - WIN) // LANE) * LANE, LANE)
    return start, h * HD - start


def lane_masks(off, rows):
    lane = lax.broadcasted_iota(jnp.int32, (rows, WIN), 1)
    return (lane >= off) & (lane < off + HD), lane >= WIN - 4


def attend_kernel(first, last, wide, qkv_ref, qf_ref, kf_ref, old_ref, old_lse, out_ref, lse_ref):
    n = qkv_ref.shape[0]
    scale = (HD ** -0.5) * 1.4426950408889634
    zero = jnp.zeros((), bf16)
    if first == 0:
        out_ref[...] = jnp.zeros_like(out_ref)
    else:
        lse_ref[...] = old_lse[...]
        out_ref[...] = old_ref[...]

    def head(h, carry):
        start, off = window(h, wide)
        inside, feature = lane_masks(off, n)
        at = pl.ds(start, WIN)
        k = qkv_ref[:, pl.ds(start + wide, WIN)]
        k = jnp.where(inside, k, jnp.where(feature, kf_ref[...], zero))
        v_t = jnp.where(inside, qkv_ref[:, pl.ds(start + 2 * wide, WIN)], zero).T
        for i in range(n // CHUNK):
            rows = slice(i * CHUNK, (i + 1) * CHUNK)
            q = jnp.where(feature[:CHUNK], qf_ref[rows, :], qkv_ref[rows, at])
            s = lax.dot_general(k, q, NT, preferred_element_type=f32)
            top = jnp.max(s, axis=0, keepdims=True) * scale
            p = jnp.exp2(s * scale - top)
            total = jnp.sum(p, axis=0, keepdims=True)
            o_t = lax.dot_general(v_t, p.astype(bf16), NN, preferred_element_type=f32)
            out = (o_t / total).T.astype(bf16)
            out_ref[rows, at] = jnp.where(inside[:CHUNK], out, out_ref[rows, at])
            lse_ref[pl.ds(h, 1), rows] = top + jnp.log2(total)
        return carry

    lax.fori_loop(first, last, head, 0)


def attend(first, last, qkv, qf, kf, *old):
    n, wide = qkv.shape[0], qkv.shape[1] // 3
    heads = H // 2
    if not old:
        old = (jnp.zeros((16, LANE), bf16), jnp.zeros((8, LANE), f32))
    return tuple(
        pl.pallas_call(
            functools.partial(attend_kernel, first, last, wide),
            out_shape=(
                jax.ShapeDtypeStruct((n, wide), bf16),
                jax.ShapeDtypeStruct((heads, n), f32),
            ),
            compiler_params=pltpu.CompilerParams(vmem_limit_bytes=28 * 1024 * 1024),
            cost_estimate=COST,
        )(qkv, qf, kf, *old)
    )


def back_kernel(first, last, wide, qkv_ref, do_ref, qf_ref, kf_ref, lse_ref, old_ref, out_ref):
    n = qkv_ref.shape[0]
    scale = HD ** -0.5
    scale_two = scale * 1.4426950408889634
    zero = jnp.zeros((), bf16)
    if first == 0:
        out_ref[...] = jnp.zeros_like(out_ref)
    else:
        out_ref[...] = old_ref[...]

    def head(h, carry):
        start, off = window(h, wide)
        inside, feature = lane_masks(off, n)
        at = pl.ds(start, WIN)
        at_k, at_v = pl.ds(start + wide, WIN), pl.ds(start + 2 * wide, WIN)
        k_win = qkv_ref[:, at_k]
        k = jnp.where(inside, k_win, jnp.where(feature, kf_ref[...], zero))
        k_t = jnp.where(inside, k_win, zero).T
        v = qkv_ref[:, at_v]
        dk, dv = None, None
        for i in range(n // CHUNK):
            rows = slice(i * CHUNK, (i + 1) * CHUNK)
            q_win = qkv_ref[rows, at]
            q = jnp.where(feature[:CHUNK], qf_ref[rows, :], q_win)
            q_only = jnp.where(inside[:CHUNK], q_win, zero)
            do = jnp.where(inside[:CHUNK], do_ref[rows, at], zero)
            s = lax.dot_general(k, q, NT, preferred_element_type=f32)
            p = jnp.exp2(s * scale_two - lse_ref[pl.ds(h, 1), rows])
            dp = lax.dot_general(v, do, NT, preferred_element_type=f32)
            part = lax.dot_general(p.astype(bf16), do, NN, preferred_element_type=f32)
            dv = part if dv is None else dv + part
            inner = jnp.sum(p * dp, axis=0, keepdims=True)
            ds = (p * (dp - inner)).astype(bf16)
            part = lax.dot_general(ds, q_only, NN, preferred_element_type=f32)
            dk = part if dk is None else dk + part
            dq = lax.dot_general(k_t, ds, NN, preferred_element_type=f32).T
            dq = (dq * scale).astype(bf16)
            out_ref[rows, at] = jnp.where(inside[:CHUNK], dq, out_ref[rows, at])
        out_ref[:, at_k] = jnp.where(inside, (dk * scale).astype(bf16), out_ref[:, at_k])
        out_ref[:, at_v] = jnp.where(inside, dv.astype(bf16), out_ref[:, at_v])
        return carry

    lax.fori_loop(first, last, head, 0)


def attend_back(first, last, qkv, do, qf, kf, lse, *old):
    n, wide = qkv.shape[0], qkv.shape[1] // 3
    if not old:
        old = (jnp.zeros((16, LANE), bf16),)
    return pl.pallas_call(
        functools.partial(back_kernel, first, last, wide),
        out_shape=jax.ShapeDtypeStruct(qkv.shape, bf16),
        compiler_params=pltpu.CompilerParams(vmem_limit_bytes=36 * 1024 * 1024),
        cost_estimate=COST,
    )(qkv, do, qf, kf, lse, *old)


def norm_parts(values):
    center = jnp.mean(values, axis=-1, keepdims=True)
    centered = values - center
    spread = jnp.mean(centered * centered, axis=-1, keepdims=True)
    inverse = lax.rsqrt(spread + norm_epsilon)
    return centered * inverse, inverse


def out_norm_kernel(
    core_ref, x_ref, a_ref, b_ref, w_ref, v_ref, bias_ref, gain_ref, shift_ref, res_ref, norm_ref
):
    half, cut = a_ref.shape[1], w_ref.shape[1]
    width = x_ref.shape[1]
    a, b = a_ref[...], b_ref[...]
    mine = dot(a, w_ref[:half, :]) + dot(b, w_ref[half:, :])
    theirs = dot(a, v_ref[half:, :]) + dot(b, v_ref[:half, :])
    first = core_ref[0] == 0

    @pl.when(first)
    def _():
        res_ref[:, :cut] = mine
        res_ref[:, cut:] = theirs[:, : width - cut]

    @pl.when(jnp.logical_not(first))
    def _():
        res_ref[:, :cut] = theirs
        res_ref[:, cut:] = mine[:, : width - cut]

    values = res_ref[...] + x_ref[...].astype(f32) + bias_ref[...]
    res_ref[...] = values
    unit, _ = norm_parts(values)
    norm_ref[...] = (unit * gain_ref[...] + shift_ref[...]).astype(bf16)


def out_norm(core, x, a, b, w, v, bias, gain, shift):
    t, width = x.shape
    tile = 128
    rows = lambda cols: pl.BlockSpec((tile, cols), lambda i: (i, 0))
    all_of = lambda v: pl.BlockSpec(v.shape, lambda i: (0, 0))
    return tuple(
        pl.pallas_call(
            out_norm_kernel,
            grid=(t // tile,),
            out_shape=[
                jax.ShapeDtypeStruct((t, width), f32),
                jax.ShapeDtypeStruct((t, width), bf16),
            ],
            in_specs=[
                pl.BlockSpec(memory_space=pltpu.SMEM),
                rows(width), rows(a.shape[1]), rows(b.shape[1]), all_of(w), all_of(v),
                all_of(bias), all_of(gain), all_of(shift),
            ],
            out_specs=[rows(width), rows(width)],
            compiler_params=pltpu.CompilerParams(vmem_limit_bytes=16 * 1024 * 1024),
            cost_estimate=COST,
        )(core, x, a, b, w, v, bias, gain, shift)
    )


def norm_back_kernel(t_ref, came_ref, pass_ref, values_ref, gain_ref, out_ref, low_ref, sum_ref):
    t = t_ref[...] + came_ref[...].astype(f32)
    unit, inverse = norm_parts(values_ref[...].astype(f32))
    scaled = t * gain_ref[...]
    along = jnp.mean(scaled * unit, axis=-1, keepdims=True)
    grad = (scaled - jnp.mean(scaled, axis=-1, keepdims=True) - unit * along) * inverse
    grad = pass_ref[...].astype(f32) + grad
    out_ref[...] = grad
    low = grad.astype(bf16)
    low_ref[...] = low

    @pl.when(pl.program_id(0) == 0)
    def _():
        sum_ref[...] = jnp.zeros_like(sum_ref)

    sum_ref[0:1, :] += jnp.sum(t * unit, axis=0, keepdims=True)
    sum_ref[1:2, :] += jnp.sum(t, axis=0, keepdims=True)
    sum_ref[2:3, :] += jnp.sum(low.astype(f32), axis=0, keepdims=True)


def norm_back(t, came, passed, values, gain):
    n, width = t.shape
    tile = 128
    rows = pl.BlockSpec((tile, width), lambda i: (i, 0))
    return tuple(
        pl.pallas_call(
            norm_back_kernel,
            grid=(n // tile,),
            out_shape=[
                jax.ShapeDtypeStruct((n, width), f32),
                jax.ShapeDtypeStruct((n, width), bf16),
                jax.ShapeDtypeStruct((8, width), f32),
            ],
            in_specs=[rows] * 4 + [pl.BlockSpec((1, width), lambda i: (0, 0))],
            out_specs=[rows, rows, pl.BlockSpec((8, width), lambda i: (0, 0))],
            compiler_params=pltpu.CompilerParams(vmem_limit_bytes=16 * 1024 * 1024),
            cost_estimate=COST,
        )(t, came, passed, values, gain)
    )


def column_sum(rows):
    return jnp.sum(rows.astype(f32), axis=0)


def gelu_and_slope(z):
    root = 0.7978845608028654
    cube = 0.044715 * root
    square = z * z
    h = 0.5 + 0.5 * jnp.tanh(z * (root + cube * square))
    value = z * h
    return value, h + 2.0 * value * (1.0 - h) * (root + 3.0 * cube * square)


def up_kernel(n_ref, w_ref, b_ref, value_ref, slope_ref):
    cols = w_ref.shape[1]
    step = 512
    for left in range(0, cols, step):
        part = slice(left, min(left + step, cols))
        value, slope = gelu_and_slope(dot(n_ref[...], w_ref[:, part]) + b_ref[:, part])
        value_ref[:, part] = value.astype(bf16)
        slope_ref[:, part] = slope.astype(bf16)


def hidden_kernel(g_ref, w_ref, s_ref, out_ref, sum_ref):
    cols = w_ref.shape[1]
    step = 512

    @pl.when(pl.program_id(0) == 0)
    def _():
        sum_ref[...] = jnp.zeros_like(sum_ref)

    for left in range(0, cols, step):
        part = slice(left, min(left + step, cols))
        out = (dot(g_ref[...], w_ref[:, part]) * s_ref[:, part].astype(f32)).astype(bf16)
        out_ref[:, part] = out
        sum_ref[0:1, part] += jnp.sum(out.astype(f32), axis=0, keepdims=True)


def hidden_back(g, w, s):
    t, width = g.shape
    cols = w.shape[1]
    tile = 256
    row = pl.BlockSpec((tile, cols), lambda i: (i, 0))
    return tuple(
        pl.pallas_call(
            hidden_kernel,
            grid=(t // tile,),
            out_shape=[
                jax.ShapeDtypeStruct((t, cols), bf16),
                jax.ShapeDtypeStruct((8, cols), f32),
            ],
            in_specs=[
                pl.BlockSpec((tile, width), lambda i: (i, 0)),
                pl.BlockSpec(w.shape, lambda i: (0, 0)),
                row,
            ],
            out_specs=[row, pl.BlockSpec((8, cols), lambda i: (0, 0))],
            compiler_params=pltpu.CompilerParams(vmem_limit_bytes=28 * 1024 * 1024),
            cost_estimate=COST,
        )(g, w, s)
    )


def up_gelu(n, w, b):
    t, width = n.shape
    cols = w.shape[1]
    tile = 256
    out = pl.BlockSpec((tile, cols), lambda i: (i, 0))
    return tuple(
        pl.pallas_call(
            up_kernel,
            grid=(t // tile,),
            out_shape=[jax.ShapeDtypeStruct((t, cols), bf16)] * 2,
            in_specs=[
                pl.BlockSpec((tile, width), lambda i: (i, 0)),
                pl.BlockSpec(w.shape, lambda i: (0, 0)),
                pl.BlockSpec(b.shape, lambda i: (0, 0)),
            ],
            out_specs=[out, out],
            compiler_params=pltpu.CompilerParams(vmem_limit_bytes=28 * 1024 * 1024),
            cost_estimate=COST,
        )(n, w, b)
    )


def on_device(
    tokens,
    lengths,
    norm1_gain,
    norm1_bias,
    w_query,
    query_bias,
    w_key,
    w_value,
    value_bias,
    w_out,
    out_bias,
    norm2_gain,
    norm2_bias,
    w_up,
    up_bias,
    w_down,
    down_bias,
    cotangent,
):
    at = Places(lax.axis_size("rows"), lax.axis_size("seq"))
    line = Line()
    micro, rows_here, local_len, width = tokens.shape
    full_len = local_len * lax.axis_size("seq")
    own = 2 * rows_here * local_len
    own_rows, hidden_width = w_up.shape
    at.own_rows = own_rows
    chip_rows = 2 * own_rows
    zero_core = at.c == 0
    nz = at.nz
    head_width = width // 2
    wide = -(-head_width // LANE) * LANE
    out_cut = wide
    half_width = -(-hidden_width // (2 * LANE)) * LANE

    def by_core(a, b):
        return jnp.where(zero_core, a, b)

    def swapped_in(mine, came):
        low = jnp.where(at.x == 0, mine, came)
        high = jnp.where(at.x == 0, came, mine)
        return jnp.stack([low, high]).reshape(own, width)

    def for_swap_out(values):
        values = values.reshape(2, rows_here, local_len, width)
        return pick(values, at.x), pick(values, 1 - at.x).astype(bf16)

    def swapped_out(mine, came):
        came = came.astype(mine.dtype)
        return jnp.stack([jnp.where(at.x == 0, mine, came), jnp.where(at.x == 0, came, mine)])

    def fill(v, to):
        return jnp.pad(v, ((0, 0), (0, to - v.shape[1])))

    vectors = jnp.stack(
        [norm1_gain, norm1_bias, query_bias, value_bias, out_bias, norm2_gain, norm2_bias, down_bias]
    )
    vectors = dot(jnp.eye(own_rows, dtype=bf16), vectors, NT, bf16)
    me = lax.axis_index("rows") * lax.axis_size("seq") + lax.axis_index("seq")

    spot = jnp.arange(chip_rows, dtype=jnp.int32)
    spot = flip(at.c, spot // own_rows) * own_rows + spot % own_rows
    turn = (jnp.arange(chip_rows, dtype=jnp.int32)[:, None] == spot[None, :]).astype(bf16)
    s_cut, u_cut, d_cut = 10 * LANE, 13 * LANE, 10 * LANE
    s_wide, u_wide, d_wide = 3 * wide, out_cut + half_width, half_width
    s_pieces = Pieces(at, chip_rows, s_wide)
    u_pieces = Pieces(at, chip_rows, u_wide)
    d_pieces = Pieces(at, chip_rows, d_wide)

    def qkv_half(c):
        part = slice(c * head_width, (c + 1) * head_width)
        query = fill(jnp.concatenate([w_query[:, part], vectors], axis=1), wide)
        return jnp.concatenate([query] + [fill(w[:, part], wide) for w in (w_key, w_value)], axis=1)

    def chip_shard(turn, keep, came):
        return dot(turn, jnp.concatenate([keep, came], axis=0), NN, bf16)

    def pair_parts(cut):
        def step(mine, low, high):
            pair = jnp.stack([mine, jnp.concatenate([low, high], axis=1)])
            return pair, pair[:, :, :cut], pair[:, :, cut:]

        return step

    def stack_parts(cut):
        def step(*v):
            return jnp.stack([p[..., :cut] for p in v]), jnp.stack([p[..., cut:] for p in v])

        return step

    def add_pair(pieces, k, array, cut):
        cols = pieces.cols
        pieces.add(
            array,
            [((a,), 0, (k, a, 0), 0, cut) for a in range(2)]
            + [((a,), cut, (k, 0, a), cut, cols - cut) for a in range(2)],
        )

    def add_across(pieces, ks, low, high, cut):
        cols = pieces.cols
        index = lambda i, a: (a,) if len(ks) == 1 and low.ndim == 3 else (i, a)
        every = [(i, k, a) for i, k in enumerate(ks) for a in range(2)]
        pieces.add(low, [(index(i, a), 0, (k, a, 1), 0, cut) for i, k, a in every])
        pieces.add(high, [(index(i, a), 0, (k, 1, a), cut, cols - cut) for i, k, a in every])

    def add_line(pieces, k, array, dx, dy):
        pieces.add(array, [((), 0, (k, dx, dy), 0, pieces.cols)])

    low, high = qkv_half(0), qkv_half(1)
    keep_s, give_s = by_core(low, high), by_core(high, low)
    core = line.start(give_s, at.to_core)
    up_full = fill(w_up, 2 * half_width)
    down_full = fill(dot(jnp.eye(own_rows, dtype=bf16), w_down, NT, bf16), 2 * half_width)
    low = [w_out[:, :out_cut], up_full[:, :half_width], down_full[:, :half_width]]
    high = [fill(w_out[:, out_cut:], out_cut), up_full[:, half_width:], down_full[:, half_width:]]
    low, high = jnp.concatenate(low, axis=1), jnp.concatenate(high, axis=1)
    keep_f, give_f = by_core(low, high), by_core(high, low)

    def other_shards(turn, keep, came):
        both = jnp.concatenate([keep, came], axis=0)
        u, d = dot(turn, both[:, :u_wide], NN, bf16), dot(turn, both[:, u_wide:], NN, bf16)
        return u, u[:, :u_cut], u[:, u_cut:], d, d[:, :d_cut], d[:, d_cut:]

    def tokens_step(tokens, came):
        return swapped_in(pick(tokens, at.x), came)

    def unit_step(own, other):
        return norm_parts(jnp.concatenate([own, other]).astype(f32))[0]

    def stack(*v):
        return jnp.stack(v)

    def low_of(*v):
        return jnp.concatenate([p[..., :s_cut] for p in v])

    def high_of(*v):
        return jnp.concatenate([p[..., s_cut:] for p in v])

    half_z = nz // 2
    ring = [line.run(chip_shard, turn, keep_s, line.done(core))]
    z, y = line.start(ring[0], at.to_z), line.start(ring[0], at.to_y)
    x = line.start(line.run(lambda v: pick(v, 1 - at.x), tokens), at.to_x)
    core = line.start(give_f, at.to_core)
    ring.append(line.done(z))
    z = line.start(ring[-1], at.to_z)
    y_zero, tokens_came, core = line.done(y, x, core)
    shard_u, u_low, u_high, shard_d, d_low, d_high = line.run(other_shards, turn, keep_f, core)
    tokens_own = line.run(tokens_step, tokens, tokens_came)
    for _ in range(2, nz):
        ring.append(line.done(z))
        if len(ring) < nz:
            z = line.start(ring[-1], at.to_z)
        if len(ring) == 3:
            x, y = line.start(u_low, at.to_x), line.start(u_high, at.to_y)
            core = line.start(tokens_own, at.to_core)
    u_low, u_high, ring_tokens = line.done(x, y, core)
    u_pair, u_low, u_high = line.run(pair_parts(u_cut), shard_u, u_low, u_high)
    x = line.start(line.run(stack, *ring[:half_z]), at.to_x)
    y = line.start(line.run(stack, *ring[1:]), at.to_y)
    u_ring = [u_pair]
    z = line.start(u_pair, at.to_z)
    later = line.run(stack, *ring[half_z:])
    xs = [line.done(x)]
    x = line.start(later, at.to_x)
    ys = [y_zero, line.done(y)]
    y = line.start(line.run(low_of, xs[0]), at.to_y)
    x_both = line.start(line.run(high_of, ys[0][None], ys[1]), at.to_x)
    u_ring.append(line.done(z))
    xs.append(line.done(x))
    y_later = line.start(line.run(low_of, xs[1]), at.to_y)
    unit_one = line.run(unit_step, tokens_own, ring_tokens)
    z = line.start(u_ring[-1], at.to_z)
    both_y = [line.done(y)]
    both_x = line.done(x_both)
    both_y.append(line.done(y_later))

    row_lengths = pick(lengths, at.x)[0]
    ends_at = jnp.cumsum(row_lengths)
    inside = jnp.arange(own, dtype=jnp.int32)

    def segment_of(core):
        spots = (inside // local_len) * (full_len // 2) + core * local_len + inside % local_len
        return jnp.sum((spots[:, None] >= ends_at[None, :]).astype(jnp.int32), axis=-1)

    segments = jnp.concatenate([segment_of(at.c), segment_of(1 - at.c)])
    lane = (jnp.arange(WIN, dtype=jnp.int32) % 4)[None, :]
    feat_q = (segments[:, None] == lane).astype(bf16)
    feat_k = jnp.where(segments[:, None] == lane, 0.0, -BIG).astype(bf16)
    feat_q, feat_k = line.run(lambda *v: v, feat_q, feat_k)
    for k in range(nz):
        add_line(s_pieces, k, ring[k], 0, 0)
    for i, ks in enumerate((range(half_z), range(half_z, nz))):
        s_pieces.add(xs[i], [((j,), 0, (k, 1, 0), 0, s_wide) for j, k in enumerate(ks)])
        s_pieces.add(both_y[i], [((j,), 0, (k, 1, 1), 0, s_cut) for j, k in enumerate(ks)])
    add_line(s_pieces, 0, ys[0], 0, 1)
    s_pieces.add(ys[1], [((k - 1,), 0, (k, 0, 1), 0, s_wide) for k in range(1, nz)])
    s_pieces.add(both_x, [((k,), 0, (k, 1, 1), s_cut, s_wide - s_cut) for k in range(nz)])

    weight_s = s_pieces.place(line, (s_wide,))
    chosen = jnp.eye(vectors.shape[1], s_wide, head_width, dtype=bf16)
    left = (head_width // LANE) * LANE
    vectors = line.run(
        lambda e, w: dot(e[:, left:wide], w[:, left:wide], NT), chosen, weight_s
    )
    gain_one, shift_one, bias_q, bias_v, bias_o, gain_two, shift_two, bias_d = [
        vectors[i][None] for i in range(8)
    ]
    halves = [by_core(b[:, :head_width], b[:, head_width:]) for b in (bias_q, bias_v)]
    bias_qkv = jnp.concatenate(
        [fill(halves[0], wide), jnp.zeros((1, wide), f32), fill(halves[1], wide)], axis=1
    )
    normed = line.run(lambda u, g, s: (u * g + s).astype(bf16), unit_one, gain_one, shift_one)
    u_ring.append(line.done(z))
    for _ in range(3, nz - 1):
        u_ring.append(line.done(line.start(u_ring[-1], at.to_z)))
    x_pair, y_pair = line.start(d_low, at.to_x), line.start(d_high, at.to_y)
    x, y = line.start(u_high, at.to_x), line.start(u_low, at.to_y)
    z = line.start(u_ring[-1], at.to_z)
    qkv = line.run(lambda n, w, b: (dot(n, w) + b).astype(bf16), normed, weight_s, bias_qkv)
    add_pair(u_pieces, 0, u_pair, u_cut)
    d_low, d_high = line.done(x_pair, y_pair)
    d_pair, d_low, d_high = line.run(pair_parts(d_cut), shard_d, d_low, d_high)
    high, low = line.done(x, y)
    add_across(u_pieces, [0], low, high, u_cut)
    low, high = line.run(stack_parts(u_cut), *u_ring[1:half_z])
    x, y = line.start(high, at.to_x), line.start(low, at.to_y)
    heads = H // 2
    attended, lse = line.run(functools.partial(attend, 0, heads // 2), qkv, feat_q, feat_k)
    u_ring.append(line.done(z))
    high, low = line.done(x, y)
    add_across(u_pieces, list(range(1, half_z)), low, high, u_cut)
    low, high = line.run(stack_parts(u_cut), *u_ring[half_z:-1])
    z = line.start(d_pair, at.to_z)
    x, y = line.start(high, at.to_x), line.start(low, at.to_y)
    low, high = line.run(stack_parts(u_cut), u_ring[-1])
    attended, lse = line.run(
        functools.partial(attend, heads // 2, heads), qkv, feat_q, feat_k, attended, lse
    )
    d_ring = [d_pair, line.done(z)]
    for k in range(1, nz):
        add_pair(u_pieces, k, u_ring[k], u_cut)
    high_two, low_two = line.done(x, y)
    add_across(u_pieces, list(range(half_z, nz - 1)), low_two, high_two, u_cut)
    attended_own, give = line.run(
        lambda a: (a[:own, :head_width], a[own:, :head_width]), attended
    )
    core = line.start(give, at.to_core)
    x, y = line.start(high, at.to_x), line.start(low, at.to_y)
    z = line.start(d_ring[-1], at.to_z)
    cotangent_theirs = line.run(lambda v: pick(v, 1 - at.x), cotangent)
    attended_other = line.done(core)
    high, low = line.done(x, y)
    add_across(u_pieces, [nz - 1], low, high, u_cut)
    x, y = line.start(cotangent_theirs, at.to_x), line.start(d_low, at.to_y)
    weight_half_o, weight_u = u_pieces.place(line, (out_cut, half_width), (True, False))
    d_ring.append(line.done(z))
    out_came, d_low = line.done(x, y)
    core = line.start(weight_half_o, at.to_core)
    for _ in range(3, nz - 1):
        d_ring.append(line.done(line.start(d_ring[-1], at.to_z)))
    x = line.start(d_high, at.to_x)
    low, high = line.run(stack_parts(d_cut), *d_ring[1:])
    y = line.start(low, at.to_y)
    z = line.start(d_ring[-1], at.to_z)
    grad_out = line.run(
        lambda v, came: swapped_in(pick(v, at.x), came), cotangent, out_came
    )
    other_half_o = line.done(core)
    zero_flag = jnp.reshape(at.c, (1,)).astype(jnp.int32)
    residual_one, normed_two_own = line.run(
        out_norm, zero_flag, tokens_own, attended_own, attended_other, weight_half_o, other_half_o,
        bias_o, gain_two, shift_two,
    )
    add_pair(d_pieces, 0, d_pair, d_cut)
    d_high = line.done(x)
    add_across(d_pieces, [0], d_low, d_high, d_cut)
    low = line.done(y)
    d_ring.append(line.done(z))
    core = line.start(normed_two_own, at.to_core)
    x = line.start(high, at.to_x)
    low_last, high_last = line.run(stack_parts(d_cut), d_ring[-1])
    y, x_last = line.start(low_last, at.to_y), line.start(high_last, at.to_x)
    normed_two = line.run(
        lambda a, b: jnp.concatenate([a, b]), normed_two_own, line.done(core)
    )
    bias_up = fill(up_bias.astype(f32)[None], 2 * half_width)
    bias_up = by_core(bias_up[:, :half_width], bias_up[:, half_width:])

    def up_step(n, w, b):
        return up_gelu(n, w, b)

    active, slope = line.run(up_step, normed_two, weight_u, bias_up)
    high = line.done(x)
    add_across(d_pieces, list(range(1, nz - 1)), low, high, d_cut)
    low, high = line.done(y, x_last)
    add_across(d_pieces, [nz - 1], low, high, d_cut)
    for k in range(1, nz):
        add_pair(d_pieces, k, d_ring[k], d_cut)
    core = line.start(grad_out, at.to_core)
    weight_d = d_pieces.place(line, (half_width,))
    grad_out_all = line.run(lambda a, b: jnp.concatenate([a, b]), grad_out, line.done(core))

    d_down = line.run(lambda g, a: dot(g, a, TN, bf16), grad_out_all, active)
    quarter = nz // 4
    d_scatter = Scatter(line, at, d_cut, True, (quarter, 2 * quarter, 3 * quarter))
    d_scatter.cut_out(d_down)
    d_scatter.begin()
    grad_hidden, hidden_sums = line.run(hidden_back, grad_out_all, weight_d, slope)
    d_scatter.arrive()
    hidden_sums = hidden_sums[0]

    def rows_other(a, w):
        return dot(a[own:], w, NT, bf16)

    def rows_own(a, w):
        return dot(a[:own], w, NT)

    d_scatter.begin()
    give = line.run(rows_other, grad_hidden, weight_u)
    back_own = line.run(rows_own, grad_hidden, weight_u)
    d_scatter.arrive()
    core = line.start(give, at.to_core)
    d_scatter.begin()
    d_up = line.run(lambda n, g: dot(n, g, TN, bf16), normed_two, grad_hidden)
    core = line.done(core)
    d_scatter.arrive()
    d_scatter.begin()
    grad_residual, grad_branch, sums_two = line.run(
        norm_back, back_own, core, grad_out, residual_one, gain_two
    )

    def branch_columns(g):
        a, b = g[:, :out_cut], fill(g[:, out_cut:], out_cut)
        return by_core(a, b), by_core(b, a)

    branch_own, branch_peer = line.run(branch_columns, grad_branch)

    def heads_back(a, v, b, w):
        return (dot(a, v, NT) + dot(b, w, NT)).astype(bf16)

    def out_weight(a, b, g):
        return jnp.concatenate([dot(a, g, TN, bf16), dot(b, g, TN, bf16)])

    give = line.run(
        heads_back, branch_own, weight_half_o[head_width:], branch_peer, other_half_o[:head_width]
    )
    d_out_peer = line.run(out_weight, attended_other, attended_own, branch_peer)
    d_scatter.arrive()
    core = line.start(give, at.to_core)
    d_out_came = line.start(d_out_peer, at.to_core)
    d_scatter.keep()
    u_scatter = Scatter(line, at, u_cut, True, (nz // 2,))
    u_scatter.cut_out(d_up)
    u_scatter.begin()
    grad_att_own = line.run(
        heads_back, branch_own, weight_half_o[:head_width], branch_peer, other_half_o[head_width:]
    )
    grad_att = line.run(
        lambda a, b: fill(jnp.concatenate([a, b]), wide), grad_att_own, line.done(core)
    )

    def out_weight_own(a, b, g, came):
        total = jnp.concatenate([dot(a, g, TN), dot(b, g, TN)]) + came.astype(f32)
        half = total.shape[0] // 2
        low, high = total[:half], total[half:]
        return jnp.concatenate([by_core(low, high), by_core(high, low)]).astype(bf16)

    d_out = line.run(
        out_weight_own, attended_own, attended_other, branch_own, line.done(d_out_came)
    )
    d_scatter.arrive()
    u_scatter.arrive()
    d_scatter.ring()
    u_scatter.begin()
    u_scatter.more(d_out)
    d_qkv = line.run(
        functools.partial(attend_back, 0, heads // 2), qkv, grad_att, feat_q, feat_k, lse
    )
    d_scatter.arrive()
    u_scatter.arrive()
    d_scatter.ring()
    u_scatter.keep()
    d_qkv = line.run(
        functools.partial(attend_back, heads // 2, heads), qkv, grad_att, feat_q, feat_k, lse, d_qkv
    )
    d_scatter.arrive()
    d_scatter.last_start()
    s_scatter = Scatter(line, at, 8 * LANE, False)
    d_s = line.run(lambda n, g: dot(n, g, TN, bf16), normed, d_qkv)
    give = line.run(rows_other, d_qkv, weight_s)
    core = line.start(give, at.to_core)
    s_scatter.cut_out(d_s)
    s_scatter.begin()
    u_scatter.ring()
    back_own = line.run(rows_own, d_qkv, weight_s)
    d_scatter.last()
    grad_tokens, _, sums_one = line.run(
        norm_back, back_own, line.done(core), grad_residual, tokens_own, gain_one
    )
    token_mine, token_theirs = line.run(for_swap_out, grad_tokens)
    give = line.run(rows_other, active, weight_d)
    result_own = line.run(rows_own, active, weight_d)
    s_scatter.arrive()
    u_scatter.arrive()
    def full(half):
        zeros = jnp.zeros_like(half)
        return jnp.concatenate([by_core(half, zeros), by_core(zeros, half)])

    qkv_sums = column_sum(d_qkv)
    sums = jnp.concatenate(
        [
            column_sum(grad_out),
            sums_two[2],
            sums_two[0],
            sums_two[1],
            full(qkv_sums[:head_width]),
            full(qkv_sums[2 * wide : 2 * wide + head_width]),
            sums_one[0],
            sums_one[1],
            full(hidden_sums),
        ]
    )
    sums = jnp.pad(sums, (0, -sums.shape[0] % (8 * LANE))).reshape(-1, LANE)
    sums = line.run(lambda v: v, sums)
    core = line.start(give, at.to_core)
    sums_at = Sums(line, at, sums)
    sums_at.step()
    s_scatter.keep()
    u_scatter.ring()
    block_output = line.run(
        lambda r, t, c, b: (r + t + c.astype(f32) + b).astype(bf16),
        residual_one, result_own, line.done(core), bias_d,
    )
    out_mine, out_theirs = line.run(for_swap_out, block_output)
    s_scatter.arrive()
    sums_at.step()
    s_scatter.second()
    token_came = line.start(token_theirs, at.to_x)
    u_scatter.arrive()
    sums_at.step()
    u_scatter.last_start()
    s_scatter.ring()
    out_came = line.start(out_theirs, at.to_x)
    sums_at.step()
    s_scatter.ring()
    u_scatter.last()
    sums_at.step()
    s_scatter.last()
    sums_at.step()
    sums = sums_at.result()
    grad_tokens = swapped_out(token_mine, line.done(token_came))
    block_output = swapped_out(out_mine, line.done(out_came))
    sums = sums.reshape(-1)

    def my_part(i):
        return lax.dynamic_slice_in_dim(sums, i * width + me * own_rows, own_rows)

    def joined(parts, left, right):
        return jnp.concatenate([p[:, left:right] for p in parts], axis=1)

    d_down, d_up, d_qkv = d_scatter.result(), u_scatter.result(), s_scatter.result()
    return (
        block_output,
        grad_tokens,
        my_part(6),
        my_part(7),
        joined(d_qkv, 0, head_width),
        my_part(4),
        joined(d_qkv, wide, wide + head_width),
        joined(d_qkv, 2 * wide, 2 * wide + head_width),
        my_part(5),
        joined(d_up, half_width, u_wide)[:, :width],
        my_part(1),
        my_part(2),
        my_part(3),
        joined(d_up, 0, half_width)[:, :hidden_width],
        sums[8 * width : 8 * width + hidden_width],
        joined(d_down, 0, half_width)[:, :hidden_width].T,
        my_part(0),
    )


def solution(mesh):
    feature = P(AXES)
    matrix = P(AXES, None)
    row = P(None, "rows", "seq", None)
    return jax.shard_map(
        on_device,
        mesh=mesh,
        in_specs=(
            row,
            P(None, "rows", None),
            feature,
            feature,
            matrix,
            feature,
            matrix,
            matrix,
            feature,
            matrix,
            feature,
            feature,
            feature,
            matrix,
            P(),
            P(None, AXES),
            feature,
            row,
        ),
        out_specs=(
            row,
            row,
            feature,
            feature,
            matrix,
            feature,
            matrix,
            matrix,
            feature,
            matrix,
            feature,
            feature,
            feature,
            matrix,
            P(),
            P(None, AXES),
            feature,
        ),
        check_vma=False,
    )
```

time: 812 us -> 527 us (0.65)
  waiting for transfers between devices: 352 us -> 139 us
  blocking collectives: 107 us -> 0 us
  matrix products: 143 us -> 56.1 us
  local copies, waits for them, and re-layouts: 19.5 us -> 87.7 us
  other arithmetic: 30.7 us -> 67.7 us
  starting transfers between devices: 55.2 us -> 77.2 us
    ppermute x101 -> x88, waiting for transfers between devices: 352 us -> 139 us  [send(): return lax.ppermute(value, AXES, pairs)]
    dot_general x56 -> x24, matrix products: 143 us -> 56.1 us  [dot(): return lax.dot_general(a, b, dims, preferred_element_type=f32).astype(out)]
    all_gather x1 -> x0, blocking collectives: 59.2 us -> none  [on_device(): vectors = lax.all_gather(vectors, AXES, axis=0)]
    psum x1 -> x0, blocking collectives: 47.8 us -> none  [on_device(): late = lax.psum(late, AXES)]
    unnamed x194 -> x244, local copies, waits for them, and re-layouts: 11 us -> 40 us
    ppermute x101 -> x88, starting transfers between devices: 55.2 us -> 77.2 us  [send(): return lax.ppermute(value, AXES, pairs)]
    slice x14 -> x49, local copies, waits for them, and re-layouts: 2.28 us -> 19.9 us  [the longest x4 3.22 us: step(): v[i:j]]
    another operation x1 -> x16, local copies, waits for them, and re-layouts: 0.01 us -> 10.8 us  [the longest x6 5.97 us: step(): jnp.stack([p[..., :cut] for p in v])]
  transfers between devices with their start and end apart: 101 -> 88, of which waited for: 50 -> 34; matrix products, arithmetic and copies ran while one was open for 21% -> 25% of each run, Pallas kernels for 12% -> 16%
where the time goes in v2:
time: 527 us; the launch traced here: 518 us
  waiting for transfers between devices  139 us (26%)
  local copies, waits for them, and re-layouts  87.7 us (17%)
  Pallas kernels  87 us (17%)
  starting transfers between devices  77.2 us (15%)
  other arithmetic  67.7 us (13%)
  matrix products  56.1 us (11%)
    ppermute x88, waiting for transfers between devices, send(): return lax.ppermute(value, AXES, pairs)  139 us
    ppermute x88, starting transfers between devices, send(): return lax.ppermute(value, AXES, pairs)  77.2 us
    dot_general x24, matrix products, dot(): return lax.dot_general(a, b, dims, preferred_element_type=f32).astype(out)  56.1 us
    unnamed x244, local copies, waits for them, and re-layouts  40 us
    pallas_call x2, Pallas kernels, attend_back(): pl.pallas_call(functools.partial(back_kernel, first, last, wide), out_sha...  33.4 us
    pallas_call x2, Pallas kernels, attend(): pl.pallas_call(functools.partial(attend_kernel, first, last, wide), out_s...  19 us
  transfers between devices with their start and end apart: 88, of which 34 were waited for; matrix products, arithmetic and copies ran while one was open for 25% of the time, Pallas kernels for 16%

profile of v2, /device:TPU:0, one launch (start us, length us, event | category | flops | bytes accessed | tf_op | source)
XLA Modules:
  0.0 517.9 jit_solution(5701375463686395226)
XLA Ops:
  8.3 2.9 collective-permute-start.1
  15.2 7.8 %collective-permute-done.3.refs_2_ = bf16[72,1920]{1,0:T(8,128)(2,1)S(1)} collective-permute-done((bf16[72,1920]{1,0:T(8,128)(2,1)S(1)}, bf16[72,1920]{1,0:T(8,128)(2,1)S(1)}, u32[]{:S(2)}, u32[]{:S(2)}) %collective-permute-start.3) | collective-permute-done | bytes 276512 | tf_op jit(solution)/shard_map/ppermute | solution.py:61
  29.9 3.2 collective-permute-done.5.refs_3_
  37.5 7.2 %collective-permute-done.9.refs_4_ = bf16[72,1920]{1,0:T(8,128)(2,1)S(1)} collective-permute-done((bf16[72,1920]{1,0:T(8,128)(2,1)S(1)}, bf16[72,1920]{1,0:T(8,128)(2,1)S(1)}, u32[]{:S(2)}, u32[]{:S(2)}) %collective-permute-start.9) | collective-permute-done | bytes 276512 | tf_op jit(solution)/shard_map/ppermute | solution.py:61
  53.3 10.1 %collective-permute-done.10.refs_5_ = bf16[2,72,1920]{2,1,0:T(8,128)(2,1)} collective-permute-done((bf16[2,72,1920]{2,1,0:T(8,128)(2,1)}, bf16[2,72,1920]{2,1,0:T(8,128)(2,1)}, u32[]{:S(2)}, u32[]{:S(2)}) %collective-permute-start.10) | collective-permute-done | bytes 552992 | tf_op jit(solution)/shard_map/ppermute | solution.py:61
  64.8 6.6 %collective-permute-done.13.refs_10_ = bf16[3,72,1920]{2,1,0:T(8,128)(2,1)} collective-permute-done((bf16[3,72,1920]{2,1,0:T(8,128)(2,1)}, bf16[3,72,1920]{2,1,0:T(8,128)(2,1)}, u32[]{:S(2)}, u32[]{:S(2)}) %collective-permute-start.13) | collective-permute-done | bytes 829472 | tf_op jit(solution)/shard_map/ppermute | solution.py:61
  78.7 2.0 fusion.2
  80.8 2.2 collective-permute-start.15
  83.0 3.9 fusion
  86.9 3.3 collective-permute-done.15.refs_8_
  90.2 2.3 shard_map.305
  92.6 2.1 copy-done.23
  95.6 4.2 add_convert_fusion.1
  99.9 4.9 collective-permute-done.17.refs_7_
  107.0 8.3 %add_convert_fusion.qkv_ref = bf16[1024,1920]{1,0:T(8,128)(2,1)S(1)} fusion(f32[1920]{0:T(1024)S(1)} %reduce.2, bf16[1024,1152]{1,0:T(8,128)(2,1)} %add_convert_fusion.1, bf16[1152,1920]{1,0:T(8,128)(2,1)} %bitcast.315), kind=kOutput, calls=%fused_computation.3 | convolution fusion | flops 4533780480 | bytes 10722816 | tf_op jit(solution)/shard_map/dot_general | solution.py:26
  119.3 6.1 %collective-permute-done.19.refs_3_ = bf16[2,72,1152]{2,1,0:T(8,128)(2,1)S(1)} collective-permute-done((bf16[2,72,1152]{2,1,0:T(8,128)(2,1)S(1)}, bf16[2,72,1152]{2,1,0:T(8,128)(2,1)S(1)}, u32[]{:S(2)}, u32[]{:S(2)}) %collective-permute-start.19) | collective-permute-done | bytes 331808 | tf_op jit(solution)/shard_map/ppermute | solution.py:61
  128.3 2.3 collective-permute-start.23
  130.7 9.5 %shard_map.306 = (bf16[1024,640]{1,0:T(8,128)(2,1)S(1)}, f32[8,1024]{1,0:T(8,128)S(1)}) custom-call(bf16[1024,1920]{1,0:T(8,128)(2,1)S(1)} %add_convert_fusion.qkv_ref, bf16[1024,256]{1,0:T(8,128)(2,1)S(1)} %copy-done.19, bf16[1024,256]{1,0:T(8,128)(2,1)S(1)} %copy-done.21, bf16[16,128]{1,0:T(8,128)(2,1)S(1)} %broadcast_12_old_ref.2.old_ref, ...), custom_call_target="tpu_custom_call" | custom-call | flops 5000000000 | bytes 10000000 | tf_op jit(solution)/shard_map/pallas_call | solution.py:405
  146.5 9.5 %shard_map.307 = (bf16[1024,640]{1,0:T(8,128)(2,1)S(1)}, f32[8,1024]{1,0:T(8,128)S(1)}) custom-call(bf16[1024,1920]{1,0:T(8,128)(2,1)S(1)} %add_convert_fusion.qkv_ref, bf16[1024,256]{1,0:T(8,128)(2,1)S(1)} %copy-done.19, bf16[1024,256]{1,0:T(8,128)(2,1)S(1)} %copy-done.21, bf16[1024,640]{1,0:T(8,128)(2,1)S(1)} %get-tuple-element.916.old_ref, ...), custom_call_target="tpu_custom_call" | custom-call | flops 5000000000 | bytes 10000000 | tf_op jit(solution)/shard_map/pallas_call | solution.py:405
  157.3 2.1 copy.68
  165.0 6.6 %collective-permute-done.30.refs_12_ = bf16[1,2,72,1152]{3,2,1,0:T(8,128)(2,1)S(1)} collective-permute-done((bf16[1,2,72,1152]{3,2,1,0:T(8,128)(2,1)}, bf16[1,2,72,1152]{3,2,1,0:T(8,128)(2,1)S(1)}, u32[]{:S(2)}, u32[]{:S(2)}) %collective-permute-start.30) | collective-permute-done | bytes 331808 | tf_op jit(solution)/shard_map/ppermute | solution.py:61
  186.7 2.9 shard_map.308
  189.7 2.3 copy-done.51
  200.3 2.1 copy.69.b_ref
  206.3 4.3 shard_map.309
  212.0 3.8 collective-permute-done.36.refs_4_
  220.4 2.4 copy-done.52
  222.8 8.8 %shard_map.310 = (bf16[1024,2176]{1,0:T(8,128)(2,1)S(1)}, bf16[1024,2176]{1,0:T(8,128)(2,1)S(1)}) custom-call(bf16[1024,1152]{1,0:T(8,128)(2,1)S(1)} %pad_maximum_fusion.3.n_ref, bf16[1152,2176]{1,0:T(8,128)(2,1)S(1)} %bitcast.325, f32[1,2176]{1,0:T(1,128)S(1)} %broadcast_select_fusion.14.b_ref), custom_call_target="tpu_custom_call" | custom-call | flops 5000000000 | bytes 10000000 | tf_op jit(solution)/shard_map/pallas_call | solution.py:643
  231.7 2.0 copy-done.55
  241.3 2.7 shard_map.311
  244.0 2.5 pad_maximum_fusion.4.g_ref
  248.5 6.3 %convolution_convert_fusion.1 = bf16[1152,2176]{1,0:T(8,128)(2,1)S(1)} fusion(bf16[1024,1152]{1,0:T(8,128)(2,1)S(1)} %pad_maximum_fusion.4.g_ref, bf16[1024,2176]{1,0:T(8,128)(2,1)S(1)} %copy-done.57), kind=kOutput, calls=%fused_computation.1 | convolution fusion | flops 5136334848 | bytes 11829248 | tf_op jit(solution)/shard_map/dot_general | solution.py:26
  258.1 7.3 %shard_map.312 = (bf16[1024,2176]{1,0:T(8,128)(2,1)S(1)}, f32[8,2176]{1,0:T(8,128)S(1)}) custom-call(bf16[1024,1152]{1,0:T(8,128)(2,1)S(1)} %pad_maximum_fusion.4.g_ref, bf16[1152,2176]{1,0:T(8,128)(2,1)S(1)} %bitcast.320, bf16[1024,2176]{1,0:T(8,128)(2,1)S(1)} %bitcast.331), custom_call_target="tpu_custom_call" | custom-call | flops 5000000000 | bytes 10000000 | tf_op jit(solution)/shard_map/pallas_call | solution.py:618
  265.3 2.2 collective-permute-done.44
  267.6 4.2 convolution_convert_fusion.8
  274.7 3.2 fusion.11.t_ref
  277.9 4.9 collective-permute-done.46
  285.7 6.3 %convolution_convert_fusion = bf16[1152,2176]{1,0:T(8,128)(2,1)S(1)} fusion(bf16[1024,1152]{1,0:T(8,128)(2,1)S(1)} %copy-done.3, bf16[1024,2176]{1,0:T(8,128)(2,1)S(1)} %get-tuple-element.1099), kind=kOutput, calls=%fused_computation | convolution fusion | flops 5136334848 | bytes 11829248 | tf_op jit(solution)/shard_map/dot_general | solution.py:26
  292.0 3.1 collective-permute-done.49
  295.2 2.8 shard_map.313
  305.2 3.0 collective-permute-done.50
  321.3 2.1 copy.77
  328.4 9.5 %collective-permute-done.54 = bf16[2,72,2176]{2,1,0:T(8,128)(2,1)} collective-permute-done((bf16[2,72,2176]{2,1,0:T(8,128)(2,1)}, bf16[2,72,2176]{2,1,0:T(8,128)(2,1)}, u32[]{:S(2)}, u32[]{:S(2)}) %collective-permute-start.54) | collective-permute-done | bytes 626720 | tf_op jit(solution)/shard_map/ppermute | solution.py:61
  337.9 6.4 %collective-permute-done.56 = bf16[2,2,72,1664]{3,2,1,0:T(8,128)(2,1)} collective-permute-done((bf16[2,2,72,1664]{3,2,1,0:T(8,128)(2,1)}, bf16[2,2,72,1664]{3,2,1,0:T(8,128)(2,1)}, u32[]{:S(2)}, u32[]{:S(2)}) %collective-permute-start.56) | collective-permute-done | bytes 958496 | tf_op jit(solution)/shard_map/ppermute | solution.py:61
  347.1 4.3 collective-permute-start.58
  352.2 16.8 %shard_map.314.old_ref = bf16[1024,1920]{1,0:T(8,128)(2,1)S(1)} custom-call(bf16[1024,1920]{1,0:T(8,128)(2,1)S(1)} %copy-done.54, bf16[1024,640]{1,0:T(8,128)(2,1)S(1)} %fusion.24.do_ref, bf16[1024,256]{1,0:T(8,128)(2,1)S(1)} %copy-done.20, bf16[1024,256]{1,0:T(8,128)(2,1)S(1)} %copy-done.22, f32[8,1024]{1,0:T(8,128)S(1)} %get-tuple-element.1238.lse_ref, ...), custom_call_target="tpu_custom_call" | custom-call | flops 5000000000 | bytes 10000000 | tf_op jit(solution)/shard_map/pallas_call | solution.py:466
  375.7 3.1 collective-permute-start.62
  378.8 16.6 %shard_map.315 = bf16[1024,1920]{1,0:T(8,128)(2,1)S(1)} custom-call(bf16[1024,1920]{1,0:T(8,128)(2,1)S(1)} %copy-done.54, bf16[1024,640]{1,0:T(8,128)(2,1)S(1)} %fusion.24.do_ref, bf16[1024,256]{1,0:T(8,128)(2,1)S(1)} %copy-done.20, bf16[1024,256]{1,0:T(8,128)(2,1)S(1)} %copy-done.22, f32[8,1024]{1,0:T(8,128)S(1)} %get-tuple-element.1238.lse_ref, ...), custom_call_target="tpu_custom_call" | custom-call | flops 5000000000 | bytes 10000000 | tf_op jit(solution)/shard_map/pallas_call | solution.py:466
  398.7 5.7 %convolution_convert_fusion.2 = bf16[1152,1920]{1,0:T(8,128)(2,1)S(1)} fusion(bf16[1024,1152]{1,0:T(8,128)(2,1)S(1)} %copy-done.71, bf16[1024,1920]{1,0:T(8,128)(2,1)S(1)} %shard_map.315), kind=kOutput, calls=%fused_computation.4 | convolution fusion | flops 4532060160 | bytes 10715136 | tf_op jit(solution)/shard_map/dot_general | solution.py:26
  404.4 2.9 convolution_convert_fusion.6
  411.6 3.2 collective-permute-done.61
  417.3 2.9 fusion.16.t_ref
  422.1 3.4 shard_map.316
  427.6 4.2 convolution_convert_fusion.7
  431.8 4.7 fusion.8
  436.4 3.4 collective-permute-done.68
  447.4 2.6 fusion.19
  455.2 2.4 add_convert_fusion.2
  457.7 8.3 %collective-permute-done.71 = bf16[4,72,1024]{2,1,0:T(8,128)(2,1)} collective-permute-done((bf16[4,72,1024]{2,1,0:T(8,128)(2,1)}, bf16[4,72,1024]{2,1,0:T(8,128)(2,1)}, u32[]{:S(2)}, u32[]{:S(2)}) %collective-permute-start.71) | collective-permute-done | bytes 589856 | tf_op jit(solution)/shard_map/ppermute | solution.py:61
  471.3 3.7 collective-permute-done.75
  482.1 9.1 %collective-permute-done.80 = bf16[1,256,1152]{2,1,0:T(8,128)(2,1)S(1)} collective-permute-done((bf16[1,256,1152]{2,1,0:T(8,128)(2,1)S(1)}, bf16[1,256,1152]{2,1,0:T(8,128)(2,1)S(1)}, u32[]{:S(2)}, u32[]{:S(2)}) %collective-permute-start.80) | collective-permute-done | bytes 589856 | tf_op jit(solution)/shard_map/ppermute | solution.py:61
  492.0 4.4 collective-permute-done.78
  500.5 6.7 %collective-permute-done.77 = bf16[1,256,1152]{2,1,0:T(8,128)(2,1)S(1)} collective-permute-done((bf16[1,256,1152]{2,1,0:T(8,128)(2,1)S(1)}, bf16[1,256,1152]{2,1,0:T(8,128)(2,1)S(1)}, u32[]{:S(2)}, u32[]{:S(2)}) %collective-permute-start.77) | collective-permute-done | bytes 589856 | tf_op jit(solution)/shard_map/ppermute | solution.py:61
  509.2 3.1 collective-permute-done.84
  (602 shorter events, 200.9 us)
Async XLA Ops:
  8.3 16.7 %collective-permute-start.1 = (bf16[1,256,1152]{2,1,0:T(8,128)(2,1)}, bf16[1,256,1152]{2,1,0:T(8,128)(2,1)S(1)}, u32[]{:S(2)}, u32[]{:S(2)}) collective-permute-start(bf16[1,256,1152]{2,1,0:T(8,128)(2,1)} %dynamic-slice_bitcast_fusion.12), channel_id=1, source_target_pairs={{0,2},{1,3},{2,0},{3,1},{4,6},{5,7},{6,4},{7,5},{8,10},{9,11},{10,... | collective-permute-start | bytes 1769480 | tf_op jit(solution)/shard_map/ppermute | solution.py:61
  12.1 13.0 %collective-permute-start.4 = (bf16[36,4992]{1,0:T(8,128)(2,1)}, bf16[36,4992]{1,0:T(8,128)(2,1)S(1)}, u32[]{:S(2)}, u32[]{:S(2)}) collective-permute-start(bf16[36,4992]{1,0:T(8,128)(2,1)} %get-tuple-element.760), channel_id=1, source_target_pairs={{0,1},{1,0},{2,3},{3,2},{4,5},{5,4},{6,7},{7,6},{8,9},{9,8},{10,11... | collective-permute-start | bytes 1078280 | tf_op jit(solution)/shard_map/ppermute | solution.py:61
  12.1 10.9 %collective-permute-start.3 = (bf16[72,1920]{1,0:T(8,128)(2,1)S(1)}, bf16[72,1920]{1,0:T(8,128)(2,1)S(1)}, u32[]{:S(2)}, u32[]{:S(2)}) collective-permute-start(bf16[72,1920]{1,0:T(8,128)(2,1)S(1)} %convolution_convert_fusion.9.refs_1_), channel_id=1, source_target_pairs={{0,8},{1,9},{2,10},{3,11},{4,12},{5,13},{6,14},{7,15},{8,16},{9,17... | collective-permute-start | bytes 829448 | tf_op jit(solution)/shard_map/ppermute | solution.py:61
  33.1 11.6 %collective-permute-start.6 = (bf16[512,1152]{1,0:T(8,128)(2,1)S(1)}, bf16[512,1152]{1,0:T(8,128)(2,1)}, u32[]{:S(2)}, u32[]{:S(2)}) collective-permute-start(bf16[512,1152]{1,0:T(8,128)(2,1)S(1)} %bitcast.291), channel_id=1, source_target_pairs={{0,1},{1,0},{2,3},{3,2},{4,5},{5,4},{6,7},{7,6},{8,9},{9,8},{10,11... | collective-permute-start | bytes 3538952 | tf_op jit(solution)/shard_map/ppermute | solution.py:61
  33.4 11.3 %collective-permute-start.8 = (bf16[72,1664]{1,0:T(8,128)(2,1)}, bf16[72,1664]{1,0:T(8,128)(2,1)S(1)}, u32[]{:S(2)}, u32[]{:S(2)}) collective-permute-start(bf16[72,1664]{1,0:T(8,128)(2,1)} %slice.558), channel_id=1, source_target_pairs={{0,2},{1,3},{2,0},{3,1},{4,6},{5,7},{6,4},{7,5},{8,10},{9,11},{10,... | collective-permute-start | bytes 718856 | tf_op jit(solution)/shard_map/ppermute | solution.py:61
  49.2 14.2 %collective-permute-start.10 = (bf16[2,72,1920]{2,1,0:T(8,128)(2,1)}, bf16[2,72,1920]{2,1,0:T(8,128)(2,1)}, u32[]{:S(2)}, u32[]{:S(2)}) collective-permute-start(bf16[2,72,1920]{2,1,0:T(8,128)(2,1)} %pad_maximum_fusion.20), channel_id=1, source_target_pairs={{0,2},{1,3},{2,0},{3,1},{4,6},{5,7},{6,4},{7,5},{8,10},{9,11},{10,... | collective-permute-start | bytes 1658888 | tf_op jit(solution)/shard_map/ppermute | solution.py:61
  51.6 19.8 %collective-permute-start.13 = (bf16[3,72,1920]{2,1,0:T(8,128)(2,1)}, bf16[3,72,1920]{2,1,0:T(8,128)(2,1)}, u32[]{:S(2)}, u32[]{:S(2)}) collective-permute-start(bf16[3,72,1920]{2,1,0:T(8,128)(2,1)} %pad_maximum_fusion.13), channel_id=1, source_target_pairs={{0,4},{1,5},{2,6},{3,7},{4,0},{5,1},{6,2},{7,3},{8,12},{9,13},{10,... | collective-permute-start | bytes 2488328 | tf_op jit(solution)/shard_map/ppermute | solution.py:61
  53.2 20.7 %collective-permute-start.12 = (bf16[2,72,2816]{2,1,0:T(8,128)(2,1)S(1)}, bf16[2,72,2816]{2,1,0:T(8,128)(2,1)}, u32[]{:S(2)}, u32[]{:S(2)}) collective-permute-start(bf16[2,72,2816]{2,1,0:T(8,128)(2,1)S(1)} %pad_maximum_fusion.12.refs_1_), channel_id=1, source_target_pairs={{0,8},{1,9},{2,10},{3,11},{4,12},{5,13},{6,14},{7,15},{8,16},{9,17... | collective-permute-start | bytes 2433032 | tf_op jit(solution)/shard_map/ppermute | solution.py:61
  63.4 13.6 %collective-permute-start.11 = (bf16[2,72,1920]{2,1,0:T(8,128)(2,1)S(1)}, bf16[2,72,1920]{2,1,0:T(8,128)(2,1)S(1)}, u32[]{:S(2)}, u32[]{:S(2)}) collective-permute-start(bf16[2,72,1920]{2,1,0:T(8,128)(2,1)S(1)} %pad_maximum_fusion.21), channel_id=1, source_target_pairs={{0,2},{1,3},{2,0},{3,1},{4,6},{5,7},{6,4},{7,5},{8,10},{9,11},{10,... | collective-permute-start | bytes 1658888 | tf_op jit(solution)/shard_map/ppermute | solution.py:61
  73.9 13.0 %collective-permute-start.14 = (bf16[2,72,1280]{2,1,0:T(8,128)(2,1)S(1)}, bf16[2,72,1280]{2,1,0:T(8,128)(2,1)S(1)}, u32[]{:S(2)}, u32[]{:S(2)}) collective-permute-start(bf16[2,72,1280]{2,1,0:T(8,128)(2,1)S(1)} %slice.439), channel_id=1, source_target_pairs={{0,4},{1,5},{2,6},{3,7},{4,0},{5,1},{6,2},{7,3},{8,12},{9,13},{10,... | collective-permute-start | bytes 1105928 | tf_op jit(solution)/shard_map/ppermute | solution.py:61
  75.1 11.9 %collective-permute-start.16 = (bf16[4,72,640]{2,1,0:T(8,128)(2,1)S(1)}, bf16[4,72,640]{2,1,0:T(8,128)(2,1)S(1)}, u32[]{:S(2)}, u32[]{:S(2)}) collective-permute-start(bf16[4,72,640]{2,1,0:T(8,128)(2,1)S(1)} %pad_maximum_fusion.24), channel_id=1, source_target_pairs={{0,2},{1,3},{2,0},{3,1},{4,6},{5,7},{6,4},{7,5},{8,10},{9,11},{10,... | collective-permute-start | bytes 1105928 | tf_op jit(solution)/shard_map/ppermute | solution.py:61
  86.9 17.9 %collective-permute-start.17 = (bf16[2,72,2816]{2,1,0:T(8,128)(2,1)}, bf16[2,72,2816]{2,1,0:T(8,128)(2,1)}, u32[]{:S(2)}, u32[]{:S(2)}) collective-permute-start(bf16[2,72,2816]{2,1,0:T(8,128)(2,1)} %collective-permute-done.12.refs_6_), channel_id=1, source_target_pairs={{0,8},{1,9},{2,10},{3,11},{4,12},{5,13},{6,14},{7,15},{8,16},{9,17... | collective-permute-start | bytes 2433032 | tf_op jit(solution)/shard_map/ppermute | solution.py:61
  104.9 12.7 %collective-permute-start.20 = (bf16[72,1280]{1,0:T(8,128)(2,1)S(1)}, bf16[72,1280]{1,0:T(8,128)(2,1)S(1)}, u32[]{:S(2)}, u32[]{:S(2)}) collective-permute-start(bf16[72,1280]{1,0:T(8,128)(2,1)S(1)} %copy-done.104), channel_id=1, source_target_pairs={{0,2},{1,3},{2,0},{3,1},{4,6},{5,7},{6,4},{7,5},{8,10},{9,11},{10,... | collective-permute-start | bytes 552968 | tf_op jit(solution)/shard_map/ppermute | solution.py:61
  106.5 11.2 %collective-permute-start.21 = (bf16[72,896]{1,0:T(8,128)(2,1)S(1)}, bf16[72,896]{1,0:T(8,128)(2,1)S(1)}, u32[]{:S(2)}, u32[]{:S(2)}) collective-permute-start(bf16[72,896]{1,0:T(8,128)(2,1)S(1)} %copy-done.105), channel_id=1, source_target_pairs={{0,4},{1,5},{2,6},{3,7},{4,0},{5,1},{6,2},{7,3},{8,12},{9,13},{10,... | collective-permute-start | bytes 387080 | tf_op jit(solution)/shard_map/ppermute | solution.py:61
  115.3 10.8 %collective-permute-start.18 = (bf16[2,72,1664]{2,1,0:T(8,128)(2,1)S(1)}, bf16[2,72,1664]{2,1,0:T(8,128)(2,1)S(1)}, u32[]{:S(2)}, u32[]{:S(2)}) collective-permute-start(bf16[2,72,1664]{2,1,0:T(8,128)(2,1)S(1)} %copy-done.92), channel_id=1, source_target_pairs={{0,4},{1,5},{2,6},{3,7},{4,0},{5,1},{6,2},{7,3},{8,12},{9,13},{10,... | collective-permute-start | bytes 1437704 | tf_op jit(solution)/shard_map/ppermute | solution.py:61
  117.4 22.8 %collective-permute-start.22 = (bf16[2,72,2816]{2,1,0:T(8,128)(2,1)}, bf16[2,72,2816]{2,1,0:T(8,128)(2,1)S(1)}, u32[]{:S(2)}, u32[]{:S(2)}) collective-permute-start(bf16[2,72,2816]{2,1,0:T(8,128)(2,1)} %collective-permute-done.17.refs_7_), channel_id=1, source_target_pairs={{0,8},{1,9},{2,10},{3,11},{4,12},{5,13},{6,14},{7,15},{8,16},{9,17... | collective-permute-start | bytes 2433032 | tf_op jit(solution)/shard_map/ppermute | solution.py:61
  128.3 11.9 %collective-permute-start.23 = (bf16[1,2,72,1664]{3,2,1,0:T(8,128)(2,1)S(1)}, bf16[1,2,72,1664]{3,2,1,0:T(8,128)(2,1)S(1)}, u32[]{:S(2)}, u32[]{:S(2)}) collective-permute-start(bf16[1,2,72,1664]{3,2,1,0:T(8,128)(2,1)S(1)} %slice_bitcast_fusion.2), channel_id=1, source_target_pairs={{0,4},{1,5},{2,6},{3,7},{4,0},{5,1},{6,2},{7,3},{8,12},{9,13},{10,... | collective-permute-start | bytes 1437704 | tf_op jit(solution)/shard_map/ppermute | solution.py:61
  143.6 12.5 %collective-permute-start.25 = (bf16[1,2,72,1664]{3,2,1,0:T(8,128)(2,1)S(1)}, bf16[1,2,72,1664]{3,2,1,0:T(8,128)(2,1)S(1)}, u32[]{:S(2)}, u32[]{:S(2)}) collective-permute-start(bf16[1,2,72,1664]{3,2,1,0:T(8,128)(2,1)S(1)} %slice_bitcast_fusion.1), channel_id=1, source_target_pairs={{0,4},{1,5},{2,6},{3,7},{4,0},{5,1},{6,2},{7,3},{8,12},{9,13},{10,... | collective-permute-start | bytes 1437704 | tf_op jit(solution)/shard_map/ppermute | solution.py:61
  143.9 12.2 %collective-permute-start.27 = (bf16[2,72,2176]{2,1,0:T(8,128)(2,1)S(1)}, bf16[2,72,2176]{2,1,0:T(8,128)(2,1)S(1)}, u32[]{:S(2)}, u32[]{:S(2)}) collective-permute-start(bf16[2,72,2176]{2,1,0:T(8,128)(2,1)S(1)} %pad_maximum_fusion.15.refs_1_), channel_id=1, source_target_pairs={{0,8},{1,9},{2,10},{3,11},{4,12},{5,13},{6,14},{7,15},{8,16},{9,17... | collective-permute-start | bytes 1880072 | tf_op jit(solution)/shard_map/ppermute | solution.py:61
  144.6 11.4 %collective-permute-start.26 = (bf16[1,2,72,1152]{3,2,1,0:T(8,128)(2,1)S(1)}, bf16[1,2,72,1152]{3,2,1,0:T(8,128)(2,1)S(1)}, u32[]{:S(2)}, u32[]{:S(2)}) collective-permute-start(bf16[1,2,72,1152]{3,2,1,0:T(8,128)(2,1)S(1)} %slice_bitcast_fusion.7), channel_id=1, source_target_pairs={{0,2},{1,3},{2,0},{3,1},{4,6},{5,7},{6,4},{7,5},{8,10},{9,11},{10,... | collective-permute-start | bytes 995336 | tf_op jit(solution)/shard_map/ppermute | solution.py:61
  159.4 13.8 %collective-permute-start.29 = (bf16[1,2,72,1664]{3,2,1,0:T(8,128)(2,1)}, bf16[1,2,72,1664]{3,2,1,0:T(8,128)(2,1)S(1)}, u32[]{:S(2)}, u32[]{:S(2)}) collective-permute-start(bf16[1,2,72,1664]{3,2,1,0:T(8,128)(2,1)} %slice_bitcast_fusion), channel_id=1, source_target_pairs={{0,4},{1,5},{2,6},{3,7},{4,0},{5,1},{6,2},{7,3},{8,12},{9,13},{10,... | collective-permute-start | bytes 1437704 | tf_op jit(solution)/shard_map/ppermute | solution.py:61
  163.0 28.9 %collective-permute-start.33 = (bf16[2,72,2176]{2,1,0:T(8,128)(2,1)S(1)}, bf16[2,72,2176]{2,1,0:T(8,128)(2,1)}, u32[]{:S(2)}, u32[]{:S(2)}) collective-permute-start(bf16[2,72,2176]{2,1,0:T(8,128)(2,1)S(1)} %collective-permute-done.27.refs_8_), channel_id=1, source_target_pairs={{0,8},{1,9},{2,10},{3,11},{4,12},{5,13},{6,14},{7,15},{8,16},{9,17... | collective-permute-start | bytes 1880072 | tf_op jit(solution)/shard_map/ppermute | solution.py:61
  174.0 17.9 %collective-permute-start.32 = (bf16[1,256,1152]{2,1,0:T(8,128)(2,1)}, bf16[1,256,1152]{2,1,0:T(8,128)(2,1)}, u32[]{:S(2)}, u32[]{:S(2)}) collective-permute-start(bf16[1,256,1152]{2,1,0:T(8,128)(2,1)} %dynamic-slice_bitcast_fusion.11), channel_id=1, source_target_pairs={{0,2},{1,3},{2,0},{3,1},{4,6},{5,7},{6,4},{7,5},{8,10},{9,11},{10,... | collective-permute-start | bytes 1769480 | tf_op jit(solution)/shard_map/ppermute | solution.py:61
  175.8 16.2 %collective-permute-start.31 = (bf16[2,72,1280]{2,1,0:T(8,128)(2,1)}, bf16[2,72,1280]{2,1,0:T(8,128)(2,1)S(1)}, u32[]{:S(2)}, u32[]{:S(2)}) collective-permute-start(bf16[2,72,1280]{2,1,0:T(8,128)(2,1)} %fusion.47), channel_id=1, source_target_pairs={{0,4},{1,5},{2,6},{3,7},{4,0},{5,1},{6,2},{7,3},{8,12},{9,13},{10,... | collective-permute-start | bytes 1105928 | tf_op jit(solution)/shard_map/ppermute | solution.py:61
  196.3 19.5 %collective-permute-start.35 = (bf16[2,72,2176]{2,1,0:T(8,128)(2,1)}, bf16[2,72,2176]{2,1,0:T(8,128)(2,1)}, u32[]{:S(2)}, u32[]{:S(2)}) collective-permute-start(bf16[2,72,2176]{2,1,0:T(8,128)(2,1)} %collective-permute-done.33.refs_9_), channel_id=1, source_target_pairs={{0,8},{1,9},{2,10},{3,11},{4,12},{5,13},{6,14},{7,15},{8,16},{9,17... | collective-permute-start | bytes 1880072 | tf_op jit(solution)/shard_map/ppermute | solution.py:61
  196.6 19.3 %collective-permute-start.36 = (bf16[2,2,72,1280]{3,2,1,0:T(8,128)(2,1)}, bf16[2,2,72,1280]{3,2,1,0:T(8,128)(2,1)}, u32[]{:S(2)}, u32[]{:S(2)}) collective-permute-start(bf16[2,2,72,1280]{3,2,1,0:T(8,128)(2,1)} %pad_maximum_fusion.16), channel_id=1, source_target_pairs={{0,4},{1,5},{2,6},{3,7},{4,0},{5,1},{6,2},{7,3},{8,12},{9,13},{10,... | collective-permute-start | bytes 2211848 | tf_op jit(solution)/shard_map/ppermute | solution.py:61
  198.3 13.8 %collective-permute-start.37 = (bf16[2,72,896]{2,1,0:T(8,128)(2,1)}, bf16[2,72,896]{2,1,0:T(8,128)(2,1)S(1)}, u32[]{:S(2)}, u32[]{:S(2)}) collective-permute-start(bf16[2,72,896]{2,1,0:T(8,128)(2,1)} %fusion.62), channel_id=1, source_target_pairs={{0,2},{1,3},{2,0},{3,1},{4,6},{5,7},{6,4},{7,5},{8,10},{9,11},{10,... | collective-permute-start | bytes 774152 | tf_op jit(solution)/shard_map/ppermute | solution.py:61
  217.8 17.9 %collective-permute-start.39 = (bf16[2,2,72,896]{3,2,1,0:T(8,128)(2,1)S(1)}, bf16[2,2,72,896]{3,2,1,0:T(8,128)(2,1)S(1)}, u32[]{:S(2)}, u32[]{:S(2)}) collective-permute-start(bf16[2,2,72,896]{3,2,1,0:T(8,128)(2,1)S(1)} %copy-done.91), channel_id=1, source_target_pairs={{0,2},{1,3},{2,0},{3,1},{4,6},{5,7},{6,4},{7,5},{8,10},{9,11},{10,... | collective-permute-start | bytes 1548296 | tf_op jit(solution)/shard_map/ppermute | solution.py:61
  218.3 18.3 %collective-permute-start.40 = (bf16[1,2,72,1280]{3,2,1,0:T(8,128)(2,1)S(1)}, bf16[1,2,72,1280]{3,2,1,0:T(8,128)(2,1)S(1)}, u32[]{:S(2)}, u32[]{:S(2)}) collective-permute-start(bf16[1,2,72,1280]{3,2,1,0:T(8,128)(2,1)S(1)} %slice_bitcast_fusion.3), channel_id=1, source_target_pairs={{0,4},{1,5},{2,6},{3,7},{4,0},{5,1},{6,2},{7,3},{8,12},{9,13},{10,... | collective-permute-start | bytes 1105928 | tf_op jit(solution)/shard_map/ppermute | solution.py:61
  219.1 18.5 %collective-permute-start.41 = (bf16[1,2,72,896]{3,2,1,0:T(8,128)(2,1)S(1)}, bf16[1,2,72,896]{3,2,1,0:T(8,128)(2,1)S(1)}, u32[]{:S(2)}, u32[]{:S(2)}) collective-permute-start(bf16[1,2,72,896]{3,2,1,0:T(8,128)(2,1)S(1)} %slice_bitcast_fusion.9), channel_id=1, source_target_pairs={{0,2},{1,3},{2,0},{3,1},{4,6},{5,7},{6,4},{7,5},{8,10},{9,11},{10,... | collective-permute-start | bytes 774152 | tf_op jit(solution)/shard_map/ppermute | solution.py:61
  256.1 11.4 %collective-permute-start.43 = (bf16[1,2,72,896]{3,2,1,0:T(8,128)(2,1)S(1)}, bf16[1,2,72,896]{3,2,1,0:T(8,128)(2,1)S(1)}, u32[]{:S(2)}, u32[]{:S(2)}) collective-permute-start(bf16[1,2,72,896]{3,2,1,0:T(8,128)(2,1)S(1)} %get-tuple-element.1077), channel_id=1, source_target_pairs={{0,2},{1,3},{2,0},{3,1},{4,6},{5,7},{6,4},{7,5},{8,10},{9,11},{10,... | collective-permute-start | bytes 774152 | tf_op jit(solution)/shard_map/ppermute | solution.py:61
  256.8 10.7 %collective-permute-start.44 = (bf16[1,2,72,1280]{3,2,1,0:T(8,128)(2,1)S(1)}, bf16[1,2,72,1280]{3,2,1,0:T(8,128)(2,1)S(1)}, u32[]{:S(2)}, u32[]{:S(2)}) collective-permute-start(bf16[1,2,72,1280]{3,2,1,0:T(8,128)(2,1)S(1)} %get-tuple-element.1079), channel_id=1, source_target_pairs={{0,4},{1,5},{2,6},{3,7},{4,0},{5,1},{6,2},{7,3},{8,12},{9,13},{10,... | collective-permute-start | bytes 1105928 | tf_op jit(solution)/shard_map/ppermute | solution.py:61
  271.8 11.0 %collective-permute-start.45 = (bf16[1,2,72,896]{3,2,1,0:T(8,128)(2,1)S(1)}, bf16[1,2,72,896]{3,2,1,0:T(8,128)(2,1)S(1)}, u32[]{:S(2)}, u32[]{:S(2)}) collective-permute-start(bf16[1,2,72,896]{3,2,1,0:T(8,128)(2,1)S(1)} %get-tuple-element.1091), channel_id=1, source_target_pairs={{0,2},{1,3},{2,0},{3,1},{4,6},{5,7},{6,4},{7,5},{8,10},{9,11},{10,... | collective-permute-start | bytes 774152 | tf_op jit(solution)/shard_map/ppermute | solution.py:61
  283.8 11.3 %collective-permute-start.48 = (bf16[1,2,72,896]{3,2,1,0:T(8,128)(2,1)S(1)}, bf16[1,2,72,896]{3,2,1,0:T(8,128)(2,1)S(1)}, u32[]{:S(2)}, u32[]{:S(2)}) collective-permute-start(bf16[1,2,72,896]{3,2,1,0:T(8,128)(2,1)S(1)} %copy-done.103), channel_id=1, source_target_pairs={{0,2},{1,3},{2,0},{3,1},{4,6},{5,7},{6,4},{7,5},{8,10},{9,11},{10,... | collective-permute-start | bytes 774152 | tf_op jit(solution)/shard_map/ppermute | solution.py:61
  284.5 10.7 %collective-permute-start.49 = (bf16[1,2,72,1280]{3,2,1,0:T(8,128)(2,1)S(1)}, bf16[1,2,72,1280]{3,2,1,0:T(8,128)(2,1)S(1)}, u32[]{:S(2)}, u32[]{:S(2)}) collective-permute-start(bf16[1,2,72,1280]{3,2,1,0:T(8,128)(2,1)S(1)} %get-tuple-element.1105), channel_id=1, source_target_pairs={{0,4},{1,5},{2,6},{3,7},{4,0},{5,1},{6,2},{7,3},{8,12},{9,13},{10,... | collective-permute-start | bytes 1105928 | tf_op jit(solution)/shard_map/ppermute | solution.py:61
  309.9 15.1 %collective-permute-start.53 = (bf16[1152,640]{1,0:T(8,128)(2,1)}, bf16[1152,640]{1,0:T(8,128)(2,1)}, u32[]{:S(2)}, u32[]{:S(2)}) collective-permute-start(bf16[1152,640]{1,0:T(8,128)(2,1)} %pad_maximum_fusion.6), channel_id=1, source_target_pairs={{0,1},{1,0},{2,3},{3,2},{4,5},{5,4},{6,7},{7,6},{8,9},{9,8},{10,11... | collective-permute-start | bytes 4423688 | tf_op jit(solution)/shard_map/ppermute | solution.py:61
  319.0 18.9 %collective-permute-start.54 = (bf16[2,72,2176]{2,1,0:T(8,128)(2,1)}, bf16[2,72,2176]{2,1,0:T(8,128)(2,1)}, u32[]{:S(2)}, u32[]{:S(2)}) collective-permute-start(bf16[2,72,2176]{2,1,0:T(8,128)(2,1)} %fusion.34), channel_id=1, source_target_pairs={{0,8},{1,9},{2,10},{3,11},{4,12},{5,13},{6,14},{7,15},{8,16},{9,17... | collective-permute-start | bytes 1880072 | tf_op jit(solution)/shard_map/ppermute | solution.py:61
  319.0 25.3 %collective-permute-start.55 = (bf16[2,2,72,512]{3,2,1,0:T(8,128)(2,1)}, bf16[2,2,72,512]{3,2,1,0:T(8,128)(2,1)}, u32[]{:S(2)}, u32[]{:S(2)}) collective-permute-start(bf16[2,2,72,512]{3,2,1,0:T(8,128)(2,1)} %get-tuple-element.1189), channel_id=1, source_target_pairs={{0,2},{1,3},{2,0},{3,1},{4,6},{5,7},{6,4},{7,5},{8,10},{9,11},{10,... | collective-permute-start | bytes 884744 | tf_op jit(solution)/shard_map/ppermute | solution.py:61
  320.6 23.7 %collective-permute-start.56 = (bf16[2,2,72,1664]{3,2,1,0:T(8,128)(2,1)}, bf16[2,2,72,1664]{3,2,1,0:T(8,128)(2,1)}, u32[]{:S(2)}, u32[]{:S(2)}) collective-permute-start(bf16[2,2,72,1664]{3,2,1,0:T(8,128)(2,1)} %get-tuple-element.1191), channel_id=1, source_target_pairs={{0,4},{1,5},{2,6},{3,7},{4,0},{5,1},{6,2},{7,3},{8,12},{9,13},{10,... | collective-permute-start | bytes 2875400 | tf_op jit(solution)/shard_map/ppermute | solution.py:61
  345.5 23.5 %collective-permute-start.57 = (bf16[2,2,72,1664]{3,2,1,0:T(8,128)(2,1)S(1)}, bf16[2,2,72,1664]{3,2,1,0:T(8,128)(2,1)S(1)}, u32[]{:S(2)}, u32[]{:S(2)}) collective-permute-start(bf16[2,2,72,1664]{3,2,1,0:T(8,128)(2,1)S(1)} %copy-done.82), channel_id=1, source_target_pairs={{0,4},{1,5},{2,6},{3,7},{4,0},{5,1},{6,2},{7,3},{8,12},{9,13},{10,... | collective-permute-start | bytes 2875400 | tf_op jit(solution)/shard_map/ppermute | solution.py:61
  346.3 23.9 %collective-permute-start.60 = (bf16[4,2,72,640]{3,2,1,0:T(8,128)(2,1)S(1)}, bf16[4,2,72,640]{3,2,1,0:T(8,128)(2,1)S(1)}, u32[]{:S(2)}, u32[]{:S(2)}) collective-permute-start(bf16[4,2,72,640]{3,2,1,0:T(8,128)(2,1)S(1)} %dynamic-slice_bitcast_fusion.6), channel_id=1, source_target_pairs={{0,2},{1,3},{2,0},{3,1},{4,6},{5,7},{6,4},{7,5},{8,10},{9,11},{10,... | collective-permute-start | bytes 2211848 | tf_op jit(solution)/shard_map/ppermute | solution.py:61
  347.1 22.0 %collective-permute-start.58 = (bf16[2,72,2176]{2,1,0:T(8,128)(2,1)S(1)}, bf16[2,72,2176]{2,1,0:T(8,128)(2,1)S(1)}, u32[]{:S(2)}, u32[]{:S(2)}) collective-permute-start(bf16[2,72,2176]{2,1,0:T(8,128)(2,1)S(1)} %fusion.26), channel_id=1, source_target_pairs={{0,8},{1,9},{2,10},{3,11},{4,12},{5,13},{6,14},{7,15},{8,16},{9,17... | collective-permute-start | bytes 1880072 | tf_op jit(solution)/shard_map/ppermute | solution.py:61
  351.5 18.8 %collective-permute-start.59 = (bf16[2,2,72,512]{3,2,1,0:T(8,128)(2,1)S(1)}, bf16[2,2,72,512]{3,2,1,0:T(8,128)(2,1)S(1)}, u32[]{:S(2)}, u32[]{:S(2)}) collective-permute-start(bf16[2,2,72,512]{3,2,1,0:T(8,128)(2,1)S(1)} %get-tuple-element.1215), channel_id=1, source_target_pairs={{0,2},{1,3},{2,0},{3,1},{4,6},{5,7},{6,4},{7,5},{8,10},{9,11},{10,... | collective-permute-start | bytes 884744 | tf_op jit(solution)/shard_map/ppermute | solution.py:61
  375.7 21.3 %collective-permute-start.62 = (bf16[2,72,2176]{2,1,0:T(8,128)(2,1)S(1)}, bf16[2,72,2176]{2,1,0:T(8,128)(2,1)S(1)}, u32[]{:S(2)}, u32[]{:S(2)}) collective-permute-start(bf16[2,72,2176]{2,1,0:T(8,128)(2,1)S(1)} %fusion.25), channel_id=1, source_target_pairs={{0,8},{1,9},{2,10},{3,11},{4,12},{5,13},{6,14},{7,15},{8,16},{9,17... | collective-permute-start | bytes 1880072 | tf_op jit(solution)/shard_map/ppermute | solution.py:61
  395.4 19.4 %collective-permute-start.61 = (bf16[2,72,2816]{2,1,0:T(8,128)(2,1)S(1)}, bf16[2,72,2816]{2,1,0:T(8,128)(2,1)S(1)}, u32[]{:S(2)}, u32[]{:S(2)}) collective-permute-start(bf16[2,72,2816]{2,1,0:T(8,128)(2,1)S(1)} %dynamic-slice_bitcast_fusion.5), channel_id=1, source_target_pairs={{0,8},{1,9},{2,10},{3,11},{4,12},{5,13},{6,14},{7,15},{8,16},{9,17... | collective-permute-start | bytes 2433032 | tf_op jit(solution)/shard_map/ppermute | solution.py:61
  408.1 13.2 %collective-permute-start.63 = (bf16[512,1152]{1,0:T(8,128)(2,1)S(1)}, bf16[512,1152]{1,0:T(8,128)(2,1)S(1)}, u32[]{:S(2)}, u32[]{:S(2)}) collective-permute-start(bf16[512,1152]{1,0:T(8,128)(2,1)S(1)} %convolution_convert_fusion.6), channel_id=1, source_target_pairs={{0,1},{1,0},{2,3},{3,2},{4,5},{5,4},{6,7},{7,6},{8,9},{9,8},{10,11... | collective-permute-start | bytes 3538952 | tf_op jit(solution)/shard_map/ppermute | solution.py:61
  408.2 12.0 %collective-permute-start.64 = (bf16[72,1280]{1,0:T(8,128)(2,1)S(1)}, bf16[72,1280]{1,0:T(8,128)(2,1)S(1)}, u32[]{:S(2)}, u32[]{:S(2)}) collective-permute-start(bf16[72,1280]{1,0:T(8,128)(2,1)S(1)} %fusion.64), channel_id=1, source_target_pairs={{0,2},{1,3},{2,0},{3,1},{4,6},{5,7},{6,4},{7,5},{8,10},{9,11},{10,... | collective-permute-start | bytes 552968 | tf_op jit(solution)/shard_map/ppermute | solution.py:61
  409.0 11.2 %collective-permute-start.65 = (bf16[72,896]{1,0:T(8,128)(2,1)S(1)}, bf16[72,896]{1,0:T(8,128)(2,1)S(1)}, u32[]{:S(2)}, u32[]{:S(2)}) collective-permute-start(bf16[72,896]{1,0:T(8,128)(2,1)S(1)} %fusion.70), channel_id=1, source_target_pairs={{0,4},{1,5},{2,6},{3,7},{4,0},{5,1},{6,2},{7,3},{8,12},{9,13},{10,... | collective-permute-start | bytes 387080 | tf_op jit(solution)/shard_map/ppermute | solution.py:61
  410.3 29.5 %collective-permute-start.67 = (bf16[4,2,72,896]{3,2,1,0:T(8,128)(2,1)S(1)}, bf16[4,2,72,896]{3,2,1,0:T(8,128)(2,1)S(1)}, u32[]{:S(2)}, u32[]{:S(2)}) collective-permute-start(bf16[4,2,72,896]{3,2,1,0:T(8,128)(2,1)S(1)} %dynamic-slice_bitcast_fusion.2), channel_id=1, source_target_pairs={{0,2},{1,3},{2,0},{3,1},{4,6},{5,7},{6,4},{7,5},{8,10},{9,11},{10,... | collective-permute-start | bytes 3096584 | tf_op jit(solution)/shard_map/ppermute | solution.py:61
  414.8 25.0 %collective-permute-start.68 = (bf16[4,2,72,1024]{3,2,1,0:T(8,128)(2,1)S(1)}, bf16[4,2,72,1024]{3,2,1,0:T(8,128)(2,1)S(1)}, u32[]{:S(2)}, u32[]{:S(2)}) collective-permute-start(bf16[4,2,72,1024]{3,2,1,0:T(8,128)(2,1)S(1)} %dynamic-slice_bitcast_fusion.1), channel_id=1, source_target_pairs={{0,4},{1,5},{2,6},{3,7},{4,0},{5,1},{6,2},{7,3},{8,12},{9,13},{10,... | collective-permute-start | bytes 3538952 | tf_op jit(solution)/shard_map/ppermute | solution.py:61
  421.2 19.4 %collective-permute-start.66 = (bf16[2,72,2816]{2,1,0:T(8,128)(2,1)}, bf16[2,72,2816]{2,1,0:T(8,128)(2,1)}, u32[]{:S(2)}, u32[]{:S(2)}) collective-permute-start(bf16[2,72,2816]{2,1,0:T(8,128)(2,1)} %fusion.20), channel_id=1, source_target_pairs={{0,8},{1,9},{2,10},{3,11},{4,12},{5,13},{6,14},{7,15},{8,16},{9,17... | collective-permute-start | bytes 2433032 | tf_op jit(solution)/shard_map/ppermute | solution.py:61
  421.2 28.8 %collective-permute-start.70 = (f32[36,2176]{1,0:T(8,128)}, f32[36,2176]{1,0:T(8,128)}, u32[]{:S(2)}, u32[]{:S(2)}) collective-permute-start(f32[36,2176]{1,0:T(8,128)} %get-tuple-element.1320), channel_id=1, source_target_pairs={{0,1},{1,0},{2,3},{3,2},{4,5},{5,4},{6,7},{7,6},{8,9},{9,8},{10,11... | collective-permute-start | bytes 940040 | tf_op jit(solution)/shard_map/ppermute | solution.py:61
  444.4 10.8 %collective-permute-start.69 = (bf16[512,1152]{1,0:T(8,128)(2,1)S(1)}, bf16[512,1152]{1,0:T(8,128)(2,1)}, u32[]{:S(2)}, u32[]{:S(2)}) collective-permute-start(bf16[512,1152]{1,0:T(8,128)(2,1)S(1)} %copy-done.108), channel_id=1, source_target_pairs={{0,1},{1,0},{2,3},{3,2},{4,5},{5,4},{6,7},{7,6},{8,9},{9,8},{10,11... | collective-permute-start | bytes 3538952 | tf_op jit(solution)/shard_map/ppermute | solution.py:61
  450.0 16.0 %collective-permute-start.71 = (bf16[4,72,1024]{2,1,0:T(8,128)(2,1)}, bf16[4,72,1024]{2,1,0:T(8,128)(2,1)}, u32[]{:S(2)}, u32[]{:S(2)}) collective-permute-start(bf16[4,72,1024]{2,1,0:T(8,128)(2,1)} %get-tuple-element.1345), channel_id=1, source_target_pairs={{0,2},{1,3},{2,0},{3,1},{4,6},{5,7},{6,4},{7,5},{8,10},{9,11},{10,... | collective-permute-start | bytes 1769480 | tf_op jit(solution)/shard_map/ppermute | solution.py:61
  451.5 14.6 %collective-permute-start.73 = (bf16[4,72,896]{2,1,0:T(8,128)(2,1)}, bf16[4,72,896]{2,1,0:T(8,128)(2,1)}, u32[]{:S(2)}, u32[]{:S(2)}) collective-permute-start(bf16[4,72,896]{2,1,0:T(8,128)(2,1)} %get-tuple-element.1351), channel_id=1, source_target_pairs={{0,4},{1,5},{2,6},{3,7},{4,0},{5,1},{6,2},{7,3},{8,12},{9,13},{10,... | collective-permute-start | bytes 1548296 | tf_op jit(solution)/shard_map/ppermute | solution.py:61
  452.8 22.1 %collective-permute-start.75 = (bf16[2,72,2816]{2,1,0:T(8,128)(2,1)}, bf16[2,72,2816]{2,1,0:T(8,128)(2,1)}, u32[]{:S(2)}, u32[]{:S(2)}) collective-permute-start(bf16[2,72,2816]{2,1,0:T(8,128)(2,1)} %fusion.19), channel_id=1, source_target_pairs={{0,8},{1,9},{2,10},{3,11},{4,12},{5,13},{6,14},{7,15},{8,16},{9,17... | collective-permute-start | bytes 2433032 | tf_op jit(solution)/shard_map/ppermute | solution.py:61
  475.0 16.3 %collective-permute-start.80 = (bf16[1,256,1152]{2,1,0:T(8,128)(2,1)S(1)}, bf16[1,256,1152]{2,1,0:T(8,128)(2,1)S(1)}, u32[]{:S(2)}, u32[]{:S(2)}) collective-permute-start(bf16[1,256,1152]{2,1,0:T(8,128)(2,1)S(1)} %copy-done.88), channel_id=1, source_target_pairs={{0,2},{1,3},{2,0},{3,1},{4,6},{5,7},{6,4},{7,5},{8,10},{9,11},{10,... | collective-permute-start | bytes 1769480 | tf_op jit(solution)/shard_map/ppermute | solution.py:61
  477.7 18.7 %collective-permute-start.78 = (bf16[72,1664]{1,0:T(8,128)(2,1)S(1)}, bf16[72,1664]{1,0:T(8,128)(2,1)S(1)}, u32[]{:S(2)}, u32[]{:S(2)}) collective-permute-start(bf16[72,1664]{1,0:T(8,128)(2,1)S(1)} %fusion.63), channel_id=1, source_target_pairs={{0,2},{1,3},{2,0},{3,1},{4,6},{5,7},{6,4},{7,5},{8,10},{9,11},{10,... | collective-permute-start | bytes 718856 | tf_op jit(solution)/shard_map/ppermute | solution.py:61
  479.0 13.0 %collective-permute-start.79 = (f32[112,128]{1,0:T(8,128)S(1)}, f32[112,128]{1,0:T(8,128)S(1)}, u32[]{:S(2)}, u32[]{:S(2)}) collective-permute-start(f32[112,128]{1,0:T(8,128)S(1)} %add.515), channel_id=1, source_target_pairs={{0,4},{1,5},{2,6},{3,7},{4,0},{5,1},{6,2},{7,3},{8,12},{9,13},{10,... | collective-permute-start | bytes 172040 | tf_op jit(solution)/shard_map/ppermute | solution.py:61
  479.6 16.7 %collective-permute-start.81 = (bf16[72,1152]{1,0:T(8,128)(2,1)S(1)}, bf16[72,1152]{1,0:T(8,128)(2,1)S(1)}, u32[]{:S(2)}, u32[]{:S(2)}) collective-permute-start(bf16[72,1152]{1,0:T(8,128)(2,1)S(1)} %fusion.65), channel_id=1, source_target_pairs={{0,4},{1,5},{2,6},{3,7},{4,0},{5,1},{6,2},{7,3},{8,12},{9,13},{10,... | collective-permute-start | bytes 497672 | tf_op jit(solution)/shard_map/ppermute | solution.py:61
  481.1 15.3 %collective-permute-start.82 = (bf16[72,1920]{1,0:T(8,128)(2,1)S(1)}, bf16[72,1920]{1,0:T(8,128)(2,1)S(1)}, u32[]{:S(2)}, u32[]{:S(2)}) collective-permute-start(bf16[72,1920]{1,0:T(8,128)(2,1)S(1)} %fusion.41), channel_id=1, source_target_pairs={{0,8},{1,9},{2,10},{3,11},{4,12},{5,13},{6,14},{7,15},{8,16},{9,17... | collective-permute-start | bytes 829448 | tf_op jit(solution)/shard_map/ppermute | solution.py:61
  491.2 15.9 %collective-permute-start.77 = (bf16[1,256,1152]{2,1,0:T(8,128)(2,1)S(1)}, bf16[1,256,1152]{2,1,0:T(8,128)(2,1)S(1)}, u32[]{:S(2)}, u32[]{:S(2)}) collective-permute-start(bf16[1,256,1152]{2,1,0:T(8,128)(2,1)S(1)} %get-tuple-element.1384), channel_id=1, source_target_pairs={{0,2},{1,3},{2,0},{3,1},{4,6},{5,7},{6,4},{7,5},{8,10},{9,11},{10,... | collective-permute-start | bytes 1769480 | tf_op jit(solution)/shard_map/ppermute | solution.py:61
  496.7 12.5 %collective-permute-start.85 = (f32[36,2816]{1,0:T(8,128)S(1)}, f32[36,2816]{1,0:T(8,128)S(1)}, u32[]{:S(2)}, u32[]{:S(2)}) collective-permute-start(f32[36,2816]{1,0:T(8,128)S(1)} %get-tuple-element.1424), channel_id=1, source_target_pairs={{0,1},{1,0},{2,3},{3,2},{4,5},{5,4},{6,7},{7,6},{8,9},{9,8},{10,11... | collective-permute-start | bytes 1216520 | tf_op jit(solution)/shard_map/ppermute | solution.py:61
  496.8 11.0 %collective-permute-start.86 = (bf16[72,1920]{1,0:T(8,128)(2,1)S(1)}, bf16[72,1920]{1,0:T(8,128)(2,1)S(1)}, u32[]{:S(2)}, u32[]{:S(2)}) collective-permute-start(bf16[72,1920]{1,0:T(8,128)(2,1)S(1)} %fusion.40), channel_id=1, source_target_pairs={{0,8},{1,9},{2,10},{3,11},{4,12},{5,13},{6,14},{7,15},{8,16},{9,17... | collective-permute-start | bytes 829448 | tf_op jit(solution)/shard_map/ppermute | solution.py:61
  (148 other events, 1017.6 us)

commit v3 on v2

--- a/solution.py
+++ b/solution.py
@@ -351,6 +351,7 @@
 
 
 CHUNK = 512
+CHUNK_FORWARD = 1024
 
 
 def window(h, wide):
@@ -380,16 +381,16 @@
         k = qkv_ref[:, pl.ds(start + wide, WIN)]
         k = jnp.where(inside, k, jnp.where(feature, kf_ref[...], zero))
         v_t = jnp.where(inside, qkv_ref[:, pl.ds(start + 2 * wide, WIN)], zero).T
-        for i in range(n // CHUNK):
-            rows = slice(i * CHUNK, (i + 1) * CHUNK)
-            q = jnp.where(feature[:CHUNK], qf_ref[rows, :], qkv_ref[rows, at])
+        for i in range(n // CHUNK_FORWARD):
+            rows = slice(i * CHUNK_FORWARD, (i + 1) * CHUNK_FORWARD)
+            q = jnp.where(feature[:CHUNK_FORWARD], qf_ref[rows, :], qkv_ref[rows, at])
             s = lax.dot_general(k, q, NT, preferred_element_type=f32)
             top = jnp.max(s, axis=0, keepdims=True) * scale
             p = jnp.exp2(s * scale - top)
             total = jnp.sum(p, axis=0, keepdims=True)
             o_t = lax.dot_general(v_t, p.astype(bf16), NN, preferred_element_type=f32)
             out = (o_t / total).T.astype(bf16)
-            out_ref[rows, at] = jnp.where(inside[:CHUNK], out, out_ref[rows, at])
+            out_ref[rows, at] = jnp.where(inside[:CHUNK_FORWARD], out, out_ref[rows, at])
             lse_ref[pl.ds(h, 1), rows] = top + jnp.log2(total)
         return carry
 
@@ -482,9 +483,10 @@
 def out_norm_kernel(
     core_ref, x_ref, a_ref, b_ref, w_ref, v_ref, bias_ref, gain_ref, shift_ref, res_ref, norm_ref
 ):
-    half, cut = a_ref.shape[1], w_ref.shape[1]
+    cut = w_ref.shape[1]
     width = x_ref.shape[1]
-    a, b = a_ref[...], b_ref[...]
+    half = width // 2
+    a, b = a_ref[:, :half], b_ref[:, :half]
     mine = dot(a, w_ref[:half, :]) + dot(b, w_ref[half:, :])
     theirs = dot(a, v_ref[half:, :]) + dot(b, v_ref[:half, :])
     first = core_ref[0] == 0
@@ -719,7 +721,7 @@
     spot = jnp.arange(chip_rows, dtype=jnp.int32)
     spot = flip(at.c, spot // own_rows) * own_rows + spot % own_rows
     turn = (jnp.arange(chip_rows, dtype=jnp.int32)[:, None] == spot[None, :]).astype(bf16)
-    s_cut, u_cut, d_cut = 10 * LANE, 13 * LANE, 10 * LANE
+    u_cut, d_cut = 13 * LANE, 10 * LANE
     s_wide, u_wide, d_wide = 3 * wide, out_cut + half_width, half_width
     s_pieces = Pieces(at, chip_rows, s_wide)
     u_pieces = Pieces(at, chip_rows, u_wide)
@@ -754,12 +756,19 @@
             + [((a,), cut, (k, 0, a), cut, cols - cut) for a in range(2)],
         )
 
+    def indices(ks, array):
+        return [((a,) if array.ndim == 3 else (i, a), k, a) for i, k in enumerate(ks) for a in (0, 1)]
+
+    def add_low(pieces, ks, low, cut):
+        pieces.add(low, [(i, 0, (k, a, 1), 0, cut) for i, k, a in indices(ks, low)])
+
+    def add_high(pieces, ks, high, cut):
+        wide = pieces.cols - cut
+        pieces.add(high, [(i, 0, (k, 1, a), cut, wide) for i, k, a in indices(ks, high)])
+
     def add_across(pieces, ks, low, high, cut):
-        cols = pieces.cols
-        index = lambda i, a: (a,) if len(ks) == 1 and low.ndim == 3 else (i, a)
-        every = [(i, k, a) for i, k in enumerate(ks) for a in range(2)]
-        pieces.add(low, [(index(i, a), 0, (k, a, 1), 0, cut) for i, k, a in every])
-        pieces.add(high, [(index(i, a), 0, (k, 1, a), cut, cols - cut) for i, k, a in every])
+        add_low(pieces, ks, low, cut)
+        add_high(pieces, ks, high, cut)
 
     def add_line(pieces, k, array, dx, dy):
         pieces.add(array, [((), 0, (k, dx, dy), 0, pieces.cols)])
@@ -782,55 +791,60 @@
     def tokens_step(tokens, came):
         return swapped_in(pick(tokens, at.x), came)
 
-    def unit_step(own, other):
-        return norm_parts(jnp.concatenate([own, other]).astype(f32))[0]
-
-    def stack(*v):
-        return jnp.stack(v)
-
-    def low_of(*v):
-        return jnp.concatenate([p[..., :s_cut] for p in v])
-
-    def high_of(*v):
-        return jnp.concatenate([p[..., s_cut:] for p in v])
-
-    half_z = nz // 2
+    def center_step(values):
+        values = values.astype(f32)
+        center = jnp.mean(values, axis=-1, keepdims=True)
+        spread = jnp.mean((values - center) ** 2, axis=-1, keepdims=True)
+        return center, lax.rsqrt(spread + norm_epsilon)
+
     ring = [line.run(chip_shard, turn, keep_s, line.done(core))]
     z, y = line.start(ring[0], at.to_z), line.start(ring[0], at.to_y)
     x = line.start(line.run(lambda v: pick(v, 1 - at.x), tokens), at.to_x)
     core = line.start(give_f, at.to_core)
+    xs, ys = [], []
     ring.append(line.done(z))
     z = line.start(ring[-1], at.to_z)
-    y_zero, tokens_came, core = line.done(y, x, core)
+    ys.append(line.done(y))
+    y = line.start(ring[1], at.to_y)
+    tokens_came = line.done(x)
+    x = line.start(ring[0], at.to_x)
+    core = line.done(core)
     shard_u, u_low, u_high, shard_d, d_low, d_high = line.run(other_shards, turn, keep_f, core)
-    tokens_own = line.run(tokens_step, tokens, tokens_came)
-    for _ in range(2, nz):
+    x_pair, y_pair = line.start(u_low, at.to_x), line.start(u_high, at.to_y)
+    ring.append(line.done(z))
+    z = line.start(ring[-1], at.to_z)
+    ys.append(line.done(y))
+    y = line.start(ring[2], at.to_y)
+    xs.append(line.done(x))
+    x = line.start(ring[1], at.to_x)
+    u_low, u_high = line.done(x_pair, y_pair)
+    u_pair, u_low, u_high = line.run(pair_parts(u_cut), shard_u, u_low, u_high)
+    for k in range(3, nz):
         ring.append(line.done(z))
-        if len(ring) < nz:
+        if k < nz - 1:
             z = line.start(ring[-1], at.to_z)
-        if len(ring) == 3:
-            x, y = line.start(u_low, at.to_x), line.start(u_high, at.to_y)
-            core = line.start(tokens_own, at.to_core)
-    u_low, u_high, ring_tokens = line.done(x, y, core)
-    u_pair, u_low, u_high = line.run(pair_parts(u_cut), shard_u, u_low, u_high)
-    x = line.start(line.run(stack, *ring[:half_z]), at.to_x)
-    y = line.start(line.run(stack, *ring[1:]), at.to_y)
     u_ring = [u_pair]
     z = line.start(u_pair, at.to_z)
-    later = line.run(stack, *ring[half_z:])
-    xs = [line.done(x)]
-    x = line.start(later, at.to_x)
-    ys = [y_zero, line.done(y)]
-    y = line.start(line.run(low_of, xs[0]), at.to_y)
-    x_both = line.start(line.run(high_of, ys[0][None], ys[1]), at.to_x)
+    ys.append(line.done(y))
+    y_more = [line.start(ring[k], at.to_y) for k in range(3, nz)]
+    xs.append(line.done(x))
+    x_more = [line.start(ring[k], at.to_x) for k in range(2, nz)]
+    both = line.start(xs[0], at.to_y)
+    tokens_own = line.run(tokens_step, tokens, tokens_came)
     u_ring.append(line.done(z))
-    xs.append(line.done(x))
-    y_later = line.start(line.run(low_of, xs[1]), at.to_y)
-    unit_one = line.run(unit_step, tokens_own, ring_tokens)
+    ys += [line.done(v) for v in y_more]
+    xs += [line.done(v) for v in x_more]
+    both = [line.done(both)]
+    core = line.start(tokens_own, at.to_core)
+    both_more = [line.start(xs[k], at.to_y) for k in range(1, nz)]
     z = line.start(u_ring[-1], at.to_z)
-    both_y = [line.done(y)]
-    both_x = line.done(x_both)
-    both_y.append(line.done(y_later))
+    tokens_all = line.run(lambda a, b: jnp.concatenate([a, b]), tokens_own, line.done(core))
+    center, inverse_one = line.run(center_step, tokens_all)
+    both += [line.done(v) for v in both_more]
+    u_ring.append(line.done(z))
+    x_pair, y_pair = line.start(d_low, at.to_x), line.start(d_high, at.to_y)
+    x, y = line.start(u_high, at.to_x), line.start(u_low, at.to_y)
+    z = line.start(u_ring[-1], at.to_z)
 
     row_lengths = pick(lengths, at.x)[0]
     ends_at = jnp.cumsum(row_lengths)
@@ -847,12 +861,9 @@
     feat_q, feat_k = line.run(lambda *v: v, feat_q, feat_k)
     for k in range(nz):
         add_line(s_pieces, k, ring[k], 0, 0)
-    for i, ks in enumerate((range(half_z), range(half_z, nz))):
-        s_pieces.add(xs[i], [((j,), 0, (k, 1, 0), 0, s_wide) for j, k in enumerate(ks)])
-        s_pieces.add(both_y[i], [((j,), 0, (k, 1, 1), 0, s_cut) for j, k in enumerate(ks)])
-    add_line(s_pieces, 0, ys[0], 0, 1)
-    s_pieces.add(ys[1], [((k - 1,), 0, (k, 0, 1), 0, s_wide) for k in range(1, nz)])
-    s_pieces.add(both_x, [((k,), 0, (k, 1, 1), s_cut, s_wide - s_cut) for k in range(nz)])
+        add_line(s_pieces, k, xs[k], 1, 0)
+        add_line(s_pieces, k, ys[k], 0, 1)
+        add_line(s_pieces, k, both[k], 1, 1)
 
     weight_s = s_pieces.place(line, (s_wide,))
     chosen = jnp.eye(vectors.shape[1], s_wide, head_width, dtype=bf16)
@@ -867,49 +878,49 @@
     bias_qkv = jnp.concatenate(
         [fill(halves[0], wide), jnp.zeros((1, wide), f32), fill(halves[1], wide)], axis=1
     )
-    normed = line.run(lambda u, g, s: (u * g + s).astype(bf16), unit_one, gain_one, shift_one)
-    u_ring.append(line.done(z))
-    for _ in range(3, nz - 1):
-        u_ring.append(line.done(line.start(u_ring[-1], at.to_z)))
-    x_pair, y_pair = line.start(d_low, at.to_x), line.start(d_high, at.to_y)
-    x, y = line.start(u_high, at.to_x), line.start(u_low, at.to_y)
-    z = line.start(u_ring[-1], at.to_z)
+    normed = line.run(
+        lambda v, c, i, g, s: ((v.astype(f32) - c) * i * g + s).astype(bf16),
+        tokens_all, center, inverse_one, gain_one, shift_one,
+    )
+    d_low, d_high, u_high, u_low = line.done(x_pair, y_pair, x, y)
+    low, high = line.run(stack_parts(u_cut), u_ring[1])
+    x, y = line.start(high, at.to_x), line.start(low, at.to_y)
     qkv = line.run(lambda n, w, b: (dot(n, w) + b).astype(bf16), normed, weight_s, bias_qkv)
-    add_pair(u_pieces, 0, u_pair, u_cut)
-    d_low, d_high = line.done(x_pair, y_pair)
-    d_pair, d_low, d_high = line.run(pair_parts(d_cut), shard_d, d_low, d_high)
-    high, low = line.done(x, y)
-    add_across(u_pieces, [0], low, high, u_cut)
-    low, high = line.run(stack_parts(u_cut), *u_ring[1:half_z])
-    x, y = line.start(high, at.to_x), line.start(low, at.to_y)
-    heads = H // 2
-    attended, lse = line.run(functools.partial(attend, 0, heads // 2), qkv, feat_q, feat_k)
     u_ring.append(line.done(z))
     high, low = line.done(x, y)
-    add_across(u_pieces, list(range(1, half_z)), low, high, u_cut)
-    low, high = line.run(stack_parts(u_cut), *u_ring[half_z:-1])
+    for _ in range(4, nz):
+        u_ring.append(line.done(line.start(u_ring[-1], at.to_z)))
+    d_pair, d_low, d_high = line.run(pair_parts(d_cut), shard_d, d_low, d_high)
+    add_pair(u_pieces, 0, u_pair, u_cut)
+    add_across(u_pieces, [0], u_low, u_high, u_cut)
+    add_across(u_pieces, [1], low, high, u_cut)
+    parts = [line.run(stack_parts(u_cut), u) for u in u_ring[2:]]
+    for k in range(1, nz):
+        add_pair(u_pieces, k, u_ring[k], u_cut)
+    heads = H // 2
+    x, y = line.start(parts[0][1], at.to_x), line.start(parts[0][0], at.to_y)
+    attended, lse = line.run(functools.partial(attend, 0, heads // 2), qkv, feat_q, feat_k)
+    high, low = line.done(x, y)
+    add_across(u_pieces, [2], low, high, u_cut)
+    going = [
+        (line.start(high, at.to_x), line.start(low, at.to_y)) for low, high in parts[1:]
+    ]
     z = line.start(d_pair, at.to_z)
-    x, y = line.start(high, at.to_x), line.start(low, at.to_y)
-    low, high = line.run(stack_parts(u_cut), u_ring[-1])
     attended, lse = line.run(
         functools.partial(attend, heads // 2, heads), qkv, feat_q, feat_k, attended, lse
     )
+    for k, (x, y) in enumerate(going):
+        high, low = line.done(x, y)
+        add_across(u_pieces, [3 + k], low, high, u_cut)
     d_ring = [d_pair, line.done(z)]
-    for k in range(1, nz):
-        add_pair(u_pieces, k, u_ring[k], u_cut)
-    high_two, low_two = line.done(x, y)
-    add_across(u_pieces, list(range(half_z, nz - 1)), low_two, high_two, u_cut)
     attended_own, give = line.run(
-        lambda a: (a[:own, :head_width], a[own:, :head_width]), attended
+        lambda a: (a[:own], a[own:]), attended
     )
     core = line.start(give, at.to_core)
-    x, y = line.start(high, at.to_x), line.start(low, at.to_y)
     z = line.start(d_ring[-1], at.to_z)
     cotangent_theirs = line.run(lambda v: pick(v, 1 - at.x), cotangent)
+    x, y = line.start(cotangent_theirs, at.to_x), line.start(d_low, at.to_y)
     attended_other = line.done(core)
-    high, low = line.done(x, y)
-    add_across(u_pieces, [nz - 1], low, high, u_cut)
-    x, y = line.start(cotangent_theirs, at.to_x), line.start(d_low, at.to_y)
     weight_half_o, weight_u = u_pieces.place(line, (out_cut, half_width), (True, False))
     d_ring.append(line.done(z))
     out_came, d_low = line.done(x, y)
@@ -994,10 +1005,12 @@
     branch_own, branch_peer = line.run(branch_columns, grad_branch)
 
     def heads_back(a, v, b, w):
+        spare = ((0, wide - head_width), (0, 0))
+        v, w = jnp.pad(v, spare), jnp.pad(w, spare)
         return (dot(a, v, NT) + dot(b, w, NT)).astype(bf16)
 
     def out_weight(a, b, g):
-        return jnp.concatenate([dot(a, g, TN, bf16), dot(b, g, TN, bf16)])
+        return jnp.concatenate([dot(v, g, TN, bf16)[:head_width] for v in (a, b)])
 
     give = line.run(
         heads_back, branch_own, weight_half_o[head_width:], branch_peer, other_half_o[:head_width]
@@ -1014,11 +1027,12 @@
         heads_back, branch_own, weight_half_o[:head_width], branch_peer, other_half_o[head_width:]
     )
     grad_att = line.run(
-        lambda a, b: fill(jnp.concatenate([a, b]), wide), grad_att_own, line.done(core)
+        lambda a, b: jnp.concatenate([a, b]), grad_att_own, line.done(core)
     )
 
     def out_weight_own(a, b, g, came):
-        total = jnp.concatenate([dot(a, g, TN), dot(b, g, TN)]) + came.astype(f32)
+        total = jnp.concatenate([dot(v, g, TN)[:head_width] for v in (a, b)])
+        total = total + came.astype(f32)
         half = total.shape[0] // 2
         low, high = total[:half], total[half:]
         return jnp.concatenate([by_core(low, high), by_core(high, low)]).astype(bf16)
@@ -1056,6 +1070,7 @@
         norm_back, back_own, line.done(core), grad_residual, tokens_own, gain_one
     )
     token_mine, token_theirs = line.run(for_swap_out, grad_tokens)
+    token_came = line.start(token_theirs, at.to_x)
     give = line.run(rows_other, active, weight_d)
     result_own = line.run(rows_own, active, weight_d)
     s_scatter.arrive()
@@ -1090,18 +1105,17 @@
         residual_one, result_own, line.done(core), bias_d,
     )
     out_mine, out_theirs = line.run(for_swap_out, block_output)
+    sums_at.step()
+    out_came = line.start(out_theirs, at.to_x)
     s_scatter.arrive()
-    sums_at.step()
     s_scatter.second()
-    token_came = line.start(token_theirs, at.to_x)
     u_scatter.arrive()
     sums_at.step()
     u_scatter.last_start()
     s_scatter.ring()
-    out_came = line.start(out_theirs, at.to_x)
     sums_at.step()
+    u_scatter.last()
     s_scatter.ring()
-    u_scatter.last()
     sums_at.step()
     s_scatter.last()
     sums_at.step()

time: 527 us -> 513 us (0.973)
  other arithmetic: 67.7 us -> 50.3 us
  waiting for transfers between devices: 139 us -> 149 us
  local copies, waits for them, and re-layouts: 87.7 us -> 80.1 us
    ppermute x88 -> x93, waiting for transfers between devices: 139 us -> 149 us  [send(): return lax.ppermute(value, AXES, pairs)]
    optimization_barrier x3 -> x0, local copies, waits for them, and re-layouts: 6.43 us -> none  [pin(): return lax.optimization_barrier((values, self.token))[0]]
    unnamed x244 -> x268, local copies, waits for them, and re-layouts: 40 us -> 41.2 us
    ppermute x88 -> x93, starting transfers between devices: 77.2 us -> 78.3 us  [send(): return lax.ppermute(value, AXES, pairs)]
  transfers between devices with their start and end apart: 88 -> 93, of which waited for: 34 -> 36; matrix products, arithmetic and copies ran while one was open for 25% -> 22% of each run, Pallas kernels for 16% -> 16%
where the time goes in v3:
time: 513 us; the launch traced here: 505 us
  waiting for transfers between devices  149 us (29%)
  Pallas kernels  85.7 us (17%)
  local copies, waits for them, and re-layouts  80.1 us (16%)
  starting transfers between devices  78.3 us (15%)
  matrix products  59 us (12%)
  other arithmetic  50.3 us (10%)
    ppermute x93, waiting for transfers between devices, send(): return lax.ppermute(value, AXES, pairs)  149 us
    ppermute x93, starting transfers between devices, send(): return lax.ppermute(value, AXES, pairs)  78.3 us
    dot_general x24, matrix products, dot(): return lax.dot_general(a, b, dims, preferred_element_type=f32).astype(out)  59 us
    unnamed x268, local copies, waits for them, and re-layouts  41.2 us
    pallas_call x2, Pallas kernels, attend_back(): pl.pallas_call(functools.partial(back_kernel, first, last, wide), out_sha...  33.5 us
    pallas_call x2, Pallas kernels, attend(): pl.pallas_call(functools.partial(attend_kernel, first, last, wide), out_s...  16.6 us
  transfers between devices with their start and end apart: 93, of which 36 were waited for; matrix products, arithmetic and copies ran while one was open for 22% of the time, Pallas kernels for 16%

profile of v3, /device:TPU:0, one launch (start us, length us, event | category | flops | bytes accessed | tf_op | source)
XLA Modules:
  0.0 505.5 jit_solution(10714611554075997789)
XLA Ops:
  7.6 2.9 collective-permute-start.1
  13.8 7.7 %collective-permute-done.3.refs_5_ = bf16[72,1920]{1,0:T(8,128)(2,1)S(1)} collective-permute-done((bf16[72,1920]{1,0:T(8,128)(2,1)S(1)}, bf16[72,1920]{1,0:T(8,128)(2,1)S(1)}, u32[]{:S(2)}, u32[]{:S(2)}) %collective-permute-start.3) | collective-permute-done | bytes 276512 | tf_op jit(solution)/shard_map/ppermute | solution.py:61
  29.9 3.0 collective-permute-done.6.refs_9_
  33.5 2.2 collective-permute-done.4.refs_2_
  35.8 3.6 collective-permute-done.11
  52.3 10.9 %collective-permute-done.17.refs_6_ = bf16[2,72,2816]{2,1,0:T(8,128)(2,1)S(1)} collective-permute-done((bf16[2,72,2816]{2,1,0:T(8,128)(2,1)S(1)}, bf16[2,72,2816]{2,1,0:T(8,128)(2,1)S(1)}, u32[]{:S(2)}, u32[]{:S(2)}) %collective-permute-start.17) | collective-permute-done | bytes 811040 | tf_op jit(solution)/shard_map/ppermute | solution.py:61
  73.0 3.2 collective-permute-done.19.refs_8_
  76.2 5.9 %collective-permute-done.20.refs_12_ = bf16[72,1920]{1,0:T(8,128)(2,1)S(1)} collective-permute-done((bf16[72,1920]{1,0:T(8,128)(2,1)}, bf16[72,1920]{1,0:T(8,128)(2,1)S(1)}, u32[]{:S(2)}, u32[]{:S(2)}) %collective-permute-start.20) | collective-permute-done | bytes 276512 | tf_op jit(solution)/shard_map/ppermute | solution.py:61
  82.2 5.4 %collective-permute-done.21.refs_16_ = bf16[72,1920]{1,0:T(8,128)(2,1)S(1)} collective-permute-done((bf16[72,1920]{1,0:T(8,128)(2,1)}, bf16[72,1920]{1,0:T(8,128)(2,1)S(1)}, u32[]{:S(2)}, u32[]{:S(2)}) %collective-permute-start.21) | collective-permute-done | bytes 276512 | tf_op jit(solution)/shard_map/ppermute | solution.py:61
  87.6 4.0 collective-permute-done.22.refs_7_
  93.4 2.1 copy-done.20
  97.8 4.0 add_convert_fusion.1
  104.9 4.2 collective-permute-done.26
  115.5 8.3 %add_convert_fusion.qkv_ref = bf16[1024,1920]{1,0:T(8,128)(2,1)S(1)} fusion(f32[1920]{0:T(1024)S(1)} %reduce.2, bf16[1024,1152]{1,0:T(8,128)(2,1)} %add_convert_fusion.1, bf16[1152,1920]{1,0:T(8,128)(2,1)} %bitcast.295), kind=kOutput, calls=%fused_computation.3 | convolution fusion | flops 4533780480 | bytes 10722816 | tf_op jit(solution)/shard_map/dot_general | solution.py:26
  132.5 8.3 %shard_map.306 = (bf16[1024,640]{1,0:T(8,128)(2,1)S(1)}, f32[8,1024]{1,0:T(8,128)S(1)}) custom-call(bf16[1024,1920]{1,0:T(8,128)(2,1)S(1)} %add_convert_fusion.qkv_ref, bf16[1024,256]{1,0:T(8,128)(2,1)S(1)} %compare_convert_fusion.qf_ref, bf16[1024,256]{1,0:T(8,128)(2,1)S(1)} %copy-done.16, bf16[16,128]{1,0:T(8,128)(2,1)S(1)} %broadcast_12_old_ref.2.old_ref, ...), custom_call_target="tpu_custom_call" | custom-call | flops 5000000000 | bytes 10000000 | tf_op jit(solution)/shard_map/pallas_call | solution.py:406
  144.6 8.3 %shard_map.307 = (bf16[1024,640]{1,0:T(8,128)(2,1)S(1)}, f32[8,1024]{1,0:T(8,128)S(1)}) custom-call(bf16[1024,1920]{1,0:T(8,128)(2,1)S(1)} %add_convert_fusion.qkv_ref, bf16[1024,256]{1,0:T(8,128)(2,1)S(1)} %compare_convert_fusion.qf_ref, bf16[1024,256]{1,0:T(8,128)(2,1)S(1)} %copy-done.16, bf16[1024,640]{1,0:T(8,128)(2,1)S(1)} %get-tuple-element.933.old_ref, ...), custom_call_target="tpu_custom_call" | custom-call | flops 5000000000 | bytes 10000000 | tf_op jit(solution)/shard_map/pallas_call | solution.py:406
  153.0 2.0 copy-done.74
  155.0 2.0 collective-permute-done.32.refs_8_
  168.9 3.0 shard_map.308
  172.0 4.6 collective-permute-done.38.refs_9_
  184.6 5.5 %shard_map.309 = (f32[512,1152]{1,0:T(8,128)S(1)}, bf16[512,1152]{1,0:T(8,128)(2,1)S(1)}) custom-call(s32[1]{0:T(128)} %bitcast.core_ref, bf16[512,1152]{1,0:T(8,128)(2,1)S(1)} %bitcast.287, bf16[512,640]{1,0:T(8,128)(2,1)S(1)} %get-tuple-element.1188.a_ref, bf16[512,640]{1,0:T(8,128)(2,1)} %collective-permute-done.35.b_ref, ...), custom_call_target="tpu_custom_call" | custom-call | flops 5000000000 | bytes 10000000 | tf_op jit(solution)/shard_map/pallas_call | solution.py:516
  192.2 8.0 %collective-permute-done.41.refs_4_ = bf16[2,2,72,1280]{3,2,1,0:T(8,128)(2,1)S(1)} collective-permute-done((bf16[2,2,72,1280]{3,2,1,0:T(8,128)(2,1)S(1)}, bf16[2,2,72,1280]{3,2,1,0:T(8,128)(2,1)S(1)}, u32[]{:S(2)}, u32[]{:S(2)}) %collective-permute-start.41) | collective-permute-done | bytes 737312 | tf_op jit(solution)/shard_map/ppermute | solution.py:61
  204.1 8.9 %shard_map.310 = (bf16[1024,2176]{1,0:T(8,128)(2,1)S(1)}, bf16[1024,2176]{1,0:T(8,128)(2,1)S(1)}) custom-call(bf16[1024,1152]{1,0:T(8,128)(2,1)S(1)} %pad_maximum_fusion.3.n_ref, bf16[1152,2176]{1,0:T(8,128)(2,1)S(1)} %bitcast.303, f32[1,2176]{1,0:T(1,128)S(1)} %broadcast_select_fusion.14.b_ref), custom_call_target="tpu_custom_call" | custom-call | flops 5000000000 | bytes 10000000 | tf_op jit(solution)/shard_map/pallas_call | solution.py:645
  213.0 2.3 copy-done.73
  215.3 2.1 copy-done.76
  217.4 2.0 copy-done.77
  225.9 2.7 shard_map.311
  231.2 6.2 %convolution_convert_fusion.1 = bf16[1152,2176]{1,0:T(8,128)(2,1)S(1)} fusion(bf16[1024,1152]{1,0:T(8,128)(2,1)S(1)} %pad_maximum_fusion.4.g_ref, bf16[1024,2176]{1,0:T(8,128)(2,1)S(1)} %copy-done.78), kind=kOutput, calls=%fused_computation.1 | convolution fusion | flops 5136334848 | bytes 11829248 | tf_op jit(solution)/shard_map/dot_general | solution.py:26
  237.6 2.3 copy-done.80
  242.3 7.5 %shard_map.312 = (bf16[1024,2176]{1,0:T(8,128)(2,1)S(1)}, f32[8,2176]{1,0:T(8,128)S(1)}) custom-call(bf16[1024,1152]{1,0:T(8,128)(2,1)S(1)} %pad_maximum_fusion.4.g_ref, bf16[1152,2176]{1,0:T(8,128)(2,1)S(1)} %bitcast.300, bf16[1024,2176]{1,0:T(8,128)(2,1)S(1)} %bitcast.309), custom_call_target="tpu_custom_call" | custom-call | flops 5000000000 | bytes 10000000 | tf_op jit(solution)/shard_map/pallas_call | solution.py:620
  249.7 2.4 collective-permute-done.49
  252.2 3.2 convolution_convert_fusion.8
  257.7 3.2 fusion.8.t_ref
  261.0 4.9 collective-permute-done.51
  268.7 7.5 %convolution_convert_fusion = bf16[1152,2176]{1,0:T(8,128)(2,1)} fusion(bf16[1024,1152]{1,0:T(8,128)(2,1)S(1)} %copy-done.3, bf16[1024,2176]{1,0:T(8,128)(2,1)S(1)} %get-tuple-element.1109), kind=kOutput, calls=%fused_computation | convolution fusion | flops 5136334848 | bytes 11829248 | tf_op jit(solution)/shard_map/dot_general | solution.py:26
  276.2 1.9 collective-permute-done.54
  278.1 2.9 shard_map.313
  284.4 1.9 fusion.109
  288.0 2.7 collective-permute-done.55
  290.7 2.5 collective-permute-done.56
  306.7 12.6 %collective-permute-done.59 = bf16[2,72,2176]{2,1,0:T(8,128)(2,1)S(1)} collective-permute-done((bf16[2,72,2176]{2,1,0:T(8,128)(2,1)}, bf16[2,72,2176]{2,1,0:T(8,128)(2,1)S(1)}, u32[]{:S(2)}, u32[]{:S(2)}) %collective-permute-start.59) | collective-permute-done | bytes 626720 | tf_op jit(solution)/shard_map/ppermute | solution.py:61
  319.3 6.7 %collective-permute-done.61 = bf16[2,2,72,1664]{3,2,1,0:T(8,128)(2,1)S(1)} collective-permute-done((bf16[2,2,72,1664]{3,2,1,0:T(8,128)(2,1)S(1)}, bf16[2,2,72,1664]{3,2,1,0:T(8,128)(2,1)S(1)}, u32[]{:S(2)}, u32[]{:S(2)}) %collective-permute-start.61) | collective-permute-done | bytes 958496 | tf_op jit(solution)/shard_map/ppermute | solution.py:61
  330.4 1.9 collective-permute-start.63
  333.7 16.9 %shard_map.314.old_ref = bf16[1024,1920]{1,0:T(8,128)(2,1)S(1)} custom-call(bf16[1024,1920]{1,0:T(8,128)(2,1)S(1)} %copy-done.75, bf16[1024,640]{1,0:T(8,128)(2,1)S(1)} %pad_maximum_fusion.8.do_ref, bf16[1024,256]{1,0:T(8,128)(2,1)S(1)} %copy-done.15, bf16[1024,256]{1,0:T(8,128)(2,1)S(1)} %copy-done.17, f32[8,1024]{1,0:T(8,128)S(1)} %get-tuple-element.1248.lse_ref, ...), custom_call_target="tpu_custom_call" | custom-call | flops 5000000000 | bytes 10000000 | tf_op jit(solution)/shard_map/pallas_call | solution.py:467
  354.4 2.4 slice.585
  359.4 1.9 collective-permute-start.67
  361.3 16.6 %shard_map.315 = bf16[1024,1920]{1,0:T(8,128)(2,1)S(1)} custom-call(bf16[1024,1920]{1,0:T(8,128)(2,1)S(1)} %copy-done.75, bf16[1024,640]{1,0:T(8,128)(2,1)S(1)} %pad_maximum_fusion.8.do_ref, bf16[1024,256]{1,0:T(8,128)(2,1)S(1)} %copy-done.15, bf16[1024,256]{1,0:T(8,128)(2,1)S(1)} %copy-done.17, f32[8,1024]{1,0:T(8,128)S(1)} %get-tuple-element.1248.lse_ref, ...), custom_call_target="tpu_custom_call" | custom-call | flops 5000000000 | bytes 10000000 | tf_op jit(solution)/shard_map/pallas_call | solution.py:467
  377.9 2.1 collective-permute-start.66
  383.1 5.7 %convolution_convert_fusion.2 = bf16[1152,1920]{1,0:T(8,128)(2,1)S(1)} fusion(bf16[1024,1152]{1,0:T(8,128)(2,1)S(1)} %copy-done.86, bf16[1024,1920]{1,0:T(8,128)(2,1)S(1)} %shard_map.315), kind=kOutput, calls=%fused_computation.4 | convolution fusion | flops 4532060160 | bytes 10715136 | tf_op jit(solution)/shard_map/dot_general | solution.py:26
  388.8 3.9 convolution_convert_fusion.6
  400.0 2.9 fusion.13.t_ref
  404.1 3.4 shard_map.316
  408.5 4.2 convolution_convert_fusion.7
  412.7 4.7 fusion.5
  417.4 8.4 %collective-permute-done.73 = bf16[4,2,72,1024]{3,2,1,0:T(8,128)(2,1)S(1)} collective-permute-done((bf16[4,2,72,1024]{3,2,1,0:T(8,128)(2,1)S(1)}, bf16[4,2,72,1024]{3,2,1,0:T(8,128)(2,1)S(1)}, u32[]{:S(2)}, u32[]{:S(2)}) %collective-permute-start.73) | collective-permute-done | bytes 1179680 | tf_op jit(solution)/shard_map/ppermute | solution.py:61
  429.7 1.9 slice.595
  431.6 1.9 slice.596
  437.3 2.2 fusion.16
  443.4 6.5 %collective-permute-done.75 = bf16[1,256,1152]{2,1,0:T(8,128)(2,1)S(1)} collective-permute-done((bf16[1,256,1152]{2,1,0:T(8,128)(2,1)S(1)}, bf16[1,256,1152]{2,1,0:T(8,128)(2,1)S(1)}, u32[]{:S(2)}, u32[]{:S(2)}) %collective-permute-start.75) | collective-permute-done | bytes 589856 | tf_op jit(solution)/shard_map/ppermute | solution.py:61
  453.3 2.4 add_convert_fusion.2
  456.8 5.3 %collective-permute-done.80 = bf16[4,72,1024]{2,1,0:T(8,128)(2,1)} collective-permute-done((bf16[4,72,1024]{2,1,0:T(8,128)(2,1)}, bf16[4,72,1024]{2,1,0:T(8,128)(2,1)}, u32[]{:S(2)}, u32[]{:S(2)}) %collective-permute-start.80) | collective-permute-done | bytes 589856 | tf_op jit(solution)/shard_map/ppermute | solution.py:61
  472.8 9.8 %collective-permute-done.78 = bf16[1,256,1152]{2,1,0:T(8,128)(2,1)S(1)} collective-permute-done((bf16[1,256,1152]{2,1,0:T(8,128)(2,1)S(1)}, bf16[1,256,1152]{2,1,0:T(8,128)(2,1)S(1)}, u32[]{:S(2)}, u32[]{:S(2)}) %collective-permute-start.78) | collective-permute-done | bytes 589856 | tf_op jit(solution)/shard_map/ppermute | solution.py:61
  486.7 5.5 %collective-permute-done.86 = bf16[72,1920]{1,0:T(8,128)(2,1)S(1)} collective-permute-done((bf16[72,1920]{1,0:T(8,128)(2,1)S(1)}, bf16[72,1920]{1,0:T(8,128)(2,1)S(1)}, u32[]{:S(2)}, u32[]{:S(2)}) %collective-permute-start.86) | collective-permute-done | bytes 276512 | tf_op jit(solution)/shard_map/ppermute | solution.py:61
  493.5 7.2 %collective-permute-done.90 = bf16[72,1920]{1,0:T(8,128)(2,1)S(1)} collective-permute-done((bf16[72,1920]{1,0:T(8,128)(2,1)S(1)}, bf16[72,1920]{1,0:T(8,128)(2,1)S(1)}, u32[]{:S(2)}, u32[]{:S(2)}) %collective-permute-start.90) | collective-permute-done | bytes 276512 | tf_op jit(solution)/shard_map/ppermute | solution.py:61
  (627 shorter events, 189.0 us)
Async XLA Ops:
  7.6 16.6 %collective-permute-start.1 = (bf16[1,256,1152]{2,1,0:T(8,128)(2,1)S(1)}, bf16[1,256,1152]{2,1,0:T(8,128)(2,1)S(1)}, u32[]{:S(2)}, u32[]{:S(2)}) collective-permute-start(bf16[1,256,1152]{2,1,0:T(8,128)(2,1)S(1)} %dynamic-slice_bitcast_fusion.12), channel_id=1, source_target_pairs={{0,2},{1,3},{2,0},{3,1},{4,6},{5,7},{6,4},{7,5},{8,10},{9,11},{10,... | collective-permute-start | bytes 1769480 | tf_op jit(solution)/shard_map/ppermute | solution.py:61
  10.6 13.5 %collective-permute-start.7 = (bf16[36,4992]{1,0:T(8,128)(2,1)S(1)}, bf16[36,4992]{1,0:T(8,128)(2,1)S(1)}, u32[]{:S(2)}, u32[]{:S(2)}) collective-permute-start(bf16[36,4992]{1,0:T(8,128)(2,1)S(1)} %get-tuple-element.767), channel_id=1, source_target_pairs={{0,1},{1,0},{2,3},{3,2},{4,5},{5,4},{6,7},{7,6},{8,9},{9,8},{10,11... | collective-permute-start | bytes 1078280 | tf_op jit(solution)/shard_map/ppermute | solution.py:61
  10.7 10.9 %collective-permute-start.3 = (bf16[72,1920]{1,0:T(8,128)(2,1)S(1)}, bf16[72,1920]{1,0:T(8,128)(2,1)S(1)}, u32[]{:S(2)}, u32[]{:S(2)}) collective-permute-start(bf16[72,1920]{1,0:T(8,128)(2,1)S(1)} %convolution_convert_fusion.9.refs_1_), channel_id=1, source_target_pairs={{0,8},{1,9},{2,10},{3,11},{4,12},{5,13},{6,14},{7,15},{8,16},{9,17... | collective-permute-start | bytes 829448 | tf_op jit(solution)/shard_map/ppermute | solution.py:61
  21.6 11.3 %collective-permute-start.5 = (bf16[72,1920]{1,0:T(8,128)(2,1)S(1)}, bf16[72,1920]{1,0:T(8,128)(2,1)S(1)}, u32[]{:S(2)}, u32[]{:S(2)}) collective-permute-start(bf16[72,1920]{1,0:T(8,128)(2,1)S(1)} %collective-permute-done.3.refs_5_), channel_id=1, source_target_pairs={{0,4},{1,5},{2,6},{3,7},{4,0},{5,1},{6,2},{7,3},{8,12},{9,13},{10,... | collective-permute-start | bytes 829448 | tf_op jit(solution)/shard_map/ppermute | solution.py:61
  27.8 11.6 %collective-permute-start.11 = (bf16[72,1664]{1,0:T(8,128)(2,1)S(1)}, bf16[72,1664]{1,0:T(8,128)(2,1)S(1)}, u32[]{:S(2)}, u32[]{:S(2)}) collective-permute-start(bf16[72,1664]{1,0:T(8,128)(2,1)S(1)} %slice.560), channel_id=1, source_target_pairs={{0,2},{1,3},{2,0},{3,1},{4,6},{5,7},{6,4},{7,5},{8,10},{9,11},{10,... | collective-permute-start | bytes 718856 | tf_op jit(solution)/shard_map/ppermute | solution.py:61
  28.1 11.3 %collective-permute-start.12 = (bf16[72,1152]{1,0:T(8,128)(2,1)S(1)}, bf16[72,1152]{1,0:T(8,128)(2,1)S(1)}, u32[]{:S(2)}, u32[]{:S(2)}) collective-permute-start(bf16[72,1152]{1,0:T(8,128)(2,1)S(1)} %slice.561), channel_id=1, source_target_pairs={{0,4},{1,5},{2,6},{3,7},{4,0},{5,1},{6,2},{7,3},{8,12},{9,13},{10,... | collective-permute-start | bytes 497672 | tf_op jit(solution)/shard_map/ppermute | solution.py:61
  32.9 11.9 %collective-permute-start.9 = (bf16[72,1920]{1,0:T(8,128)(2,1)S(1)}, bf16[72,1920]{1,0:T(8,128)(2,1)S(1)}, u32[]{:S(2)}, u32[]{:S(2)}) collective-permute-start(bf16[72,1920]{1,0:T(8,128)(2,1)S(1)} %collective-permute-done.6.refs_9_), channel_id=1, source_target_pairs={{0,4},{1,5},{2,6},{3,7},{4,0},{5,1},{6,2},{7,3},{8,12},{9,13},{10,... | collective-permute-start | bytes 829448 | tf_op jit(solution)/shard_map/ppermute | solution.py:61
  43.3 19.9 %collective-permute-start.17 = (bf16[2,72,2816]{2,1,0:T(8,128)(2,1)S(1)}, bf16[2,72,2816]{2,1,0:T(8,128)(2,1)S(1)}, u32[]{:S(2)}, u32[]{:S(2)}) collective-permute-start(bf16[2,72,2816]{2,1,0:T(8,128)(2,1)S(1)} %pad_maximum_fusion.13.refs_1_), channel_id=1, source_target_pairs={{0,8},{1,9},{2,10},{3,11},{4,12},{5,13},{6,14},{7,15},{8,16},{9,17... | collective-permute-start | bytes 2433032 | tf_op jit(solution)/shard_map/ppermute | solution.py:61
  44.9 18.3 %collective-permute-start.16 = (bf16[72,1920]{1,0:T(8,128)(2,1)}, bf16[72,1920]{1,0:T(8,128)(2,1)S(1)}, u32[]{:S(2)}, u32[]{:S(2)}) collective-permute-start(bf16[72,1920]{1,0:T(8,128)(2,1)} %copy-done.57), channel_id=1, source_target_pairs={{0,4},{1,5},{2,6},{3,7},{4,0},{5,1},{6,2},{7,3},{8,12},{9,13},{10,... | collective-permute-start | bytes 829448 | tf_op jit(solution)/shard_map/ppermute | solution.py:61
  47.6 16.3 %collective-permute-start.13 = (bf16[72,1920]{1,0:T(8,128)(2,1)}, bf16[72,1920]{1,0:T(8,128)(2,1)S(1)}, u32[]{:S(2)}, u32[]{:S(2)}) collective-permute-start(bf16[72,1920]{1,0:T(8,128)(2,1)} %collective-permute-done.4.refs_2_), channel_id=1, source_target_pairs={{0,4},{1,5},{2,6},{3,7},{4,0},{5,1},{6,2},{7,3},{8,12},{9,13},{10,... | collective-permute-start | bytes 829448 | tf_op jit(solution)/shard_map/ppermute | solution.py:61
  48.7 15.2 %collective-permute-start.14 = (bf16[72,1920]{1,0:T(8,128)(2,1)}, bf16[72,1920]{1,0:T(8,128)(2,1)S(1)}, u32[]{:S(2)}, u32[]{:S(2)}) collective-permute-start(bf16[72,1920]{1,0:T(8,128)(2,1)} %copy-done.57), channel_id=1, source_target_pairs={{0,2},{1,3},{2,0},{3,1},{4,6},{5,7},{6,4},{7,5},{8,10},{9,11},{10,... | collective-permute-start | bytes 829448 | tf_op jit(solution)/shard_map/ppermute | solution.py:61
  50.2 13.7 %collective-permute-start.15 = (bf16[72,1920]{1,0:T(8,128)(2,1)S(1)}, bf16[72,1920]{1,0:T(8,128)(2,1)S(1)}, u32[]{:S(2)}, u32[]{:S(2)}) collective-permute-start(bf16[72,1920]{1,0:T(8,128)(2,1)S(1)} %collective-permute-done.6.refs_9_), channel_id=1, source_target_pairs={{0,2},{1,3},{2,0},{3,1},{4,6},{5,7},{6,4},{7,5},{8,10},{9,11},{10,... | collective-permute-start | bytes 829448 | tf_op jit(solution)/shard_map/ppermute | solution.py:61
  68.1 14.0 %collective-permute-start.20 = (bf16[72,1920]{1,0:T(8,128)(2,1)}, bf16[72,1920]{1,0:T(8,128)(2,1)S(1)}, u32[]{:S(2)}, u32[]{:S(2)}) collective-permute-start(bf16[72,1920]{1,0:T(8,128)(2,1)} %copy-done.67), channel_id=1, source_target_pairs={{0,4},{1,5},{2,6},{3,7},{4,0},{5,1},{6,2},{7,3},{8,12},{9,13},{10,... | collective-permute-start | bytes 829448 | tf_op jit(solution)/shard_map/ppermute | solution.py:61
  68.6 18.9 %collective-permute-start.21 = (bf16[72,1920]{1,0:T(8,128)(2,1)}, bf16[72,1920]{1,0:T(8,128)(2,1)S(1)}, u32[]{:S(2)}, u32[]{:S(2)}) collective-permute-start(bf16[72,1920]{1,0:T(8,128)(2,1)} %copy-done.65), channel_id=1, source_target_pairs={{0,4},{1,5},{2,6},{3,7},{4,0},{5,1},{6,2},{7,3},{8,12},{9,13},{10,... | collective-permute-start | bytes 829448 | tf_op jit(solution)/shard_map/ppermute | solution.py:61
  70.2 21.4 %collective-permute-start.22 = (bf16[2,72,2816]{2,1,0:T(8,128)(2,1)S(1)}, bf16[2,72,2816]{2,1,0:T(8,128)(2,1)}, u32[]{:S(2)}, u32[]{:S(2)}) collective-permute-start(bf16[2,72,2816]{2,1,0:T(8,128)(2,1)S(1)} %collective-permute-done.17.refs_6_), channel_id=1, source_target_pairs={{0,8},{1,9},{2,10},{3,11},{4,12},{5,13},{6,14},{7,15},{8,16},{9,17... | collective-permute-start | bytes 2433032 | tf_op jit(solution)/shard_map/ppermute | solution.py:61
  96.4 15.2 %collective-permute-start.23 = (bf16[2,72,1664]{2,1,0:T(8,128)(2,1)}, bf16[2,72,1664]{2,1,0:T(8,128)(2,1)S(1)}, u32[]{:S(2)}, u32[]{:S(2)}) collective-permute-start(bf16[2,72,1664]{2,1,0:T(8,128)(2,1)} %fusion.48), channel_id=1, source_target_pairs={{0,4},{1,5},{2,6},{3,7},{4,0},{5,1},{6,2},{7,3},{8,12},{9,13},{10,... | collective-permute-start | bytes 1437704 | tf_op jit(solution)/shard_map/ppermute | solution.py:61
  97.0 13.9 %collective-permute-start.24 = (bf16[2,72,1152]{2,1,0:T(8,128)(2,1)}, bf16[2,72,1152]{2,1,0:T(8,128)(2,1)S(1)}, u32[]{:S(2)}, u32[]{:S(2)}) collective-permute-start(bf16[2,72,1152]{2,1,0:T(8,128)(2,1)} %fusion.54), channel_id=1, source_target_pairs={{0,2},{1,3},{2,0},{3,1},{4,6},{5,7},{6,4},{7,5},{8,10},{9,11},{10,... | collective-permute-start | bytes 995336 | tf_op jit(solution)/shard_map/ppermute | solution.py:61
  104.7 19.8 %collective-permute-start.27 = (bf16[2,72,2816]{2,1,0:T(8,128)(2,1)}, bf16[2,72,2816]{2,1,0:T(8,128)(2,1)}, u32[]{:S(2)}, u32[]{:S(2)}) collective-permute-start(bf16[2,72,2816]{2,1,0:T(8,128)(2,1)} %collective-permute-done.22.refs_7_), channel_id=1, source_target_pairs={{0,8},{1,9},{2,10},{3,11},{4,12},{5,13},{6,14},{7,15},{8,16},{9,17... | collective-permute-start | bytes 2433032 | tf_op jit(solution)/shard_map/ppermute | solution.py:61
  114.0 10.8 %collective-permute-start.28 = (bf16[1,2,72,1664]{3,2,1,0:T(8,128)(2,1)}, bf16[1,2,72,1664]{3,2,1,0:T(8,128)(2,1)S(1)}, u32[]{:S(2)}, u32[]{:S(2)}) collective-permute-start(bf16[1,2,72,1664]{3,2,1,0:T(8,128)(2,1)} %slice_bitcast_fusion.2), channel_id=1, source_target_pairs={{0,4},{1,5},{2,6},{3,7},{4,0},{5,1},{6,2},{7,3},{8,12},{9,13},{10,... | collective-permute-start | bytes 1437704 | tf_op jit(solution)/shard_map/ppermute | solution.py:61
  114.6 9.9 %collective-permute-start.29 = (bf16[1,2,72,1152]{3,2,1,0:T(8,128)(2,1)}, bf16[1,2,72,1152]{3,2,1,0:T(8,128)(2,1)S(1)}, u32[]{:S(2)}, u32[]{:S(2)}) collective-permute-start(bf16[1,2,72,1152]{3,2,1,0:T(8,128)(2,1)} %slice_bitcast_fusion.8), channel_id=1, source_target_pairs={{0,2},{1,3},{2,0},{3,1},{4,6},{5,7},{6,4},{7,5},{8,10},{9,11},{10,... | collective-permute-start | bytes 995336 | tf_op jit(solution)/shard_map/ppermute | solution.py:61
  130.6 10.9 %collective-permute-start.30 = (bf16[1,2,72,1664]{3,2,1,0:T(8,128)(2,1)S(1)}, bf16[1,2,72,1664]{3,2,1,0:T(8,128)(2,1)S(1)}, u32[]{:S(2)}, u32[]{:S(2)}) collective-permute-start(bf16[1,2,72,1664]{3,2,1,0:T(8,128)(2,1)S(1)} %slice_bitcast_fusion.1), channel_id=1, source_target_pairs={{0,4},{1,5},{2,6},{3,7},{4,0},{5,1},{6,2},{7,3},{8,12},{9,13},{10,... | collective-permute-start | bytes 1437704 | tf_op jit(solution)/shard_map/ppermute | solution.py:61
  142.4 14.6 %collective-permute-start.32 = (bf16[2,72,2176]{2,1,0:T(8,128)(2,1)S(1)}, bf16[2,72,2176]{2,1,0:T(8,128)(2,1)}, u32[]{:S(2)}, u32[]{:S(2)}) collective-permute-start(bf16[2,72,2176]{2,1,0:T(8,128)(2,1)S(1)} %pad_maximum_fusion.15.refs_1_), channel_id=1, source_target_pairs={{0,8},{1,9},{2,10},{3,11},{4,12},{5,13},{6,14},{7,15},{8,16},{9,17... | collective-permute-start | bytes 1880072 | tf_op jit(solution)/shard_map/ppermute | solution.py:61
  142.4 12.6 %collective-permute-start.33 = (bf16[1,2,72,1664]{3,2,1,0:T(8,128)(2,1)S(1)}, bf16[1,2,72,1664]{3,2,1,0:T(8,128)(2,1)S(1)}, u32[]{:S(2)}, u32[]{:S(2)}) collective-permute-start(bf16[1,2,72,1664]{3,2,1,0:T(8,128)(2,1)S(1)} %slice_bitcast_fusion), channel_id=1, source_target_pairs={{0,4},{1,5},{2,6},{3,7},{4,0},{5,1},{6,2},{7,3},{8,12},{9,13},{10,... | collective-permute-start | bytes 1437704 | tf_op jit(solution)/shard_map/ppermute | solution.py:61
  143.1 11.8 %collective-permute-start.34 = (bf16[1,2,72,1152]{3,2,1,0:T(8,128)(2,1)S(1)}, bf16[1,2,72,1152]{3,2,1,0:T(8,128)(2,1)S(1)}, u32[]{:S(2)}, u32[]{:S(2)}) collective-permute-start(bf16[1,2,72,1152]{3,2,1,0:T(8,128)(2,1)S(1)} %slice_bitcast_fusion.6), channel_id=1, source_target_pairs={{0,2},{1,3},{2,0},{3,1},{4,6},{5,7},{6,4},{7,5},{8,10},{9,11},{10,... | collective-permute-start | bytes 995336 | tf_op jit(solution)/shard_map/ppermute | solution.py:61
  158.0 18.6 %collective-permute-start.38 = (bf16[2,72,2176]{2,1,0:T(8,128)(2,1)}, bf16[2,72,2176]{2,1,0:T(8,128)(2,1)}, u32[]{:S(2)}, u32[]{:S(2)}) collective-permute-start(bf16[2,72,2176]{2,1,0:T(8,128)(2,1)} %collective-permute-done.32.refs_8_), channel_id=1, source_target_pairs={{0,8},{1,9},{2,10},{3,11},{4,12},{5,13},{6,14},{7,15},{8,16},{9,17... | collective-permute-start | bytes 1880072 | tf_op jit(solution)/shard_map/ppermute | solution.py:61
  158.9 17.7 %collective-permute-start.37 = (bf16[1,256,1152]{2,1,0:T(8,128)(2,1)}, bf16[1,256,1152]{2,1,0:T(8,128)(2,1)}, u32[]{:S(2)}, u32[]{:S(2)}) collective-permute-start(bf16[1,256,1152]{2,1,0:T(8,128)(2,1)} %dynamic-slice_bitcast_fusion.11), channel_id=1, source_target_pairs={{0,2},{1,3},{2,0},{3,1},{4,6},{5,7},{6,4},{7,5},{8,10},{9,11},{10,... | collective-permute-start | bytes 1769480 | tf_op jit(solution)/shard_map/ppermute | solution.py:61
  159.6 17.0 %collective-permute-start.36 = (bf16[2,72,1280]{2,1,0:T(8,128)(2,1)}, bf16[2,72,1280]{2,1,0:T(8,128)(2,1)S(1)}, u32[]{:S(2)}, u32[]{:S(2)}) collective-permute-start(bf16[2,72,1280]{2,1,0:T(8,128)(2,1)} %fusion.53), channel_id=1, source_target_pairs={{0,4},{1,5},{2,6},{3,7},{4,0},{5,1},{6,2},{7,3},{8,12},{9,13},{10,... | collective-permute-start | bytes 1105928 | tf_op jit(solution)/shard_map/ppermute | solution.py:61
  181.0 20.1 %collective-permute-start.40 = (bf16[2,72,2176]{2,1,0:T(8,128)(2,1)}, bf16[2,72,2176]{2,1,0:T(8,128)(2,1)S(1)}, u32[]{:S(2)}, u32[]{:S(2)}) collective-permute-start(bf16[2,72,2176]{2,1,0:T(8,128)(2,1)} %collective-permute-done.38.refs_9_), channel_id=1, source_target_pairs={{0,8},{1,9},{2,10},{3,11},{4,12},{5,13},{6,14},{7,15},{8,16},{9,17... | collective-permute-start | bytes 1880072 | tf_op jit(solution)/shard_map/ppermute | solution.py:61
  181.3 19.0 %collective-permute-start.41 = (bf16[2,2,72,1280]{3,2,1,0:T(8,128)(2,1)S(1)}, bf16[2,2,72,1280]{3,2,1,0:T(8,128)(2,1)S(1)}, u32[]{:S(2)}, u32[]{:S(2)}) collective-permute-start(bf16[2,2,72,1280]{3,2,1,0:T(8,128)(2,1)S(1)} %pad_maximum_fusion.16), channel_id=1, source_target_pairs={{0,4},{1,5},{2,6},{3,7},{4,0},{5,1},{6,2},{7,3},{8,12},{9,13},{10,... | collective-permute-start | bytes 2211848 | tf_op jit(solution)/shard_map/ppermute | solution.py:61
  201.2 18.2 %collective-permute-start.44 = (bf16[2,2,72,896]{3,2,1,0:T(8,128)(2,1)S(1)}, bf16[2,2,72,896]{3,2,1,0:T(8,128)(2,1)S(1)}, u32[]{:S(2)}, u32[]{:S(2)}) collective-permute-start(bf16[2,2,72,896]{3,2,1,0:T(8,128)(2,1)S(1)} %pad_maximum_fusion.20), channel_id=1, source_target_pairs={{0,2},{1,3},{2,0},{3,1},{4,6},{5,7},{6,4},{7,5},{8,10},{9,11},{10,... | collective-permute-start | bytes 1548296 | tf_op jit(solution)/shard_map/ppermute | solution.py:61
  201.9 18.3 %collective-permute-start.45 = (bf16[1,2,72,1280]{3,2,1,0:T(8,128)(2,1)S(1)}, bf16[1,2,72,1280]{3,2,1,0:T(8,128)(2,1)S(1)}, u32[]{:S(2)}, u32[]{:S(2)}) collective-permute-start(bf16[1,2,72,1280]{3,2,1,0:T(8,128)(2,1)S(1)} %slice_bitcast_fusion.3), channel_id=1, source_target_pairs={{0,4},{1,5},{2,6},{3,7},{4,0},{5,1},{6,2},{7,3},{8,12},{9,13},{10,... | collective-permute-start | bytes 1105928 | tf_op jit(solution)/shard_map/ppermute | solution.py:61
  203.1 17.9 %collective-permute-start.46 = (bf16[1,2,72,896]{3,2,1,0:T(8,128)(2,1)S(1)}, bf16[1,2,72,896]{3,2,1,0:T(8,128)(2,1)S(1)}, u32[]{:S(2)}, u32[]{:S(2)}) collective-permute-start(bf16[1,2,72,896]{3,2,1,0:T(8,128)(2,1)S(1)} %slice_bitcast_fusion.9), channel_id=1, source_target_pairs={{0,2},{1,3},{2,0},{3,1},{4,6},{5,7},{6,4},{7,5},{8,10},{9,11},{10,... | collective-permute-start | bytes 774152 | tf_op jit(solution)/shard_map/ppermute | solution.py:61
  240.3 11.9 %collective-permute-start.48 = (bf16[1,2,72,896]{3,2,1,0:T(8,128)(2,1)S(1)}, bf16[1,2,72,896]{3,2,1,0:T(8,128)(2,1)S(1)}, u32[]{:S(2)}, u32[]{:S(2)}) collective-permute-start(bf16[1,2,72,896]{3,2,1,0:T(8,128)(2,1)S(1)} %get-tuple-element.1087), channel_id=1, source_target_pairs={{0,2},{1,3},{2,0},{3,1},{4,6},{5,7},{6,4},{7,5},{8,10},{9,11},{10,... | collective-permute-start | bytes 774152 | tf_op jit(solution)/shard_map/ppermute | solution.py:61
  241.5 10.7 %collective-permute-start.49 = (bf16[1,2,72,1280]{3,2,1,0:T(8,128)(2,1)S(1)}, bf16[1,2,72,1280]{3,2,1,0:T(8,128)(2,1)S(1)}, u32[]{:S(2)}, u32[]{:S(2)}) collective-permute-start(bf16[1,2,72,1280]{3,2,1,0:T(8,128)(2,1)S(1)} %get-tuple-element.1089), channel_id=1, source_target_pairs={{0,4},{1,5},{2,6},{3,7},{4,0},{5,1},{6,2},{7,3},{8,12},{9,13},{10,... | collective-permute-start | bytes 1105928 | tf_op jit(solution)/shard_map/ppermute | solution.py:61
  255.5 10.4 %collective-permute-start.50 = (bf16[1,2,72,896]{3,2,1,0:T(8,128)(2,1)S(1)}, bf16[1,2,72,896]{3,2,1,0:T(8,128)(2,1)S(1)}, u32[]{:S(2)}, u32[]{:S(2)}) collective-permute-start(bf16[1,2,72,896]{3,2,1,0:T(8,128)(2,1)S(1)} %get-tuple-element.1101), channel_id=1, source_target_pairs={{0,2},{1,3},{2,0},{3,1},{4,6},{5,7},{6,4},{7,5},{8,10},{9,11},{10,... | collective-permute-start | bytes 774152 | tf_op jit(solution)/shard_map/ppermute | solution.py:61
  265.8 10.4 %collective-permute-start.52 = (bf16[512,1152]{1,0:T(8,128)(2,1)S(1)}, bf16[512,1152]{1,0:T(8,128)(2,1)S(1)}, u32[]{:S(2)}, u32[]{:S(2)}) collective-permute-start(bf16[512,1152]{1,0:T(8,128)(2,1)S(1)} %convolution_convert_fusion.8), channel_id=1, source_target_pairs={{0,1},{1,0},{2,3},{3,2},{4,5},{5,4},{6,7},{7,6},{8,9},{9,8},{10,11... | collective-permute-start | bytes 3538952 | tf_op jit(solution)/shard_map/ppermute | solution.py:61
  266.5 11.6 %collective-permute-start.53 = (bf16[1,2,72,896]{3,2,1,0:T(8,128)(2,1)S(1)}, bf16[1,2,72,896]{3,2,1,0:T(8,128)(2,1)S(1)}, u32[]{:S(2)}, u32[]{:S(2)}) collective-permute-start(bf16[1,2,72,896]{3,2,1,0:T(8,128)(2,1)S(1)} %get-tuple-element.1113), channel_id=1, source_target_pairs={{0,2},{1,3},{2,0},{3,1},{4,6},{5,7},{6,4},{7,5},{8,10},{9,11},{10,... | collective-permute-start | bytes 774152 | tf_op jit(solution)/shard_map/ppermute | solution.py:61
  267.9 10.2 %collective-permute-start.54 = (bf16[1,2,72,1280]{3,2,1,0:T(8,128)(2,1)S(1)}, bf16[1,2,72,1280]{3,2,1,0:T(8,128)(2,1)S(1)}, u32[]{:S(2)}, u32[]{:S(2)}) collective-permute-start(bf16[1,2,72,1280]{3,2,1,0:T(8,128)(2,1)S(1)} %get-tuple-element.1115), channel_id=1, source_target_pairs={{0,4},{1,5},{2,6},{3,7},{4,0},{5,1},{6,2},{7,3},{8,12},{9,13},{10,... | collective-permute-start | bytes 1105928 | tf_op jit(solution)/shard_map/ppermute | solution.py:61
  293.6 9.9 %collective-permute-start.58 = (bf16[1152,640]{1,0:T(8,128)(2,1)S(1)}, bf16[1152,640]{1,0:T(8,128)(2,1)S(1)}, u32[]{:S(2)}, u32[]{:S(2)}) collective-permute-start(bf16[1152,640]{1,0:T(8,128)(2,1)S(1)} %pad_maximum_fusion.6), channel_id=1, source_target_pairs={{0,1},{1,0},{2,3},{3,2},{4,5},{5,4},{6,7},{7,6},{8,9},{9,8},{10,11... | collective-permute-start | bytes 4423688 | tf_op jit(solution)/shard_map/ppermute | solution.py:61
  300.7 18.6 %collective-permute-start.59 = (bf16[2,72,2176]{2,1,0:T(8,128)(2,1)}, bf16[2,72,2176]{2,1,0:T(8,128)(2,1)S(1)}, u32[]{:S(2)}, u32[]{:S(2)}) collective-permute-start(bf16[2,72,2176]{2,1,0:T(8,128)(2,1)} %fusion.40), channel_id=1, source_target_pairs={{0,8},{1,9},{2,10},{3,11},{4,12},{5,13},{6,14},{7,15},{8,16},{9,17... | collective-permute-start | bytes 1880072 | tf_op jit(solution)/shard_map/ppermute | solution.py:61
  301.4 24.6 %collective-permute-start.60 = (bf16[2,2,72,512]{3,2,1,0:T(8,128)(2,1)S(1)}, bf16[2,2,72,512]{3,2,1,0:T(8,128)(2,1)S(1)}, u32[]{:S(2)}, u32[]{:S(2)}) collective-permute-start(bf16[2,2,72,512]{3,2,1,0:T(8,128)(2,1)S(1)} %get-tuple-element.1199), channel_id=1, source_target_pairs={{0,2},{1,3},{2,0},{3,1},{4,6},{5,7},{6,4},{7,5},{8,10},{9,11},{10,... | collective-permute-start | bytes 884744 | tf_op jit(solution)/shard_map/ppermute | solution.py:61
  302.9 23.0 %collective-permute-start.61 = (bf16[2,2,72,1664]{3,2,1,0:T(8,128)(2,1)S(1)}, bf16[2,2,72,1664]{3,2,1,0:T(8,128)(2,1)S(1)}, u32[]{:S(2)}, u32[]{:S(2)}) collective-permute-start(bf16[2,2,72,1664]{3,2,1,0:T(8,128)(2,1)S(1)} %get-tuple-element.1201), channel_id=1, source_target_pairs={{0,4},{1,5},{2,6},{3,7},{4,0},{5,1},{6,2},{7,3},{8,12},{9,13},{10,... | collective-permute-start | bytes 2875400 | tf_op jit(solution)/shard_map/ppermute | solution.py:61
  327.7 22.9 %collective-permute-start.62 = (bf16[2,2,72,1664]{3,2,1,0:T(8,128)(2,1)S(1)}, bf16[2,2,72,1664]{3,2,1,0:T(8,128)(2,1)S(1)}, u32[]{:S(2)}, u32[]{:S(2)}) collective-permute-start(bf16[2,2,72,1664]{3,2,1,0:T(8,128)(2,1)S(1)} %get-tuple-element.1218), channel_id=1, source_target_pairs={{0,4},{1,5},{2,6},{3,7},{4,0},{5,1},{6,2},{7,3},{8,12},{9,13},{10,... | collective-permute-start | bytes 2875400 | tf_op jit(solution)/shard_map/ppermute | solution.py:61
  328.3 23.5 %collective-permute-start.65 = (bf16[4,2,72,640]{3,2,1,0:T(8,128)(2,1)S(1)}, bf16[4,2,72,640]{3,2,1,0:T(8,128)(2,1)S(1)}, u32[]{:S(2)}, u32[]{:S(2)}) collective-permute-start(bf16[4,2,72,640]{3,2,1,0:T(8,128)(2,1)S(1)} %dynamic-slice_bitcast_fusion.6), channel_id=1, source_target_pairs={{0,2},{1,3},{2,0},{3,1},{4,6},{5,7},{6,4},{7,5},{8,10},{9,11},{10,... | collective-permute-start | bytes 2211848 | tf_op jit(solution)/shard_map/ppermute | solution.py:61
  330.4 20.1 %collective-permute-start.63 = (bf16[2,72,2176]{2,1,0:T(8,128)(2,1)}, bf16[2,72,2176]{2,1,0:T(8,128)(2,1)S(1)}, u32[]{:S(2)}, u32[]{:S(2)}) collective-permute-start(bf16[2,72,2176]{2,1,0:T(8,128)(2,1)} %fusion.22), channel_id=1, source_target_pairs={{0,8},{1,9},{2,10},{3,11},{4,12},{5,13},{6,14},{7,15},{8,16},{9,17... | collective-permute-start | bytes 1880072 | tf_op jit(solution)/shard_map/ppermute | solution.py:61
  333.0 18.8 %collective-permute-start.64 = (bf16[2,2,72,512]{3,2,1,0:T(8,128)(2,1)S(1)}, bf16[2,2,72,512]{3,2,1,0:T(8,128)(2,1)S(1)}, u32[]{:S(2)}, u32[]{:S(2)}) collective-permute-start(bf16[2,2,72,512]{3,2,1,0:T(8,128)(2,1)S(1)} %get-tuple-element.1225), channel_id=1, source_target_pairs={{0,2},{1,3},{2,0},{3,1},{4,6},{5,7},{6,4},{7,5},{8,10},{9,11},{10,... | collective-permute-start | bytes 884744 | tf_op jit(solution)/shard_map/ppermute | solution.py:61
  359.4 21.8 %collective-permute-start.67 = (bf16[2,72,2176]{2,1,0:T(8,128)(2,1)}, bf16[2,72,2176]{2,1,0:T(8,128)(2,1)S(1)}, u32[]{:S(2)}, u32[]{:S(2)}) collective-permute-start(bf16[2,72,2176]{2,1,0:T(8,128)(2,1)} %fusion.21), channel_id=1, source_target_pairs={{0,8},{1,9},{2,10},{3,11},{4,12},{5,13},{6,14},{7,15},{8,16},{9,17... | collective-permute-start | bytes 1880072 | tf_op jit(solution)/shard_map/ppermute | solution.py:61
  377.9 19.4 %collective-permute-start.66 = (bf16[2,72,2816]{2,1,0:T(8,128)(2,1)S(1)}, bf16[2,72,2816]{2,1,0:T(8,128)(2,1)S(1)}, u32[]{:S(2)}, u32[]{:S(2)}) collective-permute-start(bf16[2,72,2816]{2,1,0:T(8,128)(2,1)S(1)} %dynamic-slice_bitcast_fusion.5), channel_id=1, source_target_pairs={{0,8},{1,9},{2,10},{3,11},{4,12},{5,13},{6,14},{7,15},{8,16},{9,17... | collective-permute-start | bytes 2433032 | tf_op jit(solution)/shard_map/ppermute | solution.py:61
  393.5 10.6 %collective-permute-start.68 = (bf16[512,1152]{1,0:T(8,128)(2,1)}, bf16[512,1152]{1,0:T(8,128)(2,1)S(1)}, u32[]{:S(2)}, u32[]{:S(2)}) collective-permute-start(bf16[512,1152]{1,0:T(8,128)(2,1)} %convolution_convert_fusion.6), channel_id=1, source_target_pairs={{0,1},{1,0},{2,3},{3,2},{4,5},{5,4},{6,7},{7,6},{8,9},{9,8},{10,11... | collective-permute-start | bytes 3538952 | tf_op jit(solution)/shard_map/ppermute | solution.py:61
  395.8 30.0 %collective-permute-start.72 = (bf16[4,2,72,896]{3,2,1,0:T(8,128)(2,1)S(1)}, bf16[4,2,72,896]{3,2,1,0:T(8,128)(2,1)S(1)}, u32[]{:S(2)}, u32[]{:S(2)}) collective-permute-start(bf16[4,2,72,896]{3,2,1,0:T(8,128)(2,1)S(1)} %dynamic-slice_bitcast_fusion.2), channel_id=1, source_target_pairs={{0,2},{1,3},{2,0},{3,1},{4,6},{5,7},{6,4},{7,5},{8,10},{9,11},{10,... | collective-permute-start | bytes 3096584 | tf_op jit(solution)/shard_map/ppermute | solution.py:61
  397.3 28.5 %collective-permute-start.73 = (bf16[4,2,72,1024]{3,2,1,0:T(8,128)(2,1)S(1)}, bf16[4,2,72,1024]{3,2,1,0:T(8,128)(2,1)S(1)}, u32[]{:S(2)}, u32[]{:S(2)}) collective-permute-start(bf16[4,2,72,1024]{3,2,1,0:T(8,128)(2,1)S(1)} %dynamic-slice_bitcast_fusion.1), channel_id=1, source_target_pairs={{0,4},{1,5},{2,6},{3,7},{4,0},{5,1},{6,2},{7,3},{8,12},{9,13},{10,... | collective-permute-start | bytes 3538952 | tf_op jit(solution)/shard_map/ppermute | solution.py:61
  403.8 25.9 %collective-permute-start.71 = (bf16[2,72,2816]{2,1,0:T(8,128)(2,1)}, bf16[2,72,2816]{2,1,0:T(8,128)(2,1)S(1)}, u32[]{:S(2)}, u32[]{:S(2)}) collective-permute-start(bf16[2,72,2816]{2,1,0:T(8,128)(2,1)} %fusion.17), channel_id=1, source_target_pairs={{0,8},{1,9},{2,10},{3,11},{4,12},{5,13},{6,14},{7,15},{8,16},{9,17... | collective-permute-start | bytes 2433032 | tf_op jit(solution)/shard_map/ppermute | solution.py:61
  404.0 35.5 %collective-permute-start.76 = (f32[36,2176]{1,0:T(8,128)}, f32[36,2176]{1,0:T(8,128)}, u32[]{:S(2)}, u32[]{:S(2)}) collective-permute-start(f32[36,2176]{1,0:T(8,128)} %get-tuple-element.1332), channel_id=1, source_target_pairs={{0,1},{1,0},{2,3},{3,2},{4,5},{5,4},{6,7},{7,6},{8,9},{9,8},{10,11... | collective-permute-start | bytes 940040 | tf_op jit(solution)/shard_map/ppermute | solution.py:61
  433.5 18.8 %collective-permute-start.74 = (bf16[512,1152]{1,0:T(8,128)(2,1)S(1)}, bf16[512,1152]{1,0:T(8,128)(2,1)}, u32[]{:S(2)}, u32[]{:S(2)}) collective-permute-start(bf16[512,1152]{1,0:T(8,128)(2,1)S(1)} %copy-done.120), channel_id=1, source_target_pairs={{0,1},{1,0},{2,3},{3,2},{4,5},{5,4},{6,7},{7,6},{8,9},{9,8},{10,11... | collective-permute-start | bytes 3538952 | tf_op jit(solution)/shard_map/ppermute | solution.py:61
  433.7 16.2 %collective-permute-start.75 = (bf16[1,256,1152]{2,1,0:T(8,128)(2,1)S(1)}, bf16[1,256,1152]{2,1,0:T(8,128)(2,1)S(1)}, u32[]{:S(2)}, u32[]{:S(2)}) collective-permute-start(bf16[1,256,1152]{2,1,0:T(8,128)(2,1)S(1)} %copy-done.100), channel_id=1, source_target_pairs={{0,2},{1,3},{2,0},{3,1},{4,6},{5,7},{6,4},{7,5},{8,10},{9,11},{10,... | collective-permute-start | bytes 1769480 | tf_op jit(solution)/shard_map/ppermute | solution.py:61
  439.5 16.3 %collective-permute-start.77 = (f32[112,128]{1,0:T(8,128)}, f32[112,128]{1,0:T(8,128)}, u32[]{:S(2)}, u32[]{:S(2)}) collective-permute-start(f32[112,128]{1,0:T(8,128)} %pad_bitcast_fusion), channel_id=1, source_target_pairs={{0,1},{1,0},{2,3},{3,2},{4,5},{5,4},{6,7},{7,6},{8,9},{9,8},{10,11... | collective-permute-start | bytes 172040 | tf_op jit(solution)/shard_map/ppermute | solution.py:61
  439.7 28.1 %collective-permute-start.79 = (bf16[2,72,2816]{2,1,0:T(8,128)(2,1)}, bf16[2,72,2816]{2,1,0:T(8,128)(2,1)}, u32[]{:S(2)}, u32[]{:S(2)}) collective-permute-start(bf16[2,72,2816]{2,1,0:T(8,128)(2,1)} %fusion.16), channel_id=1, source_target_pairs={{0,8},{1,9},{2,10},{3,11},{4,12},{5,13},{6,14},{7,15},{8,16},{9,17... | collective-permute-start | bytes 2433032 | tf_op jit(solution)/shard_map/ppermute | solution.py:61
  440.0 22.1 %collective-permute-start.80 = (bf16[4,72,1024]{2,1,0:T(8,128)(2,1)}, bf16[4,72,1024]{2,1,0:T(8,128)(2,1)}, u32[]{:S(2)}, u32[]{:S(2)}) collective-permute-start(bf16[4,72,1024]{2,1,0:T(8,128)(2,1)} %get-tuple-element.1367), channel_id=1, source_target_pairs={{0,2},{1,3},{2,0},{3,1},{4,6},{5,7},{6,4},{7,5},{8,10},{9,11},{10,... | collective-permute-start | bytes 1769480 | tf_op jit(solution)/shard_map/ppermute | solution.py:61
  449.8 13.3 %collective-permute-start.81 = (bf16[4,72,896]{2,1,0:T(8,128)(2,1)}, bf16[4,72,896]{2,1,0:T(8,128)(2,1)}, u32[]{:S(2)}, u32[]{:S(2)}) collective-permute-start(bf16[4,72,896]{2,1,0:T(8,128)(2,1)} %get-tuple-element.1370), channel_id=1, source_target_pairs={{0,4},{1,5},{2,6},{3,7},{4,0},{5,1},{6,2},{7,3},{8,12},{9,13},{10,... | collective-permute-start | bytes 1548296 | tf_op jit(solution)/shard_map/ppermute | solution.py:61
  466.3 16.3 %collective-permute-start.78 = (bf16[1,256,1152]{2,1,0:T(8,128)(2,1)S(1)}, bf16[1,256,1152]{2,1,0:T(8,128)(2,1)S(1)}, u32[]{:S(2)}, u32[]{:S(2)}) collective-permute-start(bf16[1,256,1152]{2,1,0:T(8,128)(2,1)S(1)} %get-tuple-element.1362), channel_id=1, source_target_pairs={{0,2},{1,3},{2,0},{3,1},{4,6},{5,7},{6,4},{7,5},{8,10},{9,11},{10,... | collective-permute-start | bytes 1769480 | tf_op jit(solution)/shard_map/ppermute | solution.py:61
  467.8 14.8 %collective-permute-start.84 = (bf16[72,1920]{1,0:T(8,128)(2,1)S(1)}, bf16[72,1920]{1,0:T(8,128)(2,1)S(1)}, u32[]{:S(2)}, u32[]{:S(2)}) collective-permute-start(bf16[72,1920]{1,0:T(8,128)(2,1)S(1)} %fusion.64), channel_id=1, source_target_pairs={{0,8},{1,9},{2,10},{3,11},{4,12},{5,13},{6,14},{7,15},{8,16},{9,17... | collective-permute-start | bytes 829448 | tf_op jit(solution)/shard_map/ppermute | solution.py:61
  470.1 12.6 %collective-permute-start.83 = (f32[112,128]{1,0:T(8,128)S(1)}, f32[112,128]{1,0:T(8,128)S(1)}, u32[]{:S(2)}, u32[]{:S(2)}) collective-permute-start(f32[112,128]{1,0:T(8,128)S(1)} %add.525), channel_id=1, source_target_pairs={{0,4},{1,5},{2,6},{3,7},{4,0},{5,1},{6,2},{7,3},{8,12},{9,13},{10,... | collective-permute-start | bytes 172040 | tf_op jit(solution)/shard_map/ppermute | solution.py:61
  470.9 14.2 %collective-permute-start.87 = (bf16[72,1664]{1,0:T(8,128)(2,1)S(1)}, bf16[72,1664]{1,0:T(8,128)(2,1)S(1)}, u32[]{:S(2)}, u32[]{:S(2)}) collective-permute-start(bf16[72,1664]{1,0:T(8,128)(2,1)S(1)} %fusion.69), channel_id=1, source_target_pairs={{0,2},{1,3},{2,0},{3,1},{4,6},{5,7},{6,4},{7,5},{8,10},{9,11},{10,... | collective-permute-start | bytes 718856 | tf_op jit(solution)/shard_map/ppermute | solution.py:61
  472.3 12.8 %collective-permute-start.88 = (bf16[72,1152]{1,0:T(8,128)(2,1)S(1)}, bf16[72,1152]{1,0:T(8,128)(2,1)S(1)}, u32[]{:S(2)}, u32[]{:S(2)}) collective-permute-start(bf16[72,1152]{1,0:T(8,128)(2,1)S(1)} %fusion.71), channel_id=1, source_target_pairs={{0,4},{1,5},{2,6},{3,7},{4,0},{5,1},{6,2},{7,3},{8,12},{9,13},{10,... | collective-permute-start | bytes 497672 | tf_op jit(solution)/shard_map/ppermute | solution.py:61
  (165 other events, 1242.7 us)

commit v4 on v3

--- a/solution.py
+++ b/solution.py
@@ -229,8 +229,8 @@
         def step(total, *came):
             low, high = jnp.concatenate(came[:n]), jnp.concatenate(came[n : 2 * n])
             v = self.blocks(total)
-            low = pick(v[..., :cut], at.y, 1).astype(f32) + low.astype(f32)
-            high = pick(v[..., cut:], at.x, 2).astype(f32) + high.astype(f32)
+            low = pick(v, at.y, 1)[..., :cut].astype(f32) + low.astype(f32)
+            high = pick(v, at.x, 2)[..., cut:].astype(f32) + high.astype(f32)
             parts = [low, high]
             if extra:
                 mine, other = came[2 * n :]
@@ -409,7 +409,7 @@
                 jax.ShapeDtypeStruct((n, wide), bf16),
                 jax.ShapeDtypeStruct((heads, n), f32),
             ),
-            compiler_params=pltpu.CompilerParams(vmem_limit_bytes=28 * 1024 * 1024),
+            compiler_params=pltpu.CompilerParams(vmem_limit_bytes=20 * 1024 * 1024),
             cost_estimate=COST,
         )(qkv, qf, kf, *old)
     )
@@ -467,7 +467,7 @@
     return pl.pallas_call(
         functools.partial(back_kernel, first, last, wide),
         out_shape=jax.ShapeDtypeStruct(qkv.shape, bf16),
-        compiler_params=pltpu.CompilerParams(vmem_limit_bytes=36 * 1024 * 1024),
+        compiler_params=pltpu.CompilerParams(vmem_limit_bytes=26 * 1024 * 1024),
         cost_estimate=COST,
     )(qkv, do, qf, kf, lse, *old)
 
@@ -630,7 +630,7 @@
                 row,
             ],
             out_specs=[row, pl.BlockSpec((8, cols), lambda i: (0, 0))],
-            compiler_params=pltpu.CompilerParams(vmem_limit_bytes=28 * 1024 * 1024),
+            compiler_params=pltpu.CompilerParams(vmem_limit_bytes=20 * 1024 * 1024),
             cost_estimate=COST,
         )(g, w, s)
     )
@@ -652,7 +652,7 @@
                 pl.BlockSpec(b.shape, lambda i: (0, 0)),
             ],
             out_specs=[out, out],
-            compiler_params=pltpu.CompilerParams(vmem_limit_bytes=28 * 1024 * 1024),
+            compiler_params=pltpu.CompilerParams(vmem_limit_bytes=20 * 1024 * 1024),
             cost_estimate=COST,
         )(n, w, b)
     )

time: 513 us -> 506 us (0.986)
    slice x6 -> x0, local copies, waits for them, and re-layouts: 7.89 us -> none  [the longest x3 4.51 us: step(): low = pick(v[..., :cut], at.y, 1).astype(f32) + low.astype(f32)]
    unnamed x268 -> x266, local copies, waits for them, and re-layouts: 41.2 us -> 41.7 us
where the time goes in v4:
time: 506 us; the launch traced here: 499 us
  waiting for transfers between devices  150 us (30%)
  Pallas kernels  85.5 us (17%)
  starting transfers between devices  78.4 us (15%)
  local copies, waits for them, and re-layouts  76.7 us (15%)
  matrix products  58.2 us (12%)
  other arithmetic  46.9 us (9%)
    ppermute x93, waiting for transfers between devices, send(): return lax.ppermute(value, AXES, pairs)  150 us
    ppermute x93, starting transfers between devices, send(): return lax.ppermute(value, AXES, pairs)  78.4 us
    dot_general x24, matrix products, dot(): return lax.dot_general(a, b, dims, preferred_element_type=f32).astype(out)  58.2 us
    unnamed x266, local copies, waits for them, and re-layouts  41.7 us
    pallas_call x2, Pallas kernels, attend_back(): pl.pallas_call(functools.partial(back_kernel, first, last, wide), out_sha...  33.4 us
    pallas_call x2, Pallas kernels, attend(): pl.pallas_call(functools.partial(attend_kernel, first, last, wide), out_s...  16.6 us
  transfers between devices with their start and end apart: 93, of which 36 were waited for; matrix products, arithmetic and copies ran while one was open for 22% of the time, Pallas kernels for 16%

profile of v4, /device:TPU:0, one launch (start us, length us, event | category | flops | bytes accessed | tf_op | source)
XLA Modules:
  0.0 498.6 jit_solution(14332834068048138859)
XLA Ops:
  7.5 2.9 collective-permute-start.1
  13.8 7.7 %collective-permute-done.3.refs_5_ = bf16[72,1920]{1,0:T(8,128)(2,1)S(1)} collective-permute-done((bf16[72,1920]{1,0:T(8,128)(2,1)S(1)}, bf16[72,1920]{1,0:T(8,128)(2,1)S(1)}, u32[]{:S(2)}, u32[]{:S(2)}) %collective-permute-start.3) | collective-permute-done | bytes 276512 | tf_op jit(solution)/shard_map/ppermute | solution.py:61
  29.9 3.0 collective-permute-done.6.refs_9_
  33.5 2.2 collective-permute-done.4.refs_2_
  35.8 3.6 collective-permute-done.11
  52.3 10.9 %collective-permute-done.17.refs_6_ = bf16[2,72,2816]{2,1,0:T(8,128)(2,1)S(1)} collective-permute-done((bf16[2,72,2816]{2,1,0:T(8,128)(2,1)S(1)}, bf16[2,72,2816]{2,1,0:T(8,128)(2,1)S(1)}, u32[]{:S(2)}, u32[]{:S(2)}) %collective-permute-start.17) | collective-permute-done | bytes 811040 | tf_op jit(solution)/shard_map/ppermute | solution.py:61
  73.0 3.2 collective-permute-done.19.refs_8_
  76.3 5.9 %collective-permute-done.20.refs_12_ = bf16[72,1920]{1,0:T(8,128)(2,1)S(1)} collective-permute-done((bf16[72,1920]{1,0:T(8,128)(2,1)}, bf16[72,1920]{1,0:T(8,128)(2,1)S(1)}, u32[]{:S(2)}, u32[]{:S(2)}) %collective-permute-start.20) | collective-permute-done | bytes 276512 | tf_op jit(solution)/shard_map/ppermute | solution.py:61
  82.2 5.4 %collective-permute-done.21.refs_16_ = bf16[72,1920]{1,0:T(8,128)(2,1)S(1)} collective-permute-done((bf16[72,1920]{1,0:T(8,128)(2,1)}, bf16[72,1920]{1,0:T(8,128)(2,1)S(1)}, u32[]{:S(2)}, u32[]{:S(2)}) %collective-permute-start.21) | collective-permute-done | bytes 276512 | tf_op jit(solution)/shard_map/ppermute | solution.py:61
  87.6 4.0 collective-permute-done.22.refs_7_
  93.4 2.1 copy-done.20
  97.9 4.0 add_convert_fusion.1
  104.9 4.2 collective-permute-done.26
  115.5 8.3 %add_convert_fusion.qkv_ref = bf16[1024,1920]{1,0:T(8,128)(2,1)S(1)} fusion(f32[1920]{0:T(1024)S(1)} %reduce.2, bf16[1024,1152]{1,0:T(8,128)(2,1)} %add_convert_fusion.1, bf16[1152,1920]{1,0:T(8,128)(2,1)} %bitcast.289), kind=kOutput, calls=%fused_computation.3 | convolution fusion | flops 4533780480 | bytes 10722816 | tf_op jit(solution)/shard_map/dot_general | solution.py:26
  132.5 8.3 %shard_map.306 = (bf16[1024,640]{1,0:T(8,128)(2,1)S(1)}, f32[8,1024]{1,0:T(8,128)S(1)}) custom-call(bf16[1024,1920]{1,0:T(8,128)(2,1)S(1)} %add_convert_fusion.qkv_ref, bf16[1024,256]{1,0:T(8,128)(2,1)S(1)} %compare_convert_fusion.qf_ref, bf16[1024,256]{1,0:T(8,128)(2,1)S(1)} %copy-done.16, bf16[16,128]{1,0:T(8,128)(2,1)S(1)} %broadcast_12_old_ref.2.old_ref, ...), custom_call_target="tpu_custom_call" | custom-call | flops 5000000000 | bytes 10000000 | tf_op jit(solution)/shard_map/pallas_call | solution.py:406
  144.6 8.4 %shard_map.307 = (bf16[1024,640]{1,0:T(8,128)(2,1)S(1)}, f32[8,1024]{1,0:T(8,128)S(1)}) custom-call(bf16[1024,1920]{1,0:T(8,128)(2,1)S(1)} %add_convert_fusion.qkv_ref, bf16[1024,256]{1,0:T(8,128)(2,1)S(1)} %compare_convert_fusion.qf_ref, bf16[1024,256]{1,0:T(8,128)(2,1)S(1)} %copy-done.16, bf16[1024,640]{1,0:T(8,128)(2,1)S(1)} %get-tuple-element.933.old_ref, ...), custom_call_target="tpu_custom_call" | custom-call | flops 5000000000 | bytes 10000000 | tf_op jit(solution)/shard_map/pallas_call | solution.py:406
  153.0 2.0 copy-done.74
  155.0 2.0 collective-permute-done.32.refs_8_
  168.9 3.0 shard_map.308
  172.0 4.6 collective-permute-done.38.refs_9_
  184.6 5.4 %shard_map.309 = (f32[512,1152]{1,0:T(8,128)S(1)}, bf16[512,1152]{1,0:T(8,128)(2,1)S(1)}) custom-call(s32[1]{0:T(128)} %bitcast.core_ref, bf16[512,1152]{1,0:T(8,128)(2,1)S(1)} %bitcast.281, bf16[512,640]{1,0:T(8,128)(2,1)S(1)} %get-tuple-element.1188.a_ref, bf16[512,640]{1,0:T(8,128)(2,1)} %collective-permute-done.35.b_ref, ...), custom_call_target="tpu_custom_call" | custom-call | flops 5000000000 | bytes 10000000 | tf_op jit(solution)/shard_map/pallas_call | solution.py:516
  192.2 8.0 %collective-permute-done.41.refs_4_ = bf16[2,2,72,1280]{3,2,1,0:T(8,128)(2,1)S(1)} collective-permute-done((bf16[2,2,72,1280]{3,2,1,0:T(8,128)(2,1)S(1)}, bf16[2,2,72,1280]{3,2,1,0:T(8,128)(2,1)S(1)}, u32[]{:S(2)}, u32[]{:S(2)}) %collective-permute-start.41) | collective-permute-done | bytes 737312 | tf_op jit(solution)/shard_map/ppermute | solution.py:61
  204.1 9.0 %shard_map.310 = (bf16[1024,2176]{1,0:T(8,128)(2,1)S(1)}, bf16[1024,2176]{1,0:T(8,128)(2,1)S(1)}) custom-call(bf16[1024,1152]{1,0:T(8,128)(2,1)S(1)} %pad_maximum_fusion.3.n_ref, bf16[1152,2176]{1,0:T(8,128)(2,1)S(1)} %bitcast.297, f32[1,2176]{1,0:T(1,128)S(1)} %broadcast_select_fusion.14.b_ref), custom_call_target="tpu_custom_call" | custom-call | flops 5000000000 | bytes 10000000 | tf_op jit(solution)/shard_map/pallas_call | solution.py:645
  213.1 2.3 copy-done.73
  215.4 2.1 copy-done.76
  217.5 2.0 copy-done.77
  222.0 2.5 fusion.96
  226.4 2.7 shard_map.311
  231.8 6.2 %convolution_convert_fusion.1 = bf16[1152,2176]{1,0:T(8,128)(2,1)S(1)} fusion(bf16[1024,1152]{1,0:T(8,128)(2,1)S(1)} %pad_maximum_fusion.4.g_ref, bf16[1024,2176]{1,0:T(8,128)(2,1)S(1)} %copy-done.78), kind=kOutput, calls=%fused_computation.1 | convolution fusion | flops 5136334848 | bytes 11829248 | tf_op jit(solution)/shard_map/dot_general | solution.py:26
  238.2 2.3 copy-done.80
  243.6 7.3 %shard_map.312 = (bf16[1024,2176]{1,0:T(8,128)(2,1)S(1)}, f32[8,2176]{1,0:T(8,128)S(1)}) custom-call(bf16[1024,1152]{1,0:T(8,128)(2,1)S(1)} %pad_maximum_fusion.4.g_ref, bf16[1152,2176]{1,0:T(8,128)(2,1)S(1)} %bitcast.294, bf16[1024,2176]{1,0:T(8,128)(2,1)S(1)} %bitcast.303), custom_call_target="tpu_custom_call" | custom-call | flops 5000000000 | bytes 10000000 | tf_op jit(solution)/shard_map/pallas_call | solution.py:620
  250.9 2.6 collective-permute-done.49
  253.5 3.2 convolution_convert_fusion.8
  259.0 3.2 fusion.5.t_ref
  262.3 4.8 collective-permute-done.51
  271.1 7.5 %convolution_convert_fusion = bf16[1152,2176]{1,0:T(8,128)(2,1)} fusion(bf16[1024,1152]{1,0:T(8,128)(2,1)S(1)} %copy-done.3, bf16[1024,2176]{1,0:T(8,128)(2,1)S(1)} %get-tuple-element.1109), kind=kOutput, calls=%fused_computation | convolution fusion | flops 5136334848 | bytes 11829248 | tf_op jit(solution)/shard_map/dot_general | solution.py:26
  278.6 2.4 collective-permute-done.54
  281.0 2.8 shard_map.313
  287.2 1.9 fusion.103
  290.8 3.2 collective-permute-done.55
  294.0 2.5 collective-permute-done.56
  299.5 1.8 slice-done.8
  310.6 12.2 %collective-permute-done.59 = bf16[2,72,2176]{2,1,0:T(8,128)(2,1)S(1)} collective-permute-done((bf16[2,72,2176]{2,1,0:T(8,128)(2,1)}, bf16[2,72,2176]{2,1,0:T(8,128)(2,1)S(1)}, u32[]{:S(2)}, u32[]{:S(2)}) %collective-permute-start.59) | collective-permute-done | bytes 626720 | tf_op jit(solution)/shard_map/ppermute | solution.py:61
  322.8 6.7 %collective-permute-done.61 = bf16[2,2,72,1664]{3,2,1,0:T(8,128)(2,1)S(1)} collective-permute-done((bf16[2,2,72,1664]{3,2,1,0:T(8,128)(2,1)S(1)}, bf16[2,2,72,1664]{3,2,1,0:T(8,128)(2,1)S(1)}, u32[]{:S(2)}, u32[]{:S(2)}) %collective-permute-start.61) | collective-permute-done | bytes 958496 | tf_op jit(solution)/shard_map/ppermute | solution.py:61
  332.4 1.9 collective-permute-start.63
  335.7 16.7 %shard_map.314.old_ref = bf16[1024,1920]{1,0:T(8,128)(2,1)S(1)} custom-call(bf16[1024,1920]{1,0:T(8,128)(2,1)S(1)} %copy-done.75, bf16[1024,640]{1,0:T(8,128)(2,1)S(1)} %pad_maximum_fusion.8.do_ref, bf16[1024,256]{1,0:T(8,128)(2,1)S(1)} %copy-done.15, bf16[1024,256]{1,0:T(8,128)(2,1)S(1)} %copy-done.17, f32[8,1024]{1,0:T(8,128)S(1)} %get-tuple-element.1248.lse_ref, ...), custom_call_target="tpu_custom_call" | custom-call | flops 5000000000 | bytes 10000000 | tf_op jit(solution)/shard_map/pallas_call | solution.py:467
  355.0 1.9 collective-permute-start.67
  356.9 16.7 %shard_map.315 = bf16[1024,1920]{1,0:T(8,128)(2,1)S(1)} custom-call(bf16[1024,1920]{1,0:T(8,128)(2,1)S(1)} %copy-done.75, bf16[1024,640]{1,0:T(8,128)(2,1)S(1)} %pad_maximum_fusion.8.do_ref, bf16[1024,256]{1,0:T(8,128)(2,1)S(1)} %copy-done.15, bf16[1024,256]{1,0:T(8,128)(2,1)S(1)} %copy-done.17, f32[8,1024]{1,0:T(8,128)S(1)} %get-tuple-element.1248.lse_ref, ...), custom_call_target="tpu_custom_call" | custom-call | flops 5000000000 | bytes 10000000 | tf_op jit(solution)/shard_map/pallas_call | solution.py:467
  373.6 2.1 collective-permute-start.66
  378.7 5.8 %convolution_convert_fusion.2 = bf16[1152,1920]{1,0:T(8,128)(2,1)S(1)} fusion(bf16[1024,1152]{1,0:T(8,128)(2,1)S(1)} %copy-done.88, bf16[1024,1920]{1,0:T(8,128)(2,1)S(1)} %shard_map.315), kind=kOutput, calls=%fused_computation.4 | convolution fusion | flops 4532060160 | bytes 10715136 | tf_op jit(solution)/shard_map/dot_general | solution.py:26
  384.5 2.9 convolution_convert_fusion.6
  395.1 2.9 fusion.8.t_ref
  399.1 3.5 shard_map.316
  403.5 4.2 convolution_convert_fusion.7
  407.8 4.7 fusion.2
  412.5 8.0 %collective-permute-done.73 = bf16[4,2,72,1024]{3,2,1,0:T(8,128)(2,1)S(1)} collective-permute-done((bf16[4,2,72,1024]{3,2,1,0:T(8,128)(2,1)S(1)}, bf16[4,2,72,1024]{3,2,1,0:T(8,128)(2,1)S(1)}, u32[]{:S(2)}, u32[]{:S(2)}) %collective-permute-start.73) | collective-permute-done | bytes 1179680 | tf_op jit(solution)/shard_map/ppermute | solution.py:61
  424.4 1.9 dynamic-slice_bitcast_fusion.4
  430.0 2.2 fusion.11
  436.1 6.8 %collective-permute-done.75 = bf16[1,256,1152]{2,1,0:T(8,128)(2,1)S(1)} collective-permute-done((bf16[1,256,1152]{2,1,0:T(8,128)(2,1)}, bf16[1,256,1152]{2,1,0:T(8,128)(2,1)S(1)}, u32[]{:S(2)}, u32[]{:S(2)}) %collective-permute-start.75) | collective-permute-done | bytes 589856 | tf_op jit(solution)/shard_map/ppermute | solution.py:61
  446.4 2.4 add_convert_fusion.4
  449.9 5.3 %collective-permute-done.80 = bf16[4,72,1024]{2,1,0:T(8,128)(2,1)} collective-permute-done((bf16[4,72,1024]{2,1,0:T(8,128)(2,1)}, bf16[4,72,1024]{2,1,0:T(8,128)(2,1)}, u32[]{:S(2)}, u32[]{:S(2)}) %collective-permute-start.80) | collective-permute-done | bytes 589856 | tf_op jit(solution)/shard_map/ppermute | solution.py:61
  465.9 9.8 %collective-permute-done.78 = bf16[1,256,1152]{2,1,0:T(8,128)(2,1)S(1)} collective-permute-done((bf16[1,256,1152]{2,1,0:T(8,128)(2,1)S(1)}, bf16[1,256,1152]{2,1,0:T(8,128)(2,1)S(1)}, u32[]{:S(2)}, u32[]{:S(2)}) %collective-permute-start.78) | collective-permute-done | bytes 589856 | tf_op jit(solution)/shard_map/ppermute | solution.py:61
  479.8 5.5 %collective-permute-done.86 = bf16[72,1920]{1,0:T(8,128)(2,1)S(1)} collective-permute-done((bf16[72,1920]{1,0:T(8,128)(2,1)S(1)}, bf16[72,1920]{1,0:T(8,128)(2,1)S(1)}, u32[]{:S(2)}, u32[]{:S(2)}) %collective-permute-start.86) | collective-permute-done | bytes 276512 | tf_op jit(solution)/shard_map/ppermute | solution.py:61
  486.6 7.2 %collective-permute-done.90 = bf16[72,1920]{1,0:T(8,128)(2,1)S(1)} collective-permute-done((bf16[72,1920]{1,0:T(8,128)(2,1)S(1)}, bf16[72,1920]{1,0:T(8,128)(2,1)S(1)}, u32[]{:S(2)}, u32[]{:S(2)}) %collective-permute-start.90) | collective-permute-done | bytes 276512 | tf_op jit(solution)/shard_map/ppermute | solution.py:61
  (625 shorter events, 182.5 us)
Async XLA Ops:
  7.5 16.6 %collective-permute-start.1 = (bf16[1,256,1152]{2,1,0:T(8,128)(2,1)S(1)}, bf16[1,256,1152]{2,1,0:T(8,128)(2,1)S(1)}, u32[]{:S(2)}, u32[]{:S(2)}) collective-permute-start(bf16[1,256,1152]{2,1,0:T(8,128)(2,1)S(1)} %dynamic-slice_bitcast_fusion.18), channel_id=1, source_target_pairs={{0,2},{1,3},{2,0},{3,1},{4,6},{5,7},{6,4},{7,5},{8,10},{9,11},{10,... | collective-permute-start | bytes 1769480 | tf_op jit(solution)/shard_map/ppermute | solution.py:61
  10.6 13.5 %collective-permute-start.7 = (bf16[36,4992]{1,0:T(8,128)(2,1)S(1)}, bf16[36,4992]{1,0:T(8,128)(2,1)S(1)}, u32[]{:S(2)}, u32[]{:S(2)}) collective-permute-start(bf16[36,4992]{1,0:T(8,128)(2,1)S(1)} %get-tuple-element.767), channel_id=1, source_target_pairs={{0,1},{1,0},{2,3},{3,2},{4,5},{5,4},{6,7},{7,6},{8,9},{9,8},{10,11... | collective-permute-start | bytes 1078280 | tf_op jit(solution)/shard_map/ppermute | solution.py:61
  10.7 10.9 %collective-permute-start.3 = (bf16[72,1920]{1,0:T(8,128)(2,1)S(1)}, bf16[72,1920]{1,0:T(8,128)(2,1)S(1)}, u32[]{:S(2)}, u32[]{:S(2)}) collective-permute-start(bf16[72,1920]{1,0:T(8,128)(2,1)S(1)} %convolution_convert_fusion.9.refs_1_), channel_id=1, source_target_pairs={{0,8},{1,9},{2,10},{3,11},{4,12},{5,13},{6,14},{7,15},{8,16},{9,17... | collective-permute-start | bytes 829448 | tf_op jit(solution)/shard_map/ppermute | solution.py:61
  21.6 11.3 %collective-permute-start.5 = (bf16[72,1920]{1,0:T(8,128)(2,1)S(1)}, bf16[72,1920]{1,0:T(8,128)(2,1)S(1)}, u32[]{:S(2)}, u32[]{:S(2)}) collective-permute-start(bf16[72,1920]{1,0:T(8,128)(2,1)S(1)} %collective-permute-done.3.refs_5_), channel_id=1, source_target_pairs={{0,4},{1,5},{2,6},{3,7},{4,0},{5,1},{6,2},{7,3},{8,12},{9,13},{10,... | collective-permute-start | bytes 829448 | tf_op jit(solution)/shard_map/ppermute | solution.py:61
  27.9 11.5 %collective-permute-start.11 = (bf16[72,1664]{1,0:T(8,128)(2,1)S(1)}, bf16[72,1664]{1,0:T(8,128)(2,1)S(1)}, u32[]{:S(2)}, u32[]{:S(2)}) collective-permute-start(bf16[72,1664]{1,0:T(8,128)(2,1)S(1)} %slice.560), channel_id=1, source_target_pairs={{0,2},{1,3},{2,0},{3,1},{4,6},{5,7},{6,4},{7,5},{8,10},{9,11},{10,... | collective-permute-start | bytes 718856 | tf_op jit(solution)/shard_map/ppermute | solution.py:61
  28.2 11.3 %collective-permute-start.12 = (bf16[72,1152]{1,0:T(8,128)(2,1)S(1)}, bf16[72,1152]{1,0:T(8,128)(2,1)S(1)}, u32[]{:S(2)}, u32[]{:S(2)}) collective-permute-start(bf16[72,1152]{1,0:T(8,128)(2,1)S(1)} %slice.561), channel_id=1, source_target_pairs={{0,4},{1,5},{2,6},{3,7},{4,0},{5,1},{6,2},{7,3},{8,12},{9,13},{10,... | collective-permute-start | bytes 497672 | tf_op jit(solution)/shard_map/ppermute | solution.py:61
  32.9 11.9 %collective-permute-start.9 = (bf16[72,1920]{1,0:T(8,128)(2,1)S(1)}, bf16[72,1920]{1,0:T(8,128)(2,1)S(1)}, u32[]{:S(2)}, u32[]{:S(2)}) collective-permute-start(bf16[72,1920]{1,0:T(8,128)(2,1)S(1)} %collective-permute-done.6.refs_9_), channel_id=1, source_target_pairs={{0,4},{1,5},{2,6},{3,7},{4,0},{5,1},{6,2},{7,3},{8,12},{9,13},{10,... | collective-permute-start | bytes 829448 | tf_op jit(solution)/shard_map/ppermute | solution.py:61
  43.3 19.9 %collective-permute-start.17 = (bf16[2,72,2816]{2,1,0:T(8,128)(2,1)S(1)}, bf16[2,72,2816]{2,1,0:T(8,128)(2,1)S(1)}, u32[]{:S(2)}, u32[]{:S(2)}) collective-permute-start(bf16[2,72,2816]{2,1,0:T(8,128)(2,1)S(1)} %pad_maximum_fusion.13.refs_1_), channel_id=1, source_target_pairs={{0,8},{1,9},{2,10},{3,11},{4,12},{5,13},{6,14},{7,15},{8,16},{9,17... | collective-permute-start | bytes 2433032 | tf_op jit(solution)/shard_map/ppermute | solution.py:61
  44.9 18.3 %collective-permute-start.16 = (bf16[72,1920]{1,0:T(8,128)(2,1)}, bf16[72,1920]{1,0:T(8,128)(2,1)S(1)}, u32[]{:S(2)}, u32[]{:S(2)}) collective-permute-start(bf16[72,1920]{1,0:T(8,128)(2,1)} %copy-done.57), channel_id=1, source_target_pairs={{0,4},{1,5},{2,6},{3,7},{4,0},{5,1},{6,2},{7,3},{8,12},{9,13},{10,... | collective-permute-start | bytes 829448 | tf_op jit(solution)/shard_map/ppermute | solution.py:61
  47.6 16.3 %collective-permute-start.13 = (bf16[72,1920]{1,0:T(8,128)(2,1)}, bf16[72,1920]{1,0:T(8,128)(2,1)S(1)}, u32[]{:S(2)}, u32[]{:S(2)}) collective-permute-start(bf16[72,1920]{1,0:T(8,128)(2,1)} %collective-permute-done.4.refs_2_), channel_id=1, source_target_pairs={{0,4},{1,5},{2,6},{3,7},{4,0},{5,1},{6,2},{7,3},{8,12},{9,13},{10,... | collective-permute-start | bytes 829448 | tf_op jit(solution)/shard_map/ppermute | solution.py:61
  48.8 15.2 %collective-permute-start.14 = (bf16[72,1920]{1,0:T(8,128)(2,1)}, bf16[72,1920]{1,0:T(8,128)(2,1)S(1)}, u32[]{:S(2)}, u32[]{:S(2)}) collective-permute-start(bf16[72,1920]{1,0:T(8,128)(2,1)} %copy-done.57), channel_id=1, source_target_pairs={{0,2},{1,3},{2,0},{3,1},{4,6},{5,7},{6,4},{7,5},{8,10},{9,11},{10,... | collective-permute-start | bytes 829448 | tf_op jit(solution)/shard_map/ppermute | solution.py:61
  50.2 13.7 %collective-permute-start.15 = (bf16[72,1920]{1,0:T(8,128)(2,1)S(1)}, bf16[72,1920]{1,0:T(8,128)(2,1)S(1)}, u32[]{:S(2)}, u32[]{:S(2)}) collective-permute-start(bf16[72,1920]{1,0:T(8,128)(2,1)S(1)} %collective-permute-done.6.refs_9_), channel_id=1, source_target_pairs={{0,2},{1,3},{2,0},{3,1},{4,6},{5,7},{6,4},{7,5},{8,10},{9,11},{10,... | collective-permute-start | bytes 829448 | tf_op jit(solution)/shard_map/ppermute | solution.py:61
  68.1 14.0 %collective-permute-start.20 = (bf16[72,1920]{1,0:T(8,128)(2,1)}, bf16[72,1920]{1,0:T(8,128)(2,1)S(1)}, u32[]{:S(2)}, u32[]{:S(2)}) collective-permute-start(bf16[72,1920]{1,0:T(8,128)(2,1)} %copy-done.67), channel_id=1, source_target_pairs={{0,4},{1,5},{2,6},{3,7},{4,0},{5,1},{6,2},{7,3},{8,12},{9,13},{10,... | collective-permute-start | bytes 829448 | tf_op jit(solution)/shard_map/ppermute | solution.py:61
  68.6 18.9 %collective-permute-start.21 = (bf16[72,1920]{1,0:T(8,128)(2,1)}, bf16[72,1920]{1,0:T(8,128)(2,1)S(1)}, u32[]{:S(2)}, u32[]{:S(2)}) collective-permute-start(bf16[72,1920]{1,0:T(8,128)(2,1)} %copy-done.65), channel_id=1, source_target_pairs={{0,4},{1,5},{2,6},{3,7},{4,0},{5,1},{6,2},{7,3},{8,12},{9,13},{10,... | collective-permute-start | bytes 829448 | tf_op jit(solution)/shard_map/ppermute | solution.py:61
  70.2 21.4 %collective-permute-start.22 = (bf16[2,72,2816]{2,1,0:T(8,128)(2,1)S(1)}, bf16[2,72,2816]{2,1,0:T(8,128)(2,1)}, u32[]{:S(2)}, u32[]{:S(2)}) collective-permute-start(bf16[2,72,2816]{2,1,0:T(8,128)(2,1)S(1)} %collective-permute-done.17.refs_6_), channel_id=1, source_target_pairs={{0,8},{1,9},{2,10},{3,11},{4,12},{5,13},{6,14},{7,15},{8,16},{9,17... | collective-permute-start | bytes 2433032 | tf_op jit(solution)/shard_map/ppermute | solution.py:61
  96.4 15.2 %collective-permute-start.23 = (bf16[2,72,1664]{2,1,0:T(8,128)(2,1)}, bf16[2,72,1664]{2,1,0:T(8,128)(2,1)S(1)}, u32[]{:S(2)}, u32[]{:S(2)}) collective-permute-start(bf16[2,72,1664]{2,1,0:T(8,128)(2,1)} %fusion.42), channel_id=1, source_target_pairs={{0,4},{1,5},{2,6},{3,7},{4,0},{5,1},{6,2},{7,3},{8,12},{9,13},{10,... | collective-permute-start | bytes 1437704 | tf_op jit(solution)/shard_map/ppermute | solution.py:61
  97.0 13.9 %collective-permute-start.24 = (bf16[2,72,1152]{2,1,0:T(8,128)(2,1)}, bf16[2,72,1152]{2,1,0:T(8,128)(2,1)S(1)}, u32[]{:S(2)}, u32[]{:S(2)}) collective-permute-start(bf16[2,72,1152]{2,1,0:T(8,128)(2,1)} %fusion.48), channel_id=1, source_target_pairs={{0,2},{1,3},{2,0},{3,1},{4,6},{5,7},{6,4},{7,5},{8,10},{9,11},{10,... | collective-permute-start | bytes 995336 | tf_op jit(solution)/shard_map/ppermute | solution.py:61
  104.7 19.8 %collective-permute-start.27 = (bf16[2,72,2816]{2,1,0:T(8,128)(2,1)}, bf16[2,72,2816]{2,1,0:T(8,128)(2,1)}, u32[]{:S(2)}, u32[]{:S(2)}) collective-permute-start(bf16[2,72,2816]{2,1,0:T(8,128)(2,1)} %collective-permute-done.22.refs_7_), channel_id=1, source_target_pairs={{0,8},{1,9},{2,10},{3,11},{4,12},{5,13},{6,14},{7,15},{8,16},{9,17... | collective-permute-start | bytes 2433032 | tf_op jit(solution)/shard_map/ppermute | solution.py:61
  114.0 10.8 %collective-permute-start.28 = (bf16[1,2,72,1664]{3,2,1,0:T(8,128)(2,1)}, bf16[1,2,72,1664]{3,2,1,0:T(8,128)(2,1)S(1)}, u32[]{:S(2)}, u32[]{:S(2)}) collective-permute-start(bf16[1,2,72,1664]{3,2,1,0:T(8,128)(2,1)} %slice_bitcast_fusion.2), channel_id=1, source_target_pairs={{0,4},{1,5},{2,6},{3,7},{4,0},{5,1},{6,2},{7,3},{8,12},{9,13},{10,... | collective-permute-start | bytes 1437704 | tf_op jit(solution)/shard_map/ppermute | solution.py:61
  130.7 10.9 %collective-permute-start.30 = (bf16[1,2,72,1664]{3,2,1,0:T(8,128)(2,1)S(1)}, bf16[1,2,72,1664]{3,2,1,0:T(8,128)(2,1)S(1)}, u32[]{:S(2)}, u32[]{:S(2)}) collective-permute-start(bf16[1,2,72,1664]{3,2,1,0:T(8,128)(2,1)S(1)} %slice_bitcast_fusion.1), channel_id=1, source_target_pairs={{0,4},{1,5},{2,6},{3,7},{4,0},{5,1},{6,2},{7,3},{8,12},{9,13},{10,... | collective-permute-start | bytes 1437704 | tf_op jit(solution)/shard_map/ppermute | solution.py:61
  142.4 14.6 %collective-permute-start.32 = (bf16[2,72,2176]{2,1,0:T(8,128)(2,1)S(1)}, bf16[2,72,2176]{2,1,0:T(8,128)(2,1)}, u32[]{:S(2)}, u32[]{:S(2)}) collective-permute-start(bf16[2,72,2176]{2,1,0:T(8,128)(2,1)S(1)} %pad_maximum_fusion.15.refs_1_), channel_id=1, source_target_pairs={{0,8},{1,9},{2,10},{3,11},{4,12},{5,13},{6,14},{7,15},{8,16},{9,17... | collective-permute-start | bytes 1880072 | tf_op jit(solution)/shard_map/ppermute | solution.py:61
  142.4 12.6 %collective-permute-start.33 = (bf16[1,2,72,1664]{3,2,1,0:T(8,128)(2,1)S(1)}, bf16[1,2,72,1664]{3,2,1,0:T(8,128)(2,1)S(1)}, u32[]{:S(2)}, u32[]{:S(2)}) collective-permute-start(bf16[1,2,72,1664]{3,2,1,0:T(8,128)(2,1)S(1)} %slice_bitcast_fusion), channel_id=1, source_target_pairs={{0,4},{1,5},{2,6},{3,7},{4,0},{5,1},{6,2},{7,3},{8,12},{9,13},{10,... | collective-permute-start | bytes 1437704 | tf_op jit(solution)/shard_map/ppermute | solution.py:61
  143.1 11.8 %collective-permute-start.34 = (bf16[1,2,72,1152]{3,2,1,0:T(8,128)(2,1)S(1)}, bf16[1,2,72,1152]{3,2,1,0:T(8,128)(2,1)S(1)}, u32[]{:S(2)}, u32[]{:S(2)}) collective-permute-start(bf16[1,2,72,1152]{3,2,1,0:T(8,128)(2,1)S(1)} %slice_bitcast_fusion.6), channel_id=1, source_target_pairs={{0,2},{1,3},{2,0},{3,1},{4,6},{5,7},{6,4},{7,5},{8,10},{9,11},{10,... | collective-permute-start | bytes 995336 | tf_op jit(solution)/shard_map/ppermute | solution.py:61
  157.9 18.6 %collective-permute-start.38 = (bf16[2,72,2176]{2,1,0:T(8,128)(2,1)}, bf16[2,72,2176]{2,1,0:T(8,128)(2,1)}, u32[]{:S(2)}, u32[]{:S(2)}) collective-permute-start(bf16[2,72,2176]{2,1,0:T(8,128)(2,1)} %collective-permute-done.32.refs_8_), channel_id=1, source_target_pairs={{0,8},{1,9},{2,10},{3,11},{4,12},{5,13},{6,14},{7,15},{8,16},{9,17... | collective-permute-start | bytes 1880072 | tf_op jit(solution)/shard_map/ppermute | solution.py:61
  158.9 17.7 %collective-permute-start.37 = (bf16[1,256,1152]{2,1,0:T(8,128)(2,1)}, bf16[1,256,1152]{2,1,0:T(8,128)(2,1)}, u32[]{:S(2)}, u32[]{:S(2)}) collective-permute-start(bf16[1,256,1152]{2,1,0:T(8,128)(2,1)} %dynamic-slice_bitcast_fusion.17), channel_id=1, source_target_pairs={{0,2},{1,3},{2,0},{3,1},{4,6},{5,7},{6,4},{7,5},{8,10},{9,11},{10,... | collective-permute-start | bytes 1769480 | tf_op jit(solution)/shard_map/ppermute | solution.py:61
  159.7 16.9 %collective-permute-start.36 = (bf16[2,72,1280]{2,1,0:T(8,128)(2,1)}, bf16[2,72,1280]{2,1,0:T(8,128)(2,1)S(1)}, u32[]{:S(2)}, u32[]{:S(2)}) collective-permute-start(bf16[2,72,1280]{2,1,0:T(8,128)(2,1)} %fusion.47), channel_id=1, source_target_pairs={{0,4},{1,5},{2,6},{3,7},{4,0},{5,1},{6,2},{7,3},{8,12},{9,13},{10,... | collective-permute-start | bytes 1105928 | tf_op jit(solution)/shard_map/ppermute | solution.py:61
  181.0 20.1 %collective-permute-start.40 = (bf16[2,72,2176]{2,1,0:T(8,128)(2,1)}, bf16[2,72,2176]{2,1,0:T(8,128)(2,1)S(1)}, u32[]{:S(2)}, u32[]{:S(2)}) collective-permute-start(bf16[2,72,2176]{2,1,0:T(8,128)(2,1)} %collective-permute-done.38.refs_9_), channel_id=1, source_target_pairs={{0,8},{1,9},{2,10},{3,11},{4,12},{5,13},{6,14},{7,15},{8,16},{9,17... | collective-permute-start | bytes 1880072 | tf_op jit(solution)/shard_map/ppermute | solution.py:61
  181.3 19.0 %collective-permute-start.41 = (bf16[2,2,72,1280]{3,2,1,0:T(8,128)(2,1)S(1)}, bf16[2,2,72,1280]{3,2,1,0:T(8,128)(2,1)S(1)}, u32[]{:S(2)}, u32[]{:S(2)}) collective-permute-start(bf16[2,2,72,1280]{3,2,1,0:T(8,128)(2,1)S(1)} %pad_maximum_fusion.16), channel_id=1, source_target_pairs={{0,4},{1,5},{2,6},{3,7},{4,0},{5,1},{6,2},{7,3},{8,12},{9,13},{10,... | collective-permute-start | bytes 2211848 | tf_op jit(solution)/shard_map/ppermute | solution.py:61
  201.2 18.3 %collective-permute-start.44 = (bf16[2,2,72,896]{3,2,1,0:T(8,128)(2,1)S(1)}, bf16[2,2,72,896]{3,2,1,0:T(8,128)(2,1)S(1)}, u32[]{:S(2)}, u32[]{:S(2)}) collective-permute-start(bf16[2,2,72,896]{3,2,1,0:T(8,128)(2,1)S(1)} %pad_maximum_fusion.20), channel_id=1, source_target_pairs={{0,2},{1,3},{2,0},{3,1},{4,6},{5,7},{6,4},{7,5},{8,10},{9,11},{10,... | collective-permute-start | bytes 1548296 | tf_op jit(solution)/shard_map/ppermute | solution.py:61
  201.9 18.4 %collective-permute-start.45 = (bf16[1,2,72,1280]{3,2,1,0:T(8,128)(2,1)S(1)}, bf16[1,2,72,1280]{3,2,1,0:T(8,128)(2,1)S(1)}, u32[]{:S(2)}, u32[]{:S(2)}) collective-permute-start(bf16[1,2,72,1280]{3,2,1,0:T(8,128)(2,1)S(1)} %slice_bitcast_fusion.3), channel_id=1, source_target_pairs={{0,4},{1,5},{2,6},{3,7},{4,0},{5,1},{6,2},{7,3},{8,12},{9,13},{10,... | collective-permute-start | bytes 1105928 | tf_op jit(solution)/shard_map/ppermute | solution.py:61
  203.1 18.0 %collective-permute-start.46 = (bf16[1,2,72,896]{3,2,1,0:T(8,128)(2,1)S(1)}, bf16[1,2,72,896]{3,2,1,0:T(8,128)(2,1)S(1)}, u32[]{:S(2)}, u32[]{:S(2)}) collective-permute-start(bf16[1,2,72,896]{3,2,1,0:T(8,128)(2,1)S(1)} %slice_bitcast_fusion.9), channel_id=1, source_target_pairs={{0,2},{1,3},{2,0},{3,1},{4,6},{5,7},{6,4},{7,5},{8,10},{9,11},{10,... | collective-permute-start | bytes 774152 | tf_op jit(solution)/shard_map/ppermute | solution.py:61
  241.7 11.9 %collective-permute-start.48 = (bf16[1,2,72,896]{3,2,1,0:T(8,128)(2,1)S(1)}, bf16[1,2,72,896]{3,2,1,0:T(8,128)(2,1)S(1)}, u32[]{:S(2)}, u32[]{:S(2)}) collective-permute-start(bf16[1,2,72,896]{3,2,1,0:T(8,128)(2,1)S(1)} %get-tuple-element.1087), channel_id=1, source_target_pairs={{0,2},{1,3},{2,0},{3,1},{4,6},{5,7},{6,4},{7,5},{8,10},{9,11},{10,... | collective-permute-start | bytes 774152 | tf_op jit(solution)/shard_map/ppermute | solution.py:61
  242.8 10.7 %collective-permute-start.49 = (bf16[1,2,72,1280]{3,2,1,0:T(8,128)(2,1)S(1)}, bf16[1,2,72,1280]{3,2,1,0:T(8,128)(2,1)S(1)}, u32[]{:S(2)}, u32[]{:S(2)}) collective-permute-start(bf16[1,2,72,1280]{3,2,1,0:T(8,128)(2,1)S(1)} %get-tuple-element.1089), channel_id=1, source_target_pairs={{0,4},{1,5},{2,6},{3,7},{4,0},{5,1},{6,2},{7,3},{8,12},{9,13},{10,... | collective-permute-start | bytes 1105928 | tf_op jit(solution)/shard_map/ppermute | solution.py:61
  256.8 10.3 %collective-permute-start.50 = (bf16[1,2,72,896]{3,2,1,0:T(8,128)(2,1)S(1)}, bf16[1,2,72,896]{3,2,1,0:T(8,128)(2,1)S(1)}, u32[]{:S(2)}, u32[]{:S(2)}) collective-permute-start(bf16[1,2,72,896]{3,2,1,0:T(8,128)(2,1)S(1)} %get-tuple-element.1101), channel_id=1, source_target_pairs={{0,2},{1,3},{2,0},{3,1},{4,6},{5,7},{6,4},{7,5},{8,10},{9,11},{10,... | collective-permute-start | bytes 774152 | tf_op jit(solution)/shard_map/ppermute | solution.py:61
  267.9 10.7 %collective-permute-start.52 = (bf16[512,1152]{1,0:T(8,128)(2,1)S(1)}, bf16[512,1152]{1,0:T(8,128)(2,1)S(1)}, u32[]{:S(2)}, u32[]{:S(2)}) collective-permute-start(bf16[512,1152]{1,0:T(8,128)(2,1)S(1)} %convolution_convert_fusion.8), channel_id=1, source_target_pairs={{0,1},{1,0},{2,3},{3,2},{4,5},{5,4},{6,7},{7,6},{8,9},{9,8},{10,11... | collective-permute-start | bytes 3538952 | tf_op jit(solution)/shard_map/ppermute | solution.py:61
  268.9 12.1 %collective-permute-start.53 = (bf16[1,2,72,896]{3,2,1,0:T(8,128)(2,1)S(1)}, bf16[1,2,72,896]{3,2,1,0:T(8,128)(2,1)S(1)}, u32[]{:S(2)}, u32[]{:S(2)}) collective-permute-start(bf16[1,2,72,896]{3,2,1,0:T(8,128)(2,1)S(1)} %get-tuple-element.1113), channel_id=1, source_target_pairs={{0,2},{1,3},{2,0},{3,1},{4,6},{5,7},{6,4},{7,5},{8,10},{9,11},{10,... | collective-permute-start | bytes 774152 | tf_op jit(solution)/shard_map/ppermute | solution.py:61
  270.2 10.7 %collective-permute-start.54 = (bf16[1,2,72,1280]{3,2,1,0:T(8,128)(2,1)S(1)}, bf16[1,2,72,1280]{3,2,1,0:T(8,128)(2,1)S(1)}, u32[]{:S(2)}, u32[]{:S(2)}) collective-permute-start(bf16[1,2,72,1280]{3,2,1,0:T(8,128)(2,1)S(1)} %get-tuple-element.1115), channel_id=1, source_target_pairs={{0,4},{1,5},{2,6},{3,7},{4,0},{5,1},{6,2},{7,3},{8,12},{9,13},{10,... | collective-permute-start | bytes 1105928 | tf_op jit(solution)/shard_map/ppermute | solution.py:61
  284.1 10.0 %collective-permute-start.55 = (bf16[1,2,72,1280]{3,2,1,0:T(8,128)(2,1)S(1)}, bf16[1,2,72,1280]{3,2,1,0:T(8,128)(2,1)S(1)}, u32[]{:S(2)}, u32[]{:S(2)}) collective-permute-start(bf16[1,2,72,1280]{3,2,1,0:T(8,128)(2,1)S(1)} %get-tuple-element.1137), channel_id=1, source_target_pairs={{0,4},{1,5},{2,6},{3,7},{4,0},{5,1},{6,2},{7,3},{8,12},{9,13},{10,... | collective-permute-start | bytes 1105928 | tf_op jit(solution)/shard_map/ppermute | solution.py:61
  297.0 10.5 %collective-permute-start.58 = (bf16[1152,640]{1,0:T(8,128)(2,1)S(1)}, bf16[1152,640]{1,0:T(8,128)(2,1)S(1)}, u32[]{:S(2)}, u32[]{:S(2)}) collective-permute-start(bf16[1152,640]{1,0:T(8,128)(2,1)S(1)} %pad_maximum_fusion.6), channel_id=1, source_target_pairs={{0,1},{1,0},{2,3},{3,2},{4,5},{5,4},{6,7},{7,6},{8,9},{9,8},{10,11... | collective-permute-start | bytes 4423688 | tf_op jit(solution)/shard_map/ppermute | solution.py:61
  304.7 18.1 %collective-permute-start.59 = (bf16[2,72,2176]{2,1,0:T(8,128)(2,1)}, bf16[2,72,2176]{2,1,0:T(8,128)(2,1)S(1)}, u32[]{:S(2)}, u32[]{:S(2)}) collective-permute-start(bf16[2,72,2176]{2,1,0:T(8,128)(2,1)} %fusion.34), channel_id=1, source_target_pairs={{0,8},{1,9},{2,10},{3,11},{4,12},{5,13},{6,14},{7,15},{8,16},{9,17... | collective-permute-start | bytes 1880072 | tf_op jit(solution)/shard_map/ppermute | solution.py:61
  305.3 24.1 %collective-permute-start.60 = (bf16[2,2,72,512]{3,2,1,0:T(8,128)(2,1)S(1)}, bf16[2,2,72,512]{3,2,1,0:T(8,128)(2,1)S(1)}, u32[]{:S(2)}, u32[]{:S(2)}) collective-permute-start(bf16[2,2,72,512]{3,2,1,0:T(8,128)(2,1)S(1)} %get-tuple-element.1199), channel_id=1, source_target_pairs={{0,2},{1,3},{2,0},{3,1},{4,6},{5,7},{6,4},{7,5},{8,10},{9,11},{10,... | collective-permute-start | bytes 884744 | tf_op jit(solution)/shard_map/ppermute | solution.py:61
  306.9 22.6 %collective-permute-start.61 = (bf16[2,2,72,1664]{3,2,1,0:T(8,128)(2,1)S(1)}, bf16[2,2,72,1664]{3,2,1,0:T(8,128)(2,1)S(1)}, u32[]{:S(2)}, u32[]{:S(2)}) collective-permute-start(bf16[2,2,72,1664]{3,2,1,0:T(8,128)(2,1)S(1)} %get-tuple-element.1201), channel_id=1, source_target_pairs={{0,4},{1,5},{2,6},{3,7},{4,0},{5,1},{6,2},{7,3},{8,12},{9,13},{10,... | collective-permute-start | bytes 2875400 | tf_op jit(solution)/shard_map/ppermute | solution.py:61
  329.6 22.8 %collective-permute-start.62 = (bf16[2,2,72,1664]{3,2,1,0:T(8,128)(2,1)S(1)}, bf16[2,2,72,1664]{3,2,1,0:T(8,128)(2,1)S(1)}, u32[]{:S(2)}, u32[]{:S(2)}) collective-permute-start(bf16[2,2,72,1664]{3,2,1,0:T(8,128)(2,1)S(1)} %get-tuple-element.1218), channel_id=1, source_target_pairs={{0,4},{1,5},{2,6},{3,7},{4,0},{5,1},{6,2},{7,3},{8,12},{9,13},{10,... | collective-permute-start | bytes 2875400 | tf_op jit(solution)/shard_map/ppermute | solution.py:61
  330.2 23.0 %collective-permute-start.65 = (bf16[4,2,72,640]{3,2,1,0:T(8,128)(2,1)S(1)}, bf16[4,2,72,640]{3,2,1,0:T(8,128)(2,1)S(1)}, u32[]{:S(2)}, u32[]{:S(2)}) collective-permute-start(bf16[4,2,72,640]{3,2,1,0:T(8,128)(2,1)S(1)} %dynamic-slice_bitcast_fusion.12), channel_id=1, source_target_pairs={{0,2},{1,3},{2,0},{3,1},{4,6},{5,7},{6,4},{7,5},{8,10},{9,11},{10,... | collective-permute-start | bytes 2211848 | tf_op jit(solution)/shard_map/ppermute | solution.py:61
  332.4 20.0 %collective-permute-start.63 = (bf16[2,72,2176]{2,1,0:T(8,128)(2,1)S(1)}, bf16[2,72,2176]{2,1,0:T(8,128)(2,1)S(1)}, u32[]{:S(2)}, u32[]{:S(2)}) collective-permute-start(bf16[2,72,2176]{2,1,0:T(8,128)(2,1)S(1)} %fusion.17), channel_id=1, source_target_pairs={{0,8},{1,9},{2,10},{3,11},{4,12},{5,13},{6,14},{7,15},{8,16},{9,17... | collective-permute-start | bytes 1880072 | tf_op jit(solution)/shard_map/ppermute | solution.py:61
  335.0 18.3 %collective-permute-start.64 = (bf16[2,2,72,512]{3,2,1,0:T(8,128)(2,1)S(1)}, bf16[2,2,72,512]{3,2,1,0:T(8,128)(2,1)S(1)}, u32[]{:S(2)}, u32[]{:S(2)}) collective-permute-start(bf16[2,2,72,512]{3,2,1,0:T(8,128)(2,1)S(1)} %get-tuple-element.1225), channel_id=1, source_target_pairs={{0,2},{1,3},{2,0},{3,1},{4,6},{5,7},{6,4},{7,5},{8,10},{9,11},{10,... | collective-permute-start | bytes 884744 | tf_op jit(solution)/shard_map/ppermute | solution.py:61
  355.0 21.8 %collective-permute-start.67 = (bf16[2,72,2176]{2,1,0:T(8,128)(2,1)S(1)}, bf16[2,72,2176]{2,1,0:T(8,128)(2,1)S(1)}, u32[]{:S(2)}, u32[]{:S(2)}) collective-permute-start(bf16[2,72,2176]{2,1,0:T(8,128)(2,1)S(1)} %fusion.16), channel_id=1, source_target_pairs={{0,8},{1,9},{2,10},{3,11},{4,12},{5,13},{6,14},{7,15},{8,16},{9,17... | collective-permute-start | bytes 1880072 | tf_op jit(solution)/shard_map/ppermute | solution.py:61
  373.6 18.9 %collective-permute-start.66 = (bf16[2,72,2816]{2,1,0:T(8,128)(2,1)S(1)}, bf16[2,72,2816]{2,1,0:T(8,128)(2,1)S(1)}, u32[]{:S(2)}, u32[]{:S(2)}) collective-permute-start(bf16[2,72,2816]{2,1,0:T(8,128)(2,1)S(1)} %dynamic-slice_bitcast_fusion.11), channel_id=1, source_target_pairs={{0,8},{1,9},{2,10},{3,11},{4,12},{5,13},{6,14},{7,15},{8,16},{9,17... | collective-permute-start | bytes 2433032 | tf_op jit(solution)/shard_map/ppermute | solution.py:61
  388.1 10.9 %collective-permute-start.68 = (bf16[512,1152]{1,0:T(8,128)(2,1)S(1)}, bf16[512,1152]{1,0:T(8,128)(2,1)S(1)}, u32[]{:S(2)}, u32[]{:S(2)}) collective-permute-start(bf16[512,1152]{1,0:T(8,128)(2,1)S(1)} %convolution_convert_fusion.6), channel_id=1, source_target_pairs={{0,1},{1,0},{2,3},{3,2},{4,5},{5,4},{6,7},{7,6},{8,9},{9,8},{10,11... | collective-permute-start | bytes 3538952 | tf_op jit(solution)/shard_map/ppermute | solution.py:61
  390.5 30.0 %collective-permute-start.72 = (bf16[4,2,72,896]{3,2,1,0:T(8,128)(2,1)S(1)}, bf16[4,2,72,896]{3,2,1,0:T(8,128)(2,1)S(1)}, u32[]{:S(2)}, u32[]{:S(2)}) collective-permute-start(bf16[4,2,72,896]{3,2,1,0:T(8,128)(2,1)S(1)} %dynamic-slice_bitcast_fusion.8), channel_id=1, source_target_pairs={{0,2},{1,3},{2,0},{3,1},{4,6},{5,7},{6,4},{7,5},{8,10},{9,11},{10,... | collective-permute-start | bytes 3096584 | tf_op jit(solution)/shard_map/ppermute | solution.py:61
  392.4 28.0 %collective-permute-start.73 = (bf16[4,2,72,1024]{3,2,1,0:T(8,128)(2,1)S(1)}, bf16[4,2,72,1024]{3,2,1,0:T(8,128)(2,1)S(1)}, u32[]{:S(2)}, u32[]{:S(2)}) collective-permute-start(bf16[4,2,72,1024]{3,2,1,0:T(8,128)(2,1)S(1)} %dynamic-slice_bitcast_fusion.7), channel_id=1, source_target_pairs={{0,4},{1,5},{2,6},{3,7},{4,0},{5,1},{6,2},{7,3},{8,12},{9,13},{10,... | collective-permute-start | bytes 3538952 | tf_op jit(solution)/shard_map/ppermute | solution.py:61
  398.8 23.8 %collective-permute-start.71 = (bf16[2,72,2816]{2,1,0:T(8,128)(2,1)}, bf16[2,72,2816]{2,1,0:T(8,128)(2,1)S(1)}, u32[]{:S(2)}, u32[]{:S(2)}) collective-permute-start(bf16[2,72,2816]{2,1,0:T(8,128)(2,1)} %fusion.12), channel_id=1, source_target_pairs={{0,8},{1,9},{2,10},{3,11},{4,12},{5,13},{6,14},{7,15},{8,16},{9,17... | collective-permute-start | bytes 2433032 | tf_op jit(solution)/shard_map/ppermute | solution.py:61
  399.1 33.2 %collective-permute-start.76 = (f32[36,2176]{1,0:T(8,128)}, f32[36,2176]{1,0:T(8,128)}, u32[]{:S(2)}, u32[]{:S(2)}) collective-permute-start(f32[36,2176]{1,0:T(8,128)} %get-tuple-element.1332), channel_id=1, source_target_pairs={{0,1},{1,0},{2,3},{3,2},{4,5},{5,4},{6,7},{7,6},{8,9},{9,8},{10,11... | collective-permute-start | bytes 940040 | tf_op jit(solution)/shard_map/ppermute | solution.py:61
  426.4 19.1 %collective-permute-start.74 = (bf16[512,1152]{1,0:T(8,128)(2,1)S(1)}, bf16[512,1152]{1,0:T(8,128)(2,1)}, u32[]{:S(2)}, u32[]{:S(2)}) collective-permute-start(bf16[512,1152]{1,0:T(8,128)(2,1)S(1)} %copy-done.119), channel_id=1, source_target_pairs={{0,1},{1,0},{2,3},{3,2},{4,5},{5,4},{6,7},{7,6},{8,9},{9,8},{10,11... | collective-permute-start | bytes 3538952 | tf_op jit(solution)/shard_map/ppermute | solution.py:61
  426.5 16.4 %collective-permute-start.75 = (bf16[1,256,1152]{2,1,0:T(8,128)(2,1)}, bf16[1,256,1152]{2,1,0:T(8,128)(2,1)S(1)}, u32[]{:S(2)}, u32[]{:S(2)}) collective-permute-start(bf16[1,256,1152]{2,1,0:T(8,128)(2,1)} %fusion.35), channel_id=1, source_target_pairs={{0,2},{1,3},{2,0},{3,1},{4,6},{5,7},{6,4},{7,5},{8,10},{9,11},{10,... | collective-permute-start | bytes 1769480 | tf_op jit(solution)/shard_map/ppermute | solution.py:61
  432.3 16.7 %collective-permute-start.77 = (f32[112,128]{1,0:T(8,128)}, f32[112,128]{1,0:T(8,128)}, u32[]{:S(2)}, u32[]{:S(2)}) collective-permute-start(f32[112,128]{1,0:T(8,128)} %pad_bitcast_fusion), channel_id=1, source_target_pairs={{0,1},{1,0},{2,3},{3,2},{4,5},{5,4},{6,7},{7,6},{8,9},{9,8},{10,11... | collective-permute-start | bytes 172040 | tf_op jit(solution)/shard_map/ppermute | solution.py:61
  432.4 28.4 %collective-permute-start.79 = (bf16[2,72,2816]{2,1,0:T(8,128)(2,1)}, bf16[2,72,2816]{2,1,0:T(8,128)(2,1)}, u32[]{:S(2)}, u32[]{:S(2)}) collective-permute-start(bf16[2,72,2816]{2,1,0:T(8,128)(2,1)} %fusion.11), channel_id=1, source_target_pairs={{0,8},{1,9},{2,10},{3,11},{4,12},{5,13},{6,14},{7,15},{8,16},{9,17... | collective-permute-start | bytes 2433032 | tf_op jit(solution)/shard_map/ppermute | solution.py:61
  432.8 22.4 %collective-permute-start.80 = (bf16[4,72,1024]{2,1,0:T(8,128)(2,1)}, bf16[4,72,1024]{2,1,0:T(8,128)(2,1)}, u32[]{:S(2)}, u32[]{:S(2)}) collective-permute-start(bf16[4,72,1024]{2,1,0:T(8,128)(2,1)} %get-tuple-element.1367), channel_id=1, source_target_pairs={{0,2},{1,3},{2,0},{3,1},{4,6},{5,7},{6,4},{7,5},{8,10},{9,11},{10,... | collective-permute-start | bytes 1769480 | tf_op jit(solution)/shard_map/ppermute | solution.py:61
  442.9 13.3 %collective-permute-start.81 = (bf16[4,72,896]{2,1,0:T(8,128)(2,1)}, bf16[4,72,896]{2,1,0:T(8,128)(2,1)}, u32[]{:S(2)}, u32[]{:S(2)}) collective-permute-start(bf16[4,72,896]{2,1,0:T(8,128)(2,1)} %get-tuple-element.1370), channel_id=1, source_target_pairs={{0,4},{1,5},{2,6},{3,7},{4,0},{5,1},{6,2},{7,3},{8,12},{9,13},{10,... | collective-permute-start | bytes 1548296 | tf_op jit(solution)/shard_map/ppermute | solution.py:61
  459.4 16.3 %collective-permute-start.78 = (bf16[1,256,1152]{2,1,0:T(8,128)(2,1)S(1)}, bf16[1,256,1152]{2,1,0:T(8,128)(2,1)S(1)}, u32[]{:S(2)}, u32[]{:S(2)}) collective-permute-start(bf16[1,256,1152]{2,1,0:T(8,128)(2,1)S(1)} %get-tuple-element.1362), channel_id=1, source_target_pairs={{0,2},{1,3},{2,0},{3,1},{4,6},{5,7},{6,4},{7,5},{8,10},{9,11},{10,... | collective-permute-start | bytes 1769480 | tf_op jit(solution)/shard_map/ppermute | solution.py:61
  460.9 14.8 %collective-permute-start.84 = (bf16[72,1920]{1,0:T(8,128)(2,1)S(1)}, bf16[72,1920]{1,0:T(8,128)(2,1)S(1)}, u32[]{:S(2)}, u32[]{:S(2)}) collective-permute-start(bf16[72,1920]{1,0:T(8,128)(2,1)S(1)} %fusion.58), channel_id=1, source_target_pairs={{0,8},{1,9},{2,10},{3,11},{4,12},{5,13},{6,14},{7,15},{8,16},{9,17... | collective-permute-start | bytes 829448 | tf_op jit(solution)/shard_map/ppermute | solution.py:61
  463.2 12.6 %collective-permute-start.83 = (f32[112,128]{1,0:T(8,128)S(1)}, f32[112,128]{1,0:T(8,128)S(1)}, u32[]{:S(2)}, u32[]{:S(2)}) collective-permute-start(f32[112,128]{1,0:T(8,128)S(1)} %add.529), channel_id=1, source_target_pairs={{0,4},{1,5},{2,6},{3,7},{4,0},{5,1},{6,2},{7,3},{8,12},{9,13},{10,... | collective-permute-start | bytes 172040 | tf_op jit(solution)/shard_map/ppermute | solution.py:61
  464.1 14.2 %collective-permute-start.87 = (bf16[72,1664]{1,0:T(8,128)(2,1)S(1)}, bf16[72,1664]{1,0:T(8,128)(2,1)S(1)}, u32[]{:S(2)}, u32[]{:S(2)}) collective-permute-start(bf16[72,1664]{1,0:T(8,128)(2,1)S(1)} %fusion.63), channel_id=1, source_target_pairs={{0,2},{1,3},{2,0},{3,1},{4,6},{5,7},{6,4},{7,5},{8,10},{9,11},{10,... | collective-permute-start | bytes 718856 | tf_op jit(solution)/shard_map/ppermute | solution.py:61
  465.4 12.8 %collective-permute-start.88 = (bf16[72,1152]{1,0:T(8,128)(2,1)S(1)}, bf16[72,1152]{1,0:T(8,128)(2,1)S(1)}, u32[]{:S(2)}, u32[]{:S(2)}) collective-permute-start(bf16[72,1152]{1,0:T(8,128)(2,1)S(1)} %fusion.65), channel_id=1, source_target_pairs={{0,4},{1,5},{2,6},{3,7},{4,0},{5,1},{6,2},{7,3},{8,12},{9,13},{10,... | collective-permute-start | bytes 497672 | tf_op jit(solution)/shard_map/ppermute | solution.py:61
  (164 other events, 1308.2 us)
